TPU v7x, 32 devices: a whole 2x2x4 slice. The times are simulated.
32 devices in a mesh: dp: 8 (over z, x), tensor: 4 (over y, core).
Axes of the slice: x: 2, y: 2, z: 4, core: 2. Of those that a mesh axis runs over, the one named last changes fastest.
Arguments:
- tokens: bfloat16 [16384, 768], P(('dp', 'tensor')), may hold values from -6 to 6
- segment: int32 [16384], P('dp'), may hold values from 0 to 7, as said below
- cotangent: bfloat16 [16384, 768], P(('dp', 'tensor')), may hold values from -6 to 6
- ln1_gain: float32 [768], replicated, may hold values from 0.5 to 1.5
- ln1_bias: float32 [768], replicated, may hold values from -1.75 to 1.75
- w_qkv: bfloat16 [3, 768, 768], P(None, 'dp', 'tensor'), may hold values from -0.21875 to 0.21875
- qv_bias: bfloat16 [2, 12, 64], P(None, 'tensor', 'dp'), may hold values from -1.75 to 1.75
- w_out: bfloat16 [768, 768], P('tensor', 'dp'), may hold values from -0.875 to 0.875
- out_bias: bfloat16 [768], replicated, may hold values from -1.75 to 1.75
- ln2_gain: float32 [768], replicated, may hold values from 0.5 to 1.5
- ln2_bias: float32 [768], replicated, may hold values from -1.75 to 1.75
- w_up: bfloat16 [768, 3072], P('dp', 'tensor'), may hold values from -0.21875 to 0.21875
- up_bias: bfloat16 [48, 64], P('tensor', 'dp'), may hold values from -1.75 to 1.75
- w_down: bfloat16 [3072, 768], P('tensor', 'dp'), may hold values from -0.109375 to 0.109375
- down_bias: bfloat16 [768], replicated, may hold values from -1.75 to 1.75
Outputs:
- block_out: float32 [16384, 768], P(('dp', 'tensor'))
- tokens_grad: float32 [16384, 768], P(('dp', 'tensor'))
- ln1_gain_grad: float32 [768], replicated
- ln1_bias_grad: float32 [768], replicated
- w_qkv_grad: float32 [3, 768, 768], P(None, 'dp', 'tensor')
- qv_bias_grad: float32 [2, 12, 64], P(None, 'tensor', 'dp')
- w_out_grad: float32 [768, 768], P('tensor', 'dp')
- out_bias_grad: float32 [768], replicated
- ln2_gain_grad: float32 [768], replicated
- ln2_bias_grad: float32 [768], replicated
- w_up_grad: float32 [768, 3072], P('dp', 'tensor')
- up_bias_grad: float32 [48, 64], P('tensor', 'dp')
- w_down_grad: float32 [3072, 768], P('tensor', 'dp')
- down_bias_grad: float32 [768], replicated
Inputs may be any that keep to these rules, and one draw needn't show every extreme that they name: Within each packed row of 2048 tokens the segment numbers start at 0, never fall and end at 7, each taken by one run of tokens; one document of each row starts within the row's first 512 tokens and ends within its last 512.
All inputs are finite; a program needn't handle non-finite values.
Results may differ from a plain program's by a relative error of at most 0.0096.
Values may be sent and summed in bfloat16 or wider, within the bound.
No kernel may reach another device: no remote copies, remote signals or barrier semaphores. Data moves between devices by JAX's collectives and lax.ppermute only.
A program may use at most 128 MiB of HBM per device.

v0:
```python
import jax
import jax.numpy as jnp
from jax import lax
from jax.sharding import PartitionSpec as P

HD = 64
QBLK = 512


EPSILON = 1e-05
GELU_COEF = 0.7978845608028654


def cut_along(shard, dim, size):
    before, after = (shard.shape[:dim], shard.shape[dim + 1 :])
    return jnp.moveaxis(shard.reshape(*before, size, -1, *after), dim, 0)


def summed_on_arrival(shard, axis, dim):
    size = lax.axis_size(axis)
    tiles = lax.all_to_all(cut_along(shard, dim, size), axis, 0, 0, tiled=True)
    return jnp.sum(tiles.astype(jnp.float32), axis=0)


def layer_norm(values_in, gain_vec, shift_vec):
    row_mean = jnp.mean(values_in, axis=-1, keepdims=True)
    centered = values_in - row_mean
    variance = jnp.mean(centered * centered, axis=-1, keepdims=True)
    return centered * lax.rsqrt(variance + EPSILON) * gain_vec + shift_vec


def gelu_tanh(values_in):
    return (
        0.5
        * values_in
        * (1.0 + jnp.tanh(GELU_COEF * (values_in + 0.044715 * values_in * values_in * values_in)))
    )


def product(left_mat, right_mat):
    return jnp.dot(left_mat, right_mat, preferred_element_type=jnp.float32)


def contract_rows(left_mat, right_mat):
    return lax.dot_general(
        left_mat, right_mat, (((0,), (0,)), ((), ())), preferred_element_type=jnp.float32
    )


def contract_cols(left_mat, right_mat):
    return lax.dot_general(
        left_mat, right_mat, (((1,), (1,)), ((), ())), preferred_element_type=jnp.float32
    )


def rows_attention(values_in):
    return lax.all_gather(values_in, "tensor", axis=0, tiled=True)


def sums_attention(values_in):
    return lax.psum_scatter(values_in, "tensor", scatter_dimension=0, tiled=True)


def rows_mlp(values_in):
    return lax.all_gather(values_in, "tensor", axis=0, tiled=True)


def sums_mlp(values_in):
    return lax.psum_scatter(values_in, "tensor", scatter_dimension=0, tiled=True)


def masked_scores(query_block, key_head, segment, block_start):
    row_total = key_head.shape[0]
    position = jnp.arange(row_total, dtype=jnp.int32)
    position_block = block_start + jnp.arange(QBLK, dtype=jnp.int32)
    segment_block = lax.dynamic_slice_in_dim(segment, block_start, QBLK, 0)
    allowed = (position[None, :] <= position_block[:, None]) & (
        segment[None, :] == segment_block[:, None]
    )
    scores = contract_cols(query_block, key_head) * HD ** (-0.5)
    return jnp.where(allowed, scores, -1e30)


def forward_head(query_head, key_head, value_head, segment, block_starts):

    def forward_one_block(block_start):
        query_block = lax.dynamic_slice_in_dim(query_head, block_start, QBLK, 0)
        scores = masked_scores(query_block, key_head, segment, block_start)
        row_max = jnp.max(scores, axis=1, keepdims=True)
        log_total = row_max + jnp.log(jnp.sum(jnp.exp(scores - row_max), axis=1, keepdims=True))
        weights_soft = jnp.exp(scores - log_total)
        mixed_block = product(weights_soft.astype(jnp.bfloat16), value_head)
        return (mixed_block.astype(jnp.bfloat16), log_total[:, 0])

    mixed_blocks, log_totals = lax.map(forward_one_block, block_starts)
    return (mixed_blocks.reshape(-1, HD), log_totals.reshape(-1))


def backward_head(query_head, key_head, value_head, grad_head, log_totals, segment, block_starts):
    score_scale = HD ** (-0.5)

    def backward_one_block(carried, block_start):
        key_grad, value_grad = carried
        query_block = lax.dynamic_slice_in_dim(query_head, block_start, QBLK, 0)
        grad_block = lax.dynamic_slice_in_dim(grad_head, block_start, QBLK, 0)
        total_block = lax.dynamic_slice_in_dim(log_totals, block_start, QBLK, 0)
        scores = masked_scores(query_block, key_head, segment, block_start)
        weights_soft = jnp.exp(scores - total_block[:, None])
        value_grad = value_grad + contract_rows(weights_soft.astype(jnp.bfloat16), grad_block)
        weight_grad = contract_cols(grad_block, value_head)
        inner_sum = jnp.sum(weights_soft * weight_grad, axis=1, keepdims=True)
        score_grad = (weights_soft * (weight_grad - inner_sum)).astype(jnp.bfloat16)
        query_grad = product(score_grad, key_head) * score_scale
        key_grad = key_grad + contract_rows(score_grad, query_block) * score_scale
        return ((key_grad, value_grad), query_grad.astype(jnp.bfloat16))

    zero_rows = jnp.zeros(key_head.shape, jnp.float32)
    (key_grad, value_grad), query_grads = lax.scan(
        backward_one_block, (zero_rows, zero_rows), block_starts
    )
    return (
        query_grads.reshape(-1, HD),
        key_grad.astype(jnp.bfloat16),
        value_grad.astype(jnp.bfloat16),
    )


def on_device(
    tokens,
    segment,
    cotangent,
    ln1_gain,
    ln1_bias,
    w_qkv,
    qv_bias,
    w_out,
    out_bias,
    ln2_gain,
    ln2_bias,
    w_up,
    up_bias,
    w_down,
    down_bias,
):
    qkv_full, out_full, qv_full = (
        lax.all_gather(w_qkv, "dp", axis=1, tiled=True),
        lax.all_gather(w_out, "dp", axis=1, tiled=True),
        lax.all_gather(qv_bias, "dp", axis=2, tiled=True),
    )
    up_part, down_part, up_bias_part = (
        lax.all_gather(w_up, "dp", axis=0, tiled=True),
        lax.all_gather(w_down, "dp", axis=1, tiled=True),
        lax.all_gather(up_bias, "dp", axis=1, tiled=True),
    )
    token_rows = tokens.astype(jnp.float32)
    first_norm = rows_attention(layer_norm(token_rows, ln1_gain, ln1_bias).astype(jnp.bfloat16))
    queries = (
        product(first_norm, qkv_full[0]) + qv_full[0].reshape(-1).astype(jnp.float32)
    ).astype(jnp.bfloat16)
    keys_all = product(first_norm, qkv_full[1]).astype(jnp.bfloat16)
    values_all = (
        product(first_norm, qkv_full[2]) + qv_full[1].reshape(-1).astype(jnp.float32)
    ).astype(jnp.bfloat16)
    row_total = first_norm.shape[0]
    block_starts = jnp.arange(row_total // QBLK, dtype=jnp.int32) * QBLK
    head_count = queries.shape[1] // HD
    mixed_list = []
    total_list = []
    for head_index in range(head_count):
        columns = slice(head_index * HD, (head_index + 1) * HD)
        mixed_head, log_totals = forward_head(
            queries[:, columns], keys_all[:, columns], values_all[:, columns], segment, block_starts
        )
        mixed_list.append(mixed_head)
        total_list.append(log_totals)
    heads_out = jnp.concatenate(mixed_list, axis=1)
    attn_branch = sums_attention(product(heads_out, out_full))
    hidden_one = token_rows + (attn_branch + out_bias.astype(jnp.float32))
    second_own = layer_norm(hidden_one, ln2_gain, ln2_bias).astype(jnp.bfloat16)
    up_all, down_all, up_bias_all = (up_part, down_part, up_bias_part)
    second = rows_mlp(second_own)
    pre_act = product(second, up_all) + up_bias_all.reshape(-1).astype(jnp.float32)
    activation = gelu_tanh(pre_act).astype(jnp.bfloat16)
    mlp_partial = product(activation, down_all)
    mlp_branch = sums_mlp(mlp_partial)
    block_out = hidden_one + (mlp_branch + down_bias.astype(jnp.float32))
    grad_out = cotangent.astype(jnp.float32)
    grad_mlp_own = grad_out.astype(jnp.bfloat16)
    down_bias_grad = jnp.sum(grad_mlp_own, axis=0, dtype=jnp.float32)
    grad_mlp = rows_mlp(grad_mlp_own)
    down_grad = contract_rows(activation, grad_mlp)
    act_grad = contract_cols(grad_mlp, down_all)
    pre_grad = jax.vjp(gelu_tanh, pre_act)[1](act_grad)[0].astype(jnp.bfloat16)
    up_bias_grad = jnp.sum(pre_grad, axis=0, dtype=jnp.float32).reshape(up_bias_all.shape)
    up_grad = contract_rows(second, pre_grad)
    second_grad_part = contract_cols(pre_grad, up_all)
    second_grad = sums_mlp(second_grad_part)
    norm_pull = jax.vjp(layer_norm, hidden_one, ln2_gain, ln2_bias)[1]
    hidden_grad_norm, ln2_gain_grad, ln2_bias_grad = norm_pull(second_grad)
    hidden_grad = grad_out + hidden_grad_norm
    up_grad_out, down_grad_out, up_bias_grad_out = (
        lax.psum_scatter(up_grad, "dp", scatter_dimension=0, tiled=True),
        lax.psum_scatter(down_grad, "dp", scatter_dimension=1, tiled=True),
        lax.psum_scatter(up_bias_grad, "dp", scatter_dimension=1, tiled=True),
    )
    grad_attn_own = hidden_grad.astype(jnp.bfloat16)
    out_bias_grad = jnp.sum(grad_attn_own, axis=0, dtype=jnp.float32)
    grad_attn = rows_attention(grad_attn_own)
    out_grad = contract_rows(heads_out, grad_attn)
    heads_grad = contract_cols(grad_attn, out_full).astype(jnp.bfloat16)
    query_list = []
    key_list = []
    value_list = []
    for head_index in range(head_count):
        columns = slice(head_index * HD, (head_index + 1) * HD)
        query_grad, key_grad, value_grad = backward_head(
            queries[:, columns],
            keys_all[:, columns],
            values_all[:, columns],
            heads_grad[:, columns],
            total_list[head_index],
            segment,
            block_starts,
        )
        query_list.append(query_grad)
        key_list.append(key_grad)
        value_list.append(value_grad)
    query_grad = jnp.concatenate(query_list, axis=1)
    key_grad = jnp.concatenate(key_list, axis=1)
    value_grad = jnp.concatenate(value_list, axis=1)
    qkv_grad = jnp.stack(
        [
            contract_rows(first_norm, query_grad),
            contract_rows(first_norm, key_grad),
            contract_rows(first_norm, value_grad),
        ]
    )
    qv_bias_grad = jnp.stack(
        [
            jnp.sum(query_grad, axis=0, dtype=jnp.float32),
            jnp.sum(value_grad, axis=0, dtype=jnp.float32),
        ]
    ).reshape(qv_full.shape)
    first_grad = sums_attention(
        contract_cols(query_grad, qkv_full[0])
        + contract_cols(key_grad, qkv_full[1])
        + contract_cols(value_grad, qkv_full[2])
    )
    norm_pull_first = jax.vjp(layer_norm, token_rows, ln1_gain, ln1_bias)[1]
    token_grad_norm, ln1_gain_grad, ln1_bias_grad = norm_pull_first(first_grad)
    token_grad = hidden_grad + token_grad_norm
    qkv_grad_out, w_out_grad_out, qv_bias_grad_out = (
        summed_on_arrival(qkv_grad.astype(jnp.bfloat16), "dp", 1),
        summed_on_arrival(out_grad.astype(jnp.bfloat16), "dp", 1),
        summed_on_arrival(qv_bias_grad.astype(jnp.bfloat16), "dp", 2),
    )
    vectors = lax.psum(
        (ln1_gain_grad, ln1_bias_grad, out_bias_grad, ln2_gain_grad, ln2_bias_grad, down_bias_grad),
        ("dp", "tensor"),
    )
    return (
        block_out,
        token_grad,
        vectors[0],
        vectors[1],
        qkv_grad_out,
        qv_bias_grad_out,
        w_out_grad_out,
        vectors[2],
        vectors[3],
        vectors[4],
        up_grad_out,
        up_bias_grad_out,
        down_grad_out,
        vectors[5],
    )


def solution(mesh):
    in_specs = (
        P(("dp", "tensor"), None),
        P("dp"),
        P(("dp", "tensor"), None),
        P(),
        P(),
        P(None, "dp", "tensor"),
        P(None, "tensor", "dp"),
        P("tensor", "dp"),
        P(),
        P(),
        P(),
        P("dp", "tensor"),
        P("tensor", "dp"),
        P("tensor", "dp"),
        P(),
    )
    out_specs = (
        P(("dp", "tensor"), None),
        P(("dp", "tensor"), None),
        P(),
        P(),
        P(None, "dp", "tensor"),
        P(None, "tensor", "dp"),
        P("tensor", "dp"),
        P(),
        P(),
        P(),
        P("dp", "tensor"),
        P("tensor", "dp"),
        P("tensor", "dp"),
        P(),
    )
    return jax.shard_map(
        on_device, mesh=mesh, in_specs=in_specs, out_specs=out_specs, check_vma=False
    )
```

profile of v0, /device:TPU:0, one launch (start us, length us, event | category | flops | bytes accessed | tf_op | source)
XLA Modules:
  0.0 939.6 jit_solution(5499052720564949618)
XLA Ops:
  13.6 32.2 %all_gather.32 = bf16[2,3,64]{1,0,2:T(2,128)(2,1)S(1)} all-gather(bf16[2,3,8]{1,0,2:T(2,128)(2,1)S(1)} %copy.243), channel_id=1, replica_groups=mesh['dp'=8,'tensor'=4] {'dp'}, dimensions={2}, use_global_device_ids=true | all-gather | bytes 864 | tf_op jit(solution)/shard_map/all_gather | solution.py:148
  46.4 31.5 %all_gather.33 = bf16[192,768]{0,1:T(8,128)(2,1)S(1)} all-gather(bf16[192,96]{0,1:T(8,128)(2,1)S(1)} %copy.258), channel_id=1, replica_groups=mesh['dp'=8,'tensor'=4] {'dp'}, dimensions={1}, use_global_device_ids=true | all-gather | bytes 331776 | tf_op jit(solution)/shard_map/all_gather | solution.py:147
  77.9 34.0 %all_gather.31 = bf16[3,768,192]{2,1,0:T(8,128)(2,1)S(1)} all-gather(bf16[3,96,192]{2,1,0:T(8,128)(2,1)S(1)} %copy-done.45), channel_id=1, replica_groups=mesh['dp'=8,'tensor'=4] {'dp'}, dimensions={1}, use_global_device_ids=true | all-gather | bytes 995328 | tf_op jit(solution)/shard_map/all_gather | solution.py:146
  128.7 28.7 %while.83 = (s32[]{:T(128)}, bf16[4,512,64]{1,2,0:T(8,128)(2,1)S(1)}, f32[4,512]{1,0:T(4,128)S(1)}, s32[4]{0:T(128)S(1)}, s32[2048]{0:T(1024)S(1)}, /*index=5*/b...) while((s32[]{:T(128)}, ...), condition=%wide.region_13.14_spmd, body=%wide.region_10.13_spmd.sunk | while | flops 278953984 | bytes 13602999 | solution.py:95
  159.4 28.5 %while.82 = (s32[]{:T(128)}, bf16[4,512,64]{1,2,0:T(8,128)(2,1)S(1)}, f32[4,512]{1,0:T(4,128)S(1)}, s32[4]{0:T(128)S(1)}, s32[2048]{0:T(1024)S(1)}, /*index=5*/b...) while((s32[]{:T(128)}, ...), condition=%wide.region_9.10_spmd, body=%wide.region_6.9_spmd.sunk | while | flops 278953984 | bytes 13602999 | solution.py:95
  189.9 28.5 %while.81 = (s32[]{:T(128)}, bf16[4,512,64]{1,2,0:T(8,128)(2,1)S(1)}, f32[4,512]{1,0:T(4,128)S(1)}, s32[4]{0:T(128)S(1)}, s32[2048]{0:T(1024)S(1)}, /*index=5*/b...) while((s32[]{:T(128)}, ...), condition=%wide.region_5.6_spmd, body=%wide.region_2.5_spmd.sunk | while | flops 278953984 | bytes 13602999 | solution.py:95
  224.0 59.5 %reduce-scatter.8.cloned.1.call-done = f32[512,768]{1,0:T(8,128)} async-done(((f32[2048,768]{1,0:T(8,128)}), f32[512,768]{1,0:T(8,128)}) %reduce-scatter.8.cloned.1.call-update) | async-done | bytes 1572880 | tf_op jit(solution)/shard_map/reduce_scatter | solution.py:61
  288.1 26.5 %all_gather.36 = bf16[12,64]{0,1:T(8,128)(2,1)S(1)} all-gather(bf16[12,8]{0,1:T(8,128)(2,1)S(1)} %copy-done.65), channel_id=1, replica_groups=mesh['dp'=8,'tensor'=4] {'dp'}, dimensions={1}, use_global_device_ids=true | all-gather | bytes 1728 | tf_op jit(solution)/shard_map/all_gather | solution.py:153
  315.2 7.5 fusion.111
  322.7 36.4 %all-gather.13.cloned.1.call-done = bf16[768,768]{0,1:T(8,128)(2,1)} async-done(((bf16[768,96]{0,1:T(8,128)(2,1)}), bf16[768,768]{0,1:T(8,128)(2,1)}) %all-gather.13.cloned.1.call-update) | async-done | bytes 1179664 | tf_op jit(solution)/shard_map/all_gather | solution.py:152
  359.1 28.6 %all-gather.15.cloned.1.call-done = bf16[2048,768]{1,0:T(8,128)(2,1)} async-done(((bf16[512,768]{1,0:T(8,128)(2,1)}), bf16[2048,768]{1,0:T(8,128)(2,1)}) %all-gather.15.cloned.1.call-update) | async-done | bytes 3145744 | tf_op jit(solution)/shard_map/all_gather | solution.py:65
  387.6 11.9 %convert_reduce_fusion = (f32[768]{0:T(1024)}, bf16[2048,768]{1,0:T(8,128)(2,1)S(1)}, bf16[2048,768]{1,0:T(8,128)(2,1)}) fusion(f32[2048,768]{1,0:T(8,128)} %fusion.111, f32[768]{0:T(1024)S(1)} %reshape.304, bf16[2048,768]{1,0:T(8,128)(2,1)} %all-gather.15.cloned.1.call-done, bf16[768,768]{0,1:T(8,128)(2,1)} %all-gather.13.cloned.1.call-done), kind=kOutput, calls=%fused_computation.121 | convolution fusion | flops 2461531392 | bytes 16914432 | tf_op jit(solution)/shard_map/dot_general | solution.py:51
  405.9 8.0 fusion.112
  414.6 49.5 %reduce-scatter.12.cloned.1.call-done = f32[512,768]{1,0:T(8,128)} async-done(((f32[2048,768]{1,0:T(8,128)}), f32[512,768]{1,0:T(8,128)}) %reduce-scatter.12.cloned.1.call-update) | async-done | bytes 1572880 | tf_op jit(solution)/shard_map/reduce_scatter | solution.py:69
  466.8 58.2 %reduce-scatter.10.cloned.1.call-done = f32[512,768]{1,0:T(8,128)} async-done(((f32[2048,768]{1,0:T(8,128)}), f32[512,768]{1,0:T(8,128)}) %reduce-scatter.10.cloned.1.call-update) | async-done | bytes 1572880 | tf_op jit(solution)/shard_map/reduce_scatter | solution.py:69
  531.9 28.4 %all-gather.17.cloned.1.call-done = bf16[2048,768]{1,0:T(8,128)(2,1)} async-done(((bf16[512,768]{1,0:T(8,128)(2,1)}), bf16[2048,768]{1,0:T(8,128)(2,1)}) %all-gather.17.cloned.1.call-update) | async-done | bytes 3145744 | tf_op jit(solution)/shard_map/all_gather | solution.py:57
  565.0 48.2 %while.86 = (s32[]{:T(128)}, f32[2048,64]{0,1:T(8,128)}, f32[2048,64]{0,1:T(8,128)S(1)}, bf16[4,512,64]{1,2,0:T(8,128)(2,1)}, s32[4]{0:T(128)S(1)}, /*index=5*/s...) while((s32[]{:T(128)}, f32[2048,64]{0,1:T(8,128)}, ...), condition=%wide.region_29.30_spmd.clone, body=%wide.region_27.29_spmd.clone.sunk | while | flops 684392448 | bytes 40333624 | solution.py:118
  615.6 47.4 %while.85 = (s32[]{:T(128)}, f32[2048,64]{0,1:T(8,128)}, f32[2048,64]{0,1:T(8,128)S(1)}, bf16[4,512,64]{1,2,0:T(8,128)(2,1)}, s32[4]{0:T(128)S(1)}, /*index=5*/s...) while((s32[]{:T(128)}, f32[2048,64]{0,1:T(8,128)}, ...), condition=%wide.region_26.27_spmd.clone, body=%wide.region_24.26_spmd.clone.sunk | while | flops 684392448 | bytes 41382228 | solution.py:118
  665.4 40.1 %while.84 = (s32[]{:T(128)}, f32[2048,64]{0,1:T(8,128)}, f32[2048,64]{0,1:T(8,128)S(1)}, bf16[4,512,64]{1,2,0:T(8,128)(2,1)}, s32[4]{0:T(128)S(1)}, /*index=5*/s...) while((s32[]{:T(128)}, f32[2048,64]{0,1:T(8,128)}, ...), condition=%wide.region_23.24_spmd.clone, body=%wide.region_21.23_spmd.clone.sunk | while | flops 684392448 | bytes 40595768 | solution.py:118
  722.9 8.2 fusion.115
  770.8 6.1 all-to-all-start
  778.2 44.5 %all-reduce = f32[12,64]{1,0:T(8,128)S(1)} all-reduce(f32[12,64]{1,0:T(8,128)S(1)} %reshape.301), channel_id=7, replica_groups=mesh['dp'=8,'tensor'=4] {'dp'}, use_global_device_ids=true, to_apply=%region_50.51.clone | all-reduce | flops 768 | bytes 6144
  833.2 48.2 %all-reduce.1 = (f32[768]{0:T(1024)}, f32[768]{0:T(1024)}, f32[768]{0:T(1024)}, f32[768]{0:T(1024)}, f32[768]{0:T(1024)}, /*index=5*/f32[768]{0:T(1024)}) all-reduce(f32[768]{0:T(1024)S(1)} %get-tuple-element.928, f32[768]{0:T(1024)S(1)} %get-tuple-element.931, ...), channel_id=1, replica_groups=mesh['dp'=8,'tensor'=4] {'dp','tensor'}, use_global_device_ids=true, to_apply=%region_34.35 | all-reduce | flops 4608 | bytes 36864 | tf_op jit(solution)/shard_map/psum | solution.py:257
  881.4 50.4 %reduce-scatter.18.cloned.1.call-done = f32[768,96]{0,1:T(8,128)} async-done(((f32[768,768]{0,1:T(8,128)}), f32[768,96]{0,1:T(8,128)}) %reduce-scatter.18.cloned.1.call-update) | async-done | bytes 294928 | tf_op jit(solution)/shard_map/reduce_scatter | solution.py:203
  (575 shorter events, 303.6 us)
Async XLA Ops:
  8.0 69.9 %copy-start.45 = (bf16[3,96,192]{2,1,0:T(8,128)(2,1)S(1)}, bf16[3,96,192]{2,1,0:T(8,128)(2,1)}, u32[]{:S(2)}) copy-start(bf16[3,96,192]{2,1,0:T(8,128)(2,1)} %param.32) | copy-start | bytes 331780
  8.0 103.9 %all-gather.7.cloned.1.call-start = ((), (), s32[]{:S(2)}) async-start(), calls=%async_computation.9 | async-start | bytes 3932160 | tf_op jit(solution)/shard_map/all_gather | solution.py:57
  13.4 270.1 %reduce-scatter.8.cloned.1.call-start = ((), (), s32[]{:S(2)}) async-start(), calls=%async_computation.10 | async-start | bytes 7864320 | tf_op jit(solution)/shard_map/reduce_scatter | solution.py:61
  77.9 140.6 %copy-start.31 = (bf16[192,768]{0,1:T(8,128)(2,1)}, bf16[192,768]{0,1:T(8,128)(2,1)S(1)}, u32[]{:S(2)}) copy-start(bf16[192,768]{0,1:T(8,128)(2,1)S(1)} %all_gather.33) | copy-start | bytes 884740
  223.3 60.2 %copy-start.2 = (bf16[512,768]{1,0:T(8,128)(2,1)S(1)}, bf16[512,768]{1,0:T(8,128)(2,1)}, u32[]{:S(2)}) copy-start(bf16[512,768]{1,0:T(8,128)(2,1)} %param.27) | copy-start | bytes 2359300
  223.3 62.2 %copy-start.52 = (f32[768]{0:T(1024)S(1)}, f32[768]{0:T(1024)}, u32[]{:S(2)}) copy-start(f32[768]{0:T(1024)} %param.36) | copy-start | bytes 9220
  223.3 62.2 %copy-start.62 = (f32[768]{0:T(1024)S(1)}, f32[768]{0:T(1024)}, u32[]{:S(2)}) copy-start(f32[768]{0:T(1024)} %param.37) | copy-start | bytes 9220
  223.3 91.4 %all-gather.11.cloned.1.call-start = ((), (), s32[]{:S(2)}) async-start(), calls=%async_computation.12 | async-start | bytes 1327104 | tf_op jit(solution)/shard_map/all_gather | solution.py:151
  223.9 91.3 %all-gather.9.cloned.1.call-start = ((), (), s32[]{:S(2)}) async-start(), calls=%async_computation.11 | async-start | bytes 3932160 | tf_op jit(solution)/shard_map/all_gather | solution.py:65
  286.7 72.3 %all-gather.13.cloned.1.call-start = ((), (), s32[]{:S(2)}) async-start(), calls=%async_computation.13 | async-start | bytes 1327104 | tf_op jit(solution)/shard_map/all_gather | solution.py:152
  287.3 100.3 %all-gather.15.cloned.1.call-start = ((), (), s32[]{:S(2)}) async-start(), calls=%async_computation.15 | async-start | bytes 3932160 | tf_op jit(solution)/shard_map/all_gather | solution.py:65
  288.1 176.1 %reduce-scatter.12.cloned.1.call-start = ((), (), s32[]{:S(2)}) async-start(), calls=%async_computation.16 | async-start | bytes 7864320 | tf_op jit(solution)/shard_map/reduce_scatter | solution.py:69
  405.8 119.2 %reduce-scatter.10.cloned.1.call-start = ((), (), s32[]{:S(2)}) async-start(), calls=%async_computation.14 | async-start | bytes 7864320 | tf_op jit(solution)/shard_map/reduce_scatter | solution.py:69
  413.9 146.3 %all-gather.17.cloned.1.call-start = ((), (), s32[]{:S(2)}) async-start(), calls=%async_computation.17 | async-start | bytes 3932160 | tf_op jit(solution)/shard_map/all_gather | solution.py:57
  466.8 63.0 %copy-start.25 = (bf16[512,768]{1,0:T(8,128)(2,1)S(1)}, bf16[512,768]{1,0:T(8,128)(2,1)}, u32[]{:S(2)}) copy-start(bf16[512,768]{1,0:T(8,128)(2,1)} %param.29) | copy-start | bytes 2359300
  531.6 296.8 %reduce-scatter.14.cloned.1.call-start = ((), (), s32[]{:S(2)}) async-start(), calls=%async_computation.18 | async-start | bytes 7864320 | tf_op jit(solution)/shard_map/reduce_scatter | solution.py:61
  714.8 166.6 %reduce-scatter.16.cloned.1.call-start = ((), (), s32[]{:S(2)}) async-start(), calls=%async_computation.19 | async-start | bytes 2654208 | tf_op jit(solution)/shard_map/reduce_scatter | solution.py:202
  722.6 209.1 %reduce-scatter.18.cloned.1.call-start = ((), (), s32[]{:S(2)}) async-start(), calls=%async_computation.20 | async-start | bytes 2654208 | tf_op jit(solution)/shard_map/reduce_scatter | solution.py:203
  734.6 13.8 %all-to-all-start.1 = ((bf16[8,2,3,8]{3,1,2,0:T(2,128)(2,1)}), bf16[8,2,3,8]{3,1,2,0:T(2,128)(2,1)S(1)}, u32[]{:S(2)}, u32[]{:S(2)}) async-start(bf16[8,2,3,8]{3,1,2,0:T(2,128)(2,1)} %copy.279), calls=%async_computation.5 | async-start | bytes 24576 | tf_op jit(solution)/shard_map/all_to_all | solution.py:21
  748.5 22.3 %all-to-all-start.2 = ((bf16[8,192,96]{2,1,0:T(8,128)(2,1)}), bf16[8,192,96]{2,1,0:T(8,128)(2,1)}, u32[]{:S(2)}, u32[]{:S(2)}) async-start(bf16[8,192,96]{2,1,0:T(8,128)(2,1)} %bitcast.198), calls=%async_computation.6 | async-start | bytes 786432 | tf_op jit(solution)/shard_map/all_to_all | solution.py:21
  768.4 60.0 %copy-start.3 = (bf16[512,768]{1,0:T(8,128)(2,1)S(1)}, bf16[512,768]{1,0:T(8,128)(2,1)}, u32[]{:S(2)}) copy-start(bf16[512,768]{1,0:T(8,128)(2,1)} %param.27) | copy-start | bytes 2359300
  768.4 60.0 %copy-start.47 = (f32[512]{0:T(512)S(1)}, f32[512]{0:T(512)}, u32[]{:S(2)}) copy-start(f32[512]{0:T(512)} %copy-done.46) | copy-start | bytes 6148
  768.4 60.0 %copy-start.48 = (f32[768]{0:T(1024)S(1)}, f32[768]{0:T(1024)}, u32[]{:S(2)}) copy-start(f32[768]{0:T(1024)} %param.30) | copy-start | bytes 9220
  770.8 55.0 %all-to-all-start = ((bf16[8,3,96,192]{2,3,1,0:T(8,128)(2,1)}), bf16[8,3,96,192]{2,3,1,0:T(8,128)(2,1)}, u32[]{:S(2)}, u32[]{:S(2)}) async-start(bf16[8,3,96,192]{2,3,1,0:T(8,128)(2,1)} %maximum_bitcast_fusion), calls=%async_computation.4 | async-start | bytes 2359296 | tf_op jit(solution)/shard_map/all_to_all | solution.py:21
  (93 other events, 603.2 us)
Sparse Core Ops, SparseCore 0:
  13.5 31.2 all-gather.6
  223.4 59.9 reduce-scatter.7
  531.7 28.5 all-gather.16
  714.9 58.3 reduce-scatter.13
  777.2 82.7 reduce-scatter.15
  863.9 67.7 reduce-scatter.17
Sparse Core Ops, SparseCore 1:
  226.0 43.1 all-gather.10
  286.8 28.3 all-gather.8
  317.5 41.5 all-gather.12
  360.7 26.8 all-gather.14
  405.9 58.2 reduce-scatter.11
  466.7 58.2 reduce-scatter.9
where the time goes:
time: 947 us; the launch traced here: 940 us
  waiting for transfers between devices  313 us (33%)
  blocking collectives  217 us (23%)
  matrix products  193 us (20%)
  local copies, waits for them, and re-layouts  71.3 us (8%)
  other arithmetic  60 us (6%)
  loops' own time  48.9 us (5%)
  starting transfers between devices  18.6 us (2%)
  between operations  17.7 us (2%)
    reduce_scatter x2, waiting for transfers between devices, sums_mlp(): lax.psum_scatter(values_in, 'tensor', scatter_dimension=0, tiled=True)  108 us
    dot_general x42, matrix products, contract_cols(): lax.dot_general(left_mat, right_mat, (((1,), (1,)), ((), ())), preferred_...  91.4 us
    reduce_scatter x2, waiting for transfers between devices, sums_attention(): lax.psum_scatter(values_in, 'tensor', scatter_dimension=0, tiled=True)  59.5 us
    dot_general x30, matrix products, product(): return jnp.dot(left_mat, right_mat, preferred_element_type=jnp.float32)  56.5 us
    reduce_scatter x1, waiting for transfers between devices, on_device(): lax.psum_scatter(down_grad, 'dp', scatter_dimension=1, tiled=True)  50.4 us
    psum x1, blocking collectives, on_device(): lax.psum((ln1_gain_grad, ln1_bias_grad, out_bias_grad, ln2_gain_grad, ln2...  48.2 us
    dot_general x30, matrix products, contract_rows(): lax.dot_general(left_mat, right_mat, (((0,), (0,)), ((), ())), preferred_...  45 us
    unnamed x1, blocking collectives  44.5 us
  transfers between devices with their start and end apart: 15, of which 8 were waited for; matrix products, arithmetic and copies ran while one was open for 8% of the time, Pallas kernels for 0%

commit v1 on v0

v1 whole, which is shorter than its diff:
```python
import jax
import jax.numpy as jnp
from jax import lax
from jax.experimental import pallas as pl
from jax.experimental.pallas import tpu as pltpu
from jax.sharding import PartitionSpec as P

HD = 64
BLK = 256
EDGE = 512
FEW = 8
EPSILON = 1e-05
GELU_COEF = 0.7978845608028654
NT = (((1,), (1,)), ((), ()))
TN = (((0,), (0,)), ((), ()))
NN = (((1,), (0,)), ((), ()))


def dot32(left, right, dims):
    return lax.dot_general(left, right, dims, preferred_element_type=jnp.float32)


def one_document(row_total, block_a, block_b):
    low, high = EDGE // BLK, (row_total - EDGE) // BLK
    return low <= block_a < high and low <= block_b < high


def split_heads(source, first, scratch, heads, scale=None):
    for h in range(heads):
        part = source[:, first + h * HD : first + (h + 1) * HD]
        scratch[h] = part if scale is None else (part.astype(jnp.float32) * scale).astype(jnp.bfloat16)


def attend_kernel(qkv, seg_col, seg_row, out, lse, q_s, k_s, v_s, o_s, c_s):
    rows, width = out.shape
    heads = width // HD
    split_heads(qkv, 0, q_s, heads, HD ** -0.5)
    split_heads(qkv, width, k_s, heads)
    split_heads(qkv, 2 * width, v_s, heads)
    c_s[...] = jnp.broadcast_to(seg_col[...], (rows, 128))

    @pl.loop(0, heads)
    def _(h):
        for i in range(rows // BLK):
            mine = pl.ds(i * BLK, BLK)
            query = q_s[h, mine, :]
            seg_mine = c_s[mine, :]
            seg_mine = jnp.concatenate([seg_mine, seg_mine], axis=1)
            tiles = []
            for j in range(i + 1):
                other = pl.ds(j * BLK, BLK)
                score = dot32(query, k_s[h, other, :], NT)
                allowed = None
                if not one_document(rows, i, j):
                    allowed = seg_mine == seg_row[:, other]
                if i == j:
                    causal = lax.broadcasted_iota(jnp.int32, (BLK, BLK), 1) <= lax.broadcasted_iota(
                        jnp.int32, (BLK, BLK), 0
                    )
                    allowed = causal if allowed is None else allowed & causal
                if allowed is not None:
                    score = jnp.where(allowed, score, -1e30)
                tiles.append(score)
            top = tiles[0]
            for tile in tiles[1:]:
                top = jnp.maximum(top, tile)
            top = jnp.max(top, axis=1, keepdims=True)
            total = None
            mixed = None
            for j, tile in enumerate(tiles):
                weight = jnp.exp(tile - top)
                total = weight if total is None else total + weight
                term = dot32(weight.astype(jnp.bfloat16), v_s[h, pl.ds(j * BLK, BLK), :], NN)
                mixed = term if mixed is None else mixed + term
            total = jnp.sum(total, axis=1, keepdims=True)
            o_s[h, mine, :] = (mixed / total).astype(jnp.bfloat16)
            log_total = jnp.broadcast_to(top + jnp.log(total), (BLK, 128))
            lse[h, :, mine] = jnp.transpose(log_total)[0:8, :]

    for h in range(heads):
        out[:, h * HD : (h + 1) * HD] = o_s[h]


def attend(qkv, segment):
    rows = qkv.shape[0]
    width = qkv.shape[1] // 3
    heads = width // HD
    return pl.pallas_call(
        attend_kernel,
        out_shape=(
            jax.ShapeDtypeStruct((rows, width), jnp.bfloat16),
            jax.ShapeDtypeStruct((heads, 8, rows), jnp.float32),
        ),
        scratch_shapes=[pltpu.VMEM((heads, rows, HD), jnp.bfloat16)] * 4
        + [pltpu.VMEM((rows, 128), jnp.int32)],
        compiler_params=pltpu.CompilerParams(vmem_limit_bytes=48 * 2**20),
        cost_estimate=pl.CostEstimate(
            flops=heads * rows * rows * HD * 4, bytes_accessed=rows * width * 8, transcendentals=heads * rows * rows // 2
        ),
        name="attend",
    )(qkv, segment[:, None], segment[None, :])


def attend_back_kernel(
    qkv, mixed, grad, lse, seg_col, seg_row, out, q_s, k_s, v_s, g_s, d_s, dq_s, dk_s, dv_s, c_s
):
    rows, width = mixed.shape
    heads = width // HD
    split_heads(qkv, 0, q_s, heads, HD ** -0.5)
    split_heads(qkv, width, k_s, heads)
    split_heads(qkv, 2 * width, v_s, heads)
    split_heads(grad, 0, g_s, heads)
    c_s[...] = jnp.broadcast_to(seg_col[...], (rows, 128))
    for h in range(heads):
        both = mixed[:, h * HD : (h + 1) * HD].astype(jnp.float32) * g_s[h].astype(jnp.float32)
        inner = jnp.sum(both, axis=1, keepdims=True)
        d_s[h] = jnp.transpose(jnp.broadcast_to(inner, (rows, 128)))[0:8, :]

    @pl.loop(0, heads)
    def _(h):
        for i in range(rows // BLK):
            mine = pl.ds(i * BLK, BLK)
            query = q_s[h, mine, :]
            grad_mine = g_s[h, mine, :]
            log_total = lse[h, 0:1, mine]
            inner = d_s[h, 0:1, mine]
            query_grad = None
            for j in range(i + 1):
                other = pl.ds(j * BLK, BLK)
                key = k_s[h, other, :]
                score = dot32(key, query, NT)
                weight = jnp.exp(score - log_total)
                allowed = None
                if not one_document(rows, i, j):
                    seg_other = c_s[other, :]
                    seg_other = jnp.concatenate([seg_other, seg_other], axis=1)
                    allowed = seg_other == seg_row[:, mine]
                if i == j:
                    causal = lax.broadcasted_iota(jnp.int32, (BLK, BLK), 0) <= lax.broadcasted_iota(
                        jnp.int32, (BLK, BLK), 1
                    )
                    allowed = causal if allowed is None else allowed & causal
                if allowed is not None:
                    weight = jnp.where(allowed, weight, 0.0)
                weight_grad = dot32(v_s[h, other, :], grad_mine, NT)
                score_grad = (weight * (weight_grad - inner)).astype(jnp.bfloat16)
                value_term = dot32(weight.astype(jnp.bfloat16), grad_mine, NN)
                key_term = dot32(score_grad, query, NN)
                query_term = dot32(score_grad, key, TN)
                query_grad = query_term if query_grad is None else query_grad + query_term
                if i == j:
                    dv_s[h, other, :] = value_term
                    dk_s[h, other, :] = key_term
                else:
                    dv_s[h, other, :] += value_term
                    dk_s[h, other, :] += key_term
            dq_s[h, mine, :] = (query_grad * HD ** -0.5).astype(jnp.bfloat16)

    for h in range(heads):
        out[:, h * HD : (h + 1) * HD] = dq_s[h]
        out[:, width + h * HD : width + (h + 1) * HD] = dk_s[h].astype(jnp.bfloat16)
        out[:, 2 * width + h * HD : 2 * width + (h + 1) * HD] = dv_s[h].astype(jnp.bfloat16)


def attend_back(qkv, mixed, grad, lse, segment):
    rows = qkv.shape[0]
    width = qkv.shape[1] // 3
    heads = width // HD
    half = pltpu.VMEM((heads, rows, HD), jnp.bfloat16)
    full = pltpu.VMEM((heads, rows, HD), jnp.float32)
    return pl.pallas_call(
        attend_back_kernel,
        out_shape=jax.ShapeDtypeStruct((rows, 3 * width), jnp.bfloat16),
        scratch_shapes=[half, half, half, half, pltpu.VMEM((heads, 8, rows), jnp.float32), half, full, full]
        + [pltpu.VMEM((rows, 128), jnp.int32)],
        compiler_params=pltpu.CompilerParams(vmem_limit_bytes=48 * 2**20),
        cost_estimate=pl.CostEstimate(
            flops=heads * rows * rows * HD * 10, bytes_accessed=rows * width * 16, transcendentals=heads * rows * rows // 2
        ),
        name="attend_back",
    )(qkv, mixed, grad, lse, segment[:, None], segment[None, :])


def flip(values, axis, mask):
    size = lax.axis_size(axis)
    return lax.ppermute(values, axis, [(i, i ^ mask) for i in range(size)])


def core_swap(values):
    return flip(values, "tensor", 1)


def chip_swap(values):
    return flip(values, "tensor", 2)


def place(buffer, piece, index):
    return lax.dynamic_update_slice_in_dim(buffer, piece[None], index, 0)


def pick(blocks, index):
    return lax.dynamic_index_in_dim(blocks, index, 0, keepdims=False)


def gather_direct(shard, axis):
    size = lax.axis_size(axis)
    if size > FEW:
        return lax.all_gather(shard, axis)
    me = lax.axis_index(axis)
    whole = place(jnp.zeros((size,) + shard.shape, shard.dtype), shard, me)
    for mask in range(1, size):
        whole = place(whole, flip(shard, axis, mask), me ^ mask)
    return whole


def gather_two(shard):
    size = lax.axis_size("dp")
    if size > FEW:
        return lax.all_gather(shard, "dp", tiled=True)
    me = lax.axis_index("dp")
    column = place(jnp.zeros((size // 2,) + shard.shape, shard.dtype), shard, me // 2)
    for mask in range(2, size, 2):
        column = place(column, flip(shard, "dp", mask), (me ^ mask) // 2)
    other = flip(column, "dp", 1)
    whole = jnp.zeros((size // 2, 2) + shard.shape, shard.dtype)
    whole = lax.dynamic_update_slice_in_dim(whole, column[:, None], me % 2, 1)
    whole = lax.dynamic_update_slice_in_dim(whole, other[:, None], 1 - me % 2, 1)
    return whole.reshape((size * shard.shape[0],) + shard.shape[1:])


def scatter_all(whole, axis):
    blocks = low(whole).reshape((lax.axis_size(axis), -1) + whole.shape[1:])
    return jnp.sum(wide(lax.all_to_all(blocks, axis, 0, 0, tiled=True)), axis=0)


def scatter_direct(whole, axis):
    size = lax.axis_size(axis)
    if size > FEW:
        return scatter_all(whole, axis)
    me = lax.axis_index(axis)
    blocks = whole.reshape((size, -1) + whole.shape[1:])
    total = pick(blocks, me).astype(jnp.float32)
    low = blocks.astype(jnp.bfloat16)
    for mask in range(1, size):
        total = total + flip(pick(low, me ^ mask), axis, mask).astype(jnp.float32)
    return total


def scatter_two(whole):
    size = lax.axis_size("dp")
    if size > FEW:
        return scatter_all(whole, "dp")
    me = lax.axis_index("dp")
    blocks = whole.reshape((size // 2, 2, -1) + whole.shape[1:])
    keep = lax.dynamic_index_in_dim(blocks, me % 2, 1, keepdims=False)
    give = lax.dynamic_index_in_dim(blocks, 1 - me % 2, 1, keepdims=False)
    column = keep.astype(jnp.float32) + flip(give.astype(jnp.bfloat16), "dp", 1).astype(jnp.float32)
    total = pick(column, me // 2)
    low = column.astype(jnp.bfloat16)
    for mask in range(2, size, 2):
        total = total + flip(pick(low, (me ^ mask) // 2), "dp", mask).astype(jnp.float32)
    return total


def sum_everywhere(values):
    for mask in (1, 2):
        values = values + flip(values, "tensor", mask)
    mask = 1
    while mask < lax.axis_size("dp"):
        values = values + flip(values, "dp", mask)
        mask *= 2
    return values


def normalized(values_in):
    row_mean = jnp.mean(values_in, axis=-1, keepdims=True)
    centered = values_in - row_mean
    variance = jnp.mean(centered * centered, axis=-1, keepdims=True)
    return centered * lax.rsqrt(variance + EPSILON)


def layer_norm(values_in, gain_vec, shift_vec):
    return normalized(values_in) * gain_vec + shift_vec


def gelu_tanh(values_in):
    return (
        0.5
        * values_in
        * (1.0 + jnp.tanh(GELU_COEF * (values_in + 0.044715 * values_in * values_in * values_in)))
    )


def product(left_mat, right_mat):
    return jnp.dot(left_mat, right_mat, preferred_element_type=jnp.float32)


def contract_rows(left_mat, right_mat):
    return lax.dot_general(left_mat, right_mat, TN, preferred_element_type=jnp.float32)


def contract_cols(left_mat, right_mat):
    return lax.dot_general(left_mat, right_mat, NT, preferred_element_type=jnp.float32)


def low(values):
    return values.astype(jnp.bfloat16)


def wide(values):
    return values.astype(jnp.float32)


def on_device(
    tokens,
    segment,
    cotangent,
    ln1_gain,
    ln1_bias,
    w_qkv,
    qv_bias,
    w_out,
    out_bias,
    ln2_gain,
    ln2_bias,
    w_up,
    up_bias,
    w_down,
    down_bias,
):
    dp = lax.axis_size("dp")
    place_dp = lax.axis_index("dp")
    me = lax.axis_index("tensor")
    own, width = tokens.shape
    rows_shard = w_qkv.shape[1]
    span = w_qkv.shape[2]
    hidden = w_up.shape[1]

    biases = jnp.concatenate([qv_bias.reshape(-1), up_bias.reshape(-1)])
    bias_rows = jnp.zeros((16, 3 * span), jnp.bfloat16).at[0, : biases.shape[0]].set(biases)
    pack = jnp.concatenate([jnp.swapaxes(w_qkv, 0, 1).reshape(rows_shard, 3 * span), bias_rows], axis=0)
    packs = gather_direct(pack, "dp")
    qkv_full = packs[:, :rows_shard].reshape(dp * rows_shard, 3 * span)
    bias_parts = packs[:, rows_shard, : biases.shape[0]]
    qv_full = jnp.moveaxis(bias_parts[:, : qv_bias.size].reshape((dp,) + qv_bias.shape), 0, 2).reshape(2, span)
    up_bias_own = jnp.moveaxis(
        bias_parts[:, qv_bias.size :].reshape((dp,) + up_bias.shape), 0, 1
    ).reshape(hidden)
    up_bias_pair = wide(jnp.concatenate([up_bias_own, chip_swap(up_bias_own)]))

    from_chip = chip_swap(tokens)
    token_pieces = [tokens, core_swap(tokens), from_chip, core_swap(from_chip)]
    first_norm = jnp.zeros((4, own, width), jnp.bfloat16)
    for mask, piece in enumerate(token_pieces):
        first_norm = place(first_norm, low(layer_norm(wide(piece), ln1_gain, ln1_bias)), me ^ mask)
    first_norm = first_norm.reshape(4 * own, width)
    qkv_bias = wide(jnp.concatenate([qv_full[0], jnp.zeros_like(qv_full[0]), qv_full[1]]))
    qkv = low(product(first_norm, qkv_full) + qkv_bias)

    out_t = gather_direct(w_out.T, "dp").reshape(dp * rows_shard, span)
    out_own = out_t.T
    out_chip = chip_swap(out_own)
    out_near = jnp.concatenate([out_own, core_swap(out_own)], axis=0)
    out_far = jnp.concatenate([out_chip, core_swap(out_chip)], axis=0)
    up_pair = gather_two(jnp.concatenate([w_up, chip_swap(w_up)], axis=1))
    down_own = gather_two(w_down.T)
    down_chip = chip_swap(down_own)
    grad_pair = jnp.concatenate([cotangent, core_swap(cotangent)], axis=0)

    heads_out, log_totals = attend(qkv, segment)

    blocks = heads_out.reshape(4, own, span)
    to_core = jnp.stack([pick(blocks, me ^ 1), pick(blocks, me ^ 3)])
    from_core = core_swap(to_core)
    mixed_near = jnp.concatenate([pick(blocks, me), from_core[0]], axis=1)
    mixed_far = chip_swap(jnp.concatenate([pick(blocks, me ^ 2), from_core[1]], axis=1))
    token_rows = wide(tokens)
    attn_branch = product(mixed_near, out_near) + product(mixed_far, out_far)
    hidden_one = token_rows + (attn_branch + wide(out_bias))

    second_own = low(layer_norm(hidden_one, ln2_gain, ln2_bias))
    second = jnp.concatenate([second_own, core_swap(second_own)], axis=0)
    pre_act = product(second, up_pair) + up_bias_pair
    activation = low(gelu_tanh(pre_act))
    act_grad = jnp.concatenate([product(grad_pair, down_own), product(grad_pair, down_chip)], axis=1)
    pre_grad = low(jax.vjp(gelu_tanh, pre_act)[1](act_grad)[0])
    second_part = contract_cols(pre_grad, up_pair)
    second_grad = second_part[:own] + wide(core_swap(low(second_part[own:])))
    norm_pull = jax.vjp(layer_norm, hidden_one, ln2_gain, ln2_bias)[1]
    hidden_grad_norm, ln2_gain_grad, ln2_bias_grad = norm_pull(second_grad)
    hidden_grad = wide(cotangent) + hidden_grad_norm

    mlp_part = contract_cols(activation[:, :hidden], down_own) + contract_cols(activation[:, hidden:], down_chip)
    mlp_branch = mlp_part[:own] + wide(core_swap(low(mlp_part[own:])))
    block_out = hidden_one + (mlp_branch + wide(down_bias))

    down_part = scatter_two(contract_rows(grad_pair, activation))
    down_grad_out = (down_part[:, :hidden] + wide(chip_swap(low(down_part[:, hidden:])))).T
    up_part = contract_rows(second, pre_grad)
    up_grad_out = scatter_two(up_part[:, :hidden] + wide(chip_swap(low(up_part[:, hidden:]))))

    grad_attn = low(hidden_grad)
    grad_near = low(contract_cols(grad_attn, out_near))
    grad_far = chip_swap(low(contract_cols(grad_attn, out_far)))
    grad_core = core_swap(jnp.stack([grad_near[:, span:], grad_far[:, span:]]))
    heads_grad = jnp.zeros((4, own, span), jnp.bfloat16)
    for mask, piece in enumerate((grad_near[:, :span], grad_core[0], grad_far[:, :span], grad_core[1])):
        heads_grad = place(heads_grad, piece, me ^ mask)
    heads_grad = heads_grad.reshape(4 * own, span)

    out_part_near = contract_rows(mixed_near, grad_attn)
    out_part_far = contract_rows(mixed_far, grad_attn)
    out_core = core_swap(low(jnp.stack([out_part_near[span:], out_part_far[span:]])))
    out_grad = out_part_near[:span] + wide(out_core[0])
    out_grad = out_grad + wide(chip_swap(low(out_part_far[:span] + wide(out_core[1]))))
    w_out_grad_out = scatter_direct(out_grad.T, "dp").T

    up_bias_sum = jnp.sum(wide(pre_grad), axis=0)
    up_bias_rows = jnp.zeros((4, hidden), jnp.float32)
    up_bias_rows = place(up_bias_rows, up_bias_sum[:hidden], me)
    up_bias_rows = place(up_bias_rows, up_bias_sum[hidden:], me ^ 2)
    early = lax.psum(
        jnp.concatenate(
            [
                jnp.stack(
                    [
                        jnp.sum(wide(grad_attn), axis=0),
                        ln2_gain_grad,
                        ln2_bias_grad,
                        jnp.sum(wide(cotangent), axis=0),
                    ]
                ).reshape(-1),
                up_bias_rows.reshape(-1),
            ]
        ),
        ("dp", "tensor"),
    )
    vectors = early[: 4 * width].reshape(4, width)
    up_bias_grad = pick(early[4 * width :].reshape((4,) + (up_bias.shape[0], dp, up_bias.shape[1])), me)
    up_bias_grad = lax.dynamic_index_in_dim(up_bias_grad, place_dp, 1, keepdims=False)

    qkv_grad = attend_back(qkv, heads_out, heads_grad, log_totals, segment)

    grad_blocks = qkv_grad.reshape(4, own, 3 * span)
    parts = [None] * 4
    for mask in (3, 2, 1, 0):
        parts[mask] = contract_cols(pick(grad_blocks, me ^ mask), qkv_full)
    first_grad_chip = chip_swap(low(parts[2] + wide(core_swap(low(parts[3])))))
    first_grad = parts[0] + wide(core_swap(low(parts[1]))) + wide(first_grad_chip)
    qkv_sum = scatter_direct(contract_rows(first_norm, qkv_grad), "dp")
    w_qkv_grad_out = jnp.swapaxes(qkv_sum.reshape(rows_shard, 3, span), 0, 1)

    ln1_gain_part = 0.0
    ln1_bias_part = 0.0
    for part, piece in zip(parts, token_pieces):
        ln1_gain_part = ln1_gain_part + jnp.sum(part * normalized(wide(piece)), axis=0)
        ln1_bias_part = ln1_bias_part + jnp.sum(part, axis=0)
    qkv_bias_sum = jnp.sum(wide(qkv_grad), axis=0).reshape(3, span)
    bias_spread = jnp.zeros((4, 2, span), jnp.float32)
    bias_spread = place(bias_spread, jnp.stack([qkv_bias_sum[0], qkv_bias_sum[2]]), me)
    late = sum_everywhere(
        jnp.concatenate([ln1_gain_part, ln1_bias_part, bias_spread.reshape(-1)]).reshape(4, -1)
    ).reshape(-1)
    qv_bias_grad = pick(late[2 * width :].reshape((4, 2, qv_bias.shape[1], dp, qv_bias.shape[2])), me)
    qv_bias_grad = lax.dynamic_index_in_dim(qv_bias_grad, place_dp, 2, keepdims=False)

    first_pull = jax.vjp(lambda v: layer_norm(v, ln1_gain, ln1_bias), token_rows)[1]
    token_grad = hidden_grad + first_pull(first_grad)[0]
    return (
        block_out,
        token_grad,
        late[:width],
        late[width : 2 * width],
        w_qkv_grad_out,
        qv_bias_grad,
        w_out_grad_out,
        vectors[0],
        vectors[1],
        vectors[2],
        up_grad_out,
        up_bias_grad,
        down_grad_out,
        vectors[3],
    )


def solution(mesh):
    in_specs = (
        P(("dp", "tensor"), None),
        P("dp"),
        P(("dp", "tensor"), None),
        P(),
        P(),
        P(None, "dp", "tensor"),
        P(None, "tensor", "dp"),
        P("tensor", "dp"),
        P(),
        P(),
        P(),
        P("dp", "tensor"),
        P("tensor", "dp"),
        P("tensor", "dp"),
        P(),
    )
    out_specs = (
        P(("dp", "tensor"), None),
        P(("dp", "tensor"), None),
        P(),
        P(),
        P(None, "dp", "tensor"),
        P(None, "tensor", "dp"),
        P("tensor", "dp"),
        P(),
        P(),
        P(),
        P("dp", "tensor"),
        P("tensor", "dp"),
        P("tensor", "dp"),
        P(),
    )
    return jax.shard_map(
        on_device, mesh=mesh, in_specs=in_specs, out_specs=out_specs, check_vma=False
    )
```

time: 947 us -> 573 us (0.61)
  waiting for transfers between devices: 313 us -> 112 us
  blocking collectives: 217 us -> 37 us
  matrix products: 193 us -> 60 us
  local copies, waits for them, and re-layouts: 71.3 us -> 164 us
  starting transfers between devices: 18.6 us -> 83.6 us
  Pallas kernels: 0 us -> 57.5 us
  loops' own time: 48.9 us -> 0 us
  between operations: 17.7 us -> 2.71 us
  other arithmetic: 60 us -> 49.6 us
    reduce_scatter x6 -> x0, waiting for transfers between devices: 218 us -> none  [the longest x2 108 us: sums_mlp(): lax.psum_scatter(values_in, 'tensor', scatter_dimension=0, tiled=True)]
    all_gather x4 -> x0, blocking collectives: 124 us -> none  [the longest x1 34 us: on_device(): lax.all_gather(w_qkv, 'dp', axis=1, tiled=True)]
    ppermute x0 -> x73, waiting for transfers between devices: none -> 112 us  [flip(): return lax.ppermute(values, axis, [(i, i ^ mask) for i in range(size)])]
    dot_general x72 -> x14, matrix products: 136 us -> 36.2 us  [the longest x9 21.5 us: contract_cols(): lax.dot_general(left_mat, right_mat, NT, preferred_element_type=jnp.float32)]
    all_gather x6 -> x0, waiting for transfers between devices: 93.7 us -> none  [the longest x1 36.4 us: on_device(): lax.all_gather(w_down, 'dp', axis=1, tiled=True)]
    ppermute x0 -> x73, starting transfers between devices: none -> 83.6 us  [flip(): return lax.ppermute(values, axis, [(i, i ^ mask) for i in range(size)])]
    dynamic_update_slice x12 -> x34, local copies, waits for them, and re-layouts: 0.6 us -> 82 us  [the longest x30 76.4 us: place(): return lax.dynamic_update_slice_in_dim(buffer, piece[None], index, 0)]
    pallas_call x0 -> x2, Pallas kernels: none -> 57.5 us  [the longest x1 39.6 us: attend_back(): pl.pallas_call(attend_back_kernel, out_shape=jax.ShapeDtypeStruct((rows,...]
  transfers between devices with their start and end apart: 15 -> 73, of which waited for: 8 -> 21; matrix products, arithmetic and copies ran while one was open for 8% -> 41% of each run, Pallas kernels for 0% -> 10%
where the time goes in v1:
time: 573 us; the launch traced here: 567 us
  local copies, waits for them, and re-layouts  164 us (29%)
  waiting for transfers between devices  112 us (20%)
  starting transfers between devices  83.6 us (15%)
  matrix products  60 us (10%)
  Pallas kernels  57.5 us (10%)
  other arithmetic  49.6 us (9%)
  blocking collectives  37 us (6%)
    ppermute x73, waiting for transfers between devices, flip(): return lax.ppermute(values, axis, [(i, i ^ mask) for i in range(size)])  112 us
    ppermute x73, starting transfers between devices, flip(): return lax.ppermute(values, axis, [(i, i ^ mask) for i in range(size)])  83.6 us
    dynamic_update_slice x30, local copies, waits for them, and re-layouts, place(): return lax.dynamic_update_slice_in_dim(buffer, piece[None], index, 0)  76.4 us
    pallas_call x1, Pallas kernels, attend_back(): pl.pallas_call(attend_back_kernel, out_shape=jax.ShapeDtypeStruct((rows,...  39.6 us
    psum x1, blocking collectives, on_device(): lax.psum(jnp.concatenate([jnp.stack([jnp.sum(wide(grad_attn), axis=0), ln...  37 us
    unnamed x217, local copies, waits for them, and re-layouts  24.3 us
    dot_general x6, matrix products, product(): return jnp.dot(left_mat, right_mat, preferred_element_type=jnp.float32)  23.7 us
    dot_general x9, matrix products, contract_cols(): lax.dot_general(left_mat, right_mat, NT, preferred_element_type=jnp.float32)  21.5 us
  transfers between devices with their start and end apart: 73, of which 21 were waited for; matrix products, arithmetic and copies ran while one was open for 41% of the time, Pallas kernels for 10%

profile of v1, /device:TPU:0, one launch (start us, length us, event | category | flops | bytes accessed | tf_op | source)
XLA Modules:
  0.0 566.8 jit_solution(5990739187374539925)
XLA Ops:
  29.9 7.0 %dynamic_update_slice.121 = bf16[8,112,576]{2,0,1:T(8,128)(2,1)} dynamic-update-slice(bf16[8,112,576]{2,0,1:T(8,128)(2,1)} %broadcast_in_dim.208, bf16[1,112,576]{2,0,1:T(2,128)(2,1)S(1)} %copy.86, s32[]{:T(128)S(6)} %select_n.185, s32[]{:T(128)} %constant.314.clone.1, s32[]{:T(128)} %constant.314.clone.1) | dynamic-update-slice | bytes 258052 | tf_op jit(solution)/shard_map/dynamic_update_slice | solution.py:198
  82.8 6.5 %dynamic_update_slice.122 = bf16[8,112,576]{2,0,1:T(8,128)(2,1)} dynamic-update-slice(bf16[8,112,576]{2,0,1:T(8,128)(2,1)} %dynamic_update_slice.121, bf16[1,112,576]{2,0,1:T(2,128)(2,1)S(1)} %copy.87, s32[]{:T(128)S(6)} %select_n.186, s32[]{:T(128)} %constant.314.clone.1, s32[]{:T(128)} %constant.314.clone.1) | dynamic-update-slice | bytes 258052 | tf_op jit(solution)/shard_map/dynamic_update_slice | solution.py:198
  89.3 6.6 %dynamic_update_slice.123 = bf16[8,112,576]{2,0,1:T(8,128)(2,1)} dynamic-update-slice(bf16[8,112,576]{2,0,1:T(8,128)(2,1)} %dynamic_update_slice.122, bf16[1,112,576]{2,0,1:T(2,128)(2,1)} %copy.88, s32[]{:T(128)S(6)} %select_n.187, s32[]{:T(128)} %constant.314.clone.1, s32[]{:T(128)} %constant.314.clone.1) | dynamic-update-slice | bytes 258052 | tf_op jit(solution)/shard_map/dynamic_update_slice | solution.py:198
  95.9 6.5 %dynamic_update_slice.124 = bf16[8,112,576]{2,0,1:T(8,128)(2,1)} dynamic-update-slice(bf16[8,112,576]{2,0,1:T(8,128)(2,1)} %dynamic_update_slice.123, bf16[1,112,576]{2,0,1:T(2,128)(2,1)} %copy.89, s32[]{:T(128)S(6)} %select_n.188, s32[]{:T(128)} %constant.314.clone.1, s32[]{:T(128)} %constant.314.clone.1) | dynamic-update-slice | bytes 258052 | tf_op jit(solution)/shard_map/dynamic_update_slice | solution.py:198
  102.4 6.5 %dynamic_update_slice.125 = bf16[8,112,576]{2,0,1:T(8,128)(2,1)} dynamic-update-slice(bf16[8,112,576]{2,0,1:T(8,128)(2,1)} %dynamic_update_slice.124, bf16[1,112,576]{2,0,1:T(2,128)(2,1)} %copy.90, s32[]{:T(128)S(6)} %select_n.189, s32[]{:T(128)} %constant.314.clone.1, s32[]{:T(128)} %constant.314.clone.1) | dynamic-update-slice | bytes 258052 | tf_op jit(solution)/shard_map/dynamic_update_slice | solution.py:198
  108.9 6.5 %dynamic_update_slice.126 = bf16[8,112,576]{2,0,1:T(8,128)(2,1)} dynamic-update-slice(bf16[8,112,576]{2,0,1:T(8,128)(2,1)} %dynamic_update_slice.125, bf16[1,112,576]{2,0,1:T(2,128)(2,1)} %copy.91, s32[]{:T(128)S(6)} %select_n.190, s32[]{:T(128)} %constant.314.clone.1, s32[]{:T(128)} %constant.314.clone.1) | dynamic-update-slice | bytes 258052 | tf_op jit(solution)/shard_map/dynamic_update_slice | solution.py:198
  115.4 6.5 %dynamic_update_slice.127 = bf16[8,112,576]{2,0,1:T(8,128)(2,1)} dynamic-update-slice(bf16[8,112,576]{2,0,1:T(8,128)(2,1)} %dynamic_update_slice.126, bf16[1,112,576]{2,0,1:T(2,128)(2,1)} %copy.92, s32[]{:T(128)S(6)} %select_n.191, s32[]{:T(128)} %constant.314.clone.1, s32[]{:T(128)} %constant.314.clone.1) | dynamic-update-slice | bytes 258052 | tf_op jit(solution)/shard_map/dynamic_update_slice | solution.py:198
  121.9 6.6 %dynamic_update_slice.128 = bf16[8,112,576]{2,0,1:T(8,128)(2,1)} dynamic-update-slice(bf16[8,112,576]{2,0,1:T(8,128)(2,1)} %dynamic_update_slice.127, bf16[1,112,576]{2,0,1:T(2,128)(2,1)S(1)} %copy-done.52, s32[]{:T(128)S(6)} %select_n.192, s32[]{:T(128)} %constant.314.clone.1, s32[]{:T(128)} %constant.314.clone.1) | dynamic-update-slice | bytes 258052 | tf_op jit(solution)/shard_map/dynamic_update_slice | solution.py:198
  158.1 13.3 %collective-permute-done.25 = bf16[96,1536]{1,0:T(8,128)(2,1)S(1)} collective-permute-done((bf16[96,1536]{1,0:T(8,128)(2,1)S(1)}, bf16[96,1536]{1,0:T(8,128)(2,1)S(1)}, u32[]{:S(2)}, u32[]{:S(2)}) %collective-permute-start.25) | collective-permute-done | bytes 294944 | tf_op jit(solution)/shard_map/ppermute | solution.py:186
  173.3 8.4 %collective-permute-done.26 = bf16[96,1536]{1,0:T(8,128)(2,1)S(1)} collective-permute-done((bf16[96,1536]{1,0:T(8,128)(2,1)S(1)}, bf16[96,1536]{1,0:T(8,128)(2,1)S(1)}, u32[]{:S(2)}, u32[]{:S(2)}) %collective-permute-start.26) | collective-permute-done | bytes 294944 | tf_op jit(solution)/shard_map/ppermute | solution.py:186
  191.9 4.5 add_convert_fusion.qkv
  196.5 17.9 %attend.1 = (bf16[2048,192]{1,0:T(8,128)(2,1)S(1)}, f32[3,8,2048]{2,1,0:T(8,128)S(1)}) custom-call(bf16[2048,576]{1,0:T(8,128)(2,1)S(1)} %add_convert_fusion.qkv, s32[2048,1]{1,0:T(8,128)S(1)} %copy.98.seg_col, s32[1,2048]{1,0:T(1,128)S(1)} %bitcast.292), custom_call_target="tpu_custom_call" | custom-call | flops 3221225472 | bytes 3145728 | tf_op jit(solution)/shard_map/attend/pallas_call | solution.py:88
  223.5 4.9 fusion.125
  228.4 4.8 copy.118
  233.3 23.4 %collective-permute-done.19 = bf16[512,384]{1,0:T(8,128)(2,1)S(1)} collective-permute-done((bf16[512,384]{1,0:T(8,128)(2,1)S(1)}, bf16[512,384]{1,0:T(8,128)(2,1)S(1)}, u32[]{:S(2)}, u32[]{:S(2)}) %collective-permute-start.19) | collective-permute-done | bytes 393248 | tf_op jit(solution)/shard_map/ppermute | solution.py:186
  265.3 9.2 %convert_reduce_fusion = (f32[1536]{0:T(1024)S(1)}, bf16[1024,1536]{1,0:T(8,128)(2,1)S(1)}, bf16[1024,1536]{1,0:T(8,128)(2,1)S(1)}) fusion(f32[1024,768]{1,0:T(8,128)S(1)} %fusion.126, f32[1024,768]{1,0:T(8,128)S(1)} %copy-done.102, f32[1536]{0:T(1024)S(1)} %maximum_convert_fusion, bf16[768,1536]{1,0:T(8,128)(2,1)S(1)} %bitcast.306, ...), kind=kOutput, calls=%fused_computation.11 | convolution fusion | flops 2466249216 | bytes 16527360 | tf_op jit(solution)/shard_map/dot_general | solution.py:295
  287.3 5.2 fusion.49
  318.9 12.3 %collective-permute-done.68 = bf16[4,96,1536]{2,1,0:T(8,128)(2,1)} collective-permute-done((bf16[4,96,1536]{2,1,0:T(8,128)(2,1)}, bf16[4,96,1536]{2,1,0:T(8,128)(2,1)}, u32[]{:S(2)}, u32[]{:S(2)}) %collective-permute-start.68) | collective-permute-done | bytes 1179680 | tf_op jit(solution)/shard_map/ppermute | solution.py:186
  348.1 17.3 %collective-permute-done.70 = bf16[96,1536]{1,0:T(8,128)(2,1)} collective-permute-done((bf16[96,1536]{1,0:T(8,128)(2,1)}, bf16[96,1536]{1,0:T(8,128)(2,1)}, u32[]{:S(2)}, u32[]{:S(2)}) %collective-permute-start.70) | collective-permute-done | bytes 294944 | tf_op jit(solution)/shard_map/ppermute | solution.py:186
  373.9 39.6 %attend_back.1 = bf16[2048,576]{1,0:T(8,128)(2,1)S(1)} custom-call(bf16[2048,576]{1,0:T(8,128)(2,1)} %copy-done.7, bf16[2048,192]{1,0:T(8,128)(2,1)S(1)} %copy-done.1, bf16[2048,192]{1,0:T(8,128)(2,1)S(1)} %bitcast.290, f32[3,8,2048]{2,1,0:T(8,128)S(1)} %get-tuple-element.29.lse, s32[2048,1]{1,0:T(8,128)S(1)} %copy-done.3, s32[1,2048]{1,0:T(1,128)S(1)} %bitcast.293), custom_call_target="tpu_custom_call" | custom-call | flops 8053063680 | bytes 6291456 | tf_op jit(solution)/shard_map/attend_back/pallas_call | solution.py:171
  418.0 5.8 %fusion.123 = (bf16[8,96,576]{2,1,0:T(8,128)(2,1)S(1)}, f32[8,96,576]{2,1,0:T(8,128)}) fusion(bf16[8,96,2048]{2,1,0:T(8,128)(2,1)} %bitcast.305, bf16[2048,576]{1,0:T(8,128)(2,1)S(1)} %attend_back.1), kind=kOutput, calls=%fused_computation.267 | convolution fusion | flops 1812381696 | bytes 8159232 | tf_op jit(solution)/shard_map/dot_general | solution.py:299
  455.8 11.2 %collective-permute-done.47 = bf16[96,576]{1,0:T(8,128)(2,1)} collective-permute-done((bf16[96,576]{1,0:T(8,128)(2,1)}, bf16[96,576]{1,0:T(8,128)(2,1)}, u32[]{:S(2)}, u32[]{:S(2)}) %collective-permute-start.47) | collective-permute-done | bytes 110624 | tf_op jit(solution)/shard_map/ppermute | solution.py:186
  496.8 4.7 collective-permute-done.66
  519.0 37.0 %psum.7 = f32[6144]{0:T(1024)S(1)} all-reduce(f32[6144]{0:T(1024)S(1)} %pad_maximum_fusion.14), channel_id=1, replica_groups=mesh['dp'=8,'tensor'=4] {'dp','tensor'}, use_global_device_ids=true, to_apply=%region_28.29 | all-reduce | flops 6144 | bytes 49152 | tf_op jit(solution)/shard_map/psum | solution.py:422
  (561 shorter events, 291.9 us)
Async XLA Ops:
  4.4 40.6 %collective-permute-start.3 = (bf16[112,576]{0,1:T(8,128)(2,1)}, bf16[112,576]{0,1:T(8,128)(2,1)}, u32[]{:S(2)}, u32[]{:S(2)}) collective-permute-start(bf16[112,576]{0,1:T(8,128)(2,1)} %fusion.91), channel_id=1, source_target_pairs={{0,4},{4,0},{8,12},{12,8},{16,20},{20,16},{24,28},{28,24},{1,5},{5... | collective-permute-start | bytes 387080 | tf_op jit(solution)/shard_map/ppermute | solution.py:186
  7.3 39.1 %collective-permute-start.4 = (bf16[112,576]{0,1:T(8,128)(2,1)}, bf16[112,576]{0,1:T(8,128)(2,1)}, u32[]{:S(2)}, u32[]{:S(2)}) collective-permute-start(bf16[112,576]{0,1:T(8,128)(2,1)} %fusion.91), channel_id=1, source_target_pairs={{0,8},{4,12},{8,0},{12,4},{16,24},{20,28},{24,16},{28,20},{1,9},{5... | collective-permute-start | bytes 387080 | tf_op jit(solution)/shard_map/ppermute | solution.py:186
  39.3 32.2 %collective-permute-start.5 = (bf16[112,576]{0,1:T(8,128)(2,1)}, bf16[112,576]{0,1:T(8,128)(2,1)}, u32[]{:S(2)}, u32[]{:S(2)}) collective-permute-start(bf16[112,576]{0,1:T(8,128)(2,1)} %fusion.91), channel_id=1, source_target_pairs={{0,12},{4,8},{8,4},{12,0},{16,28},{20,24},{24,20},{28,16},{1,13},{... | collective-permute-start | bytes 387080 | tf_op jit(solution)/shard_map/ppermute | solution.py:186
  41.0 32.3 %collective-permute-start.6 = (bf16[112,576]{0,1:T(8,128)(2,1)}, bf16[112,576]{0,1:T(8,128)(2,1)}, u32[]{:S(2)}, u32[]{:S(2)}) collective-permute-start(bf16[112,576]{0,1:T(8,128)(2,1)} %fusion.91), channel_id=1, source_target_pairs={{0,16},{4,20},{8,24},{12,28},{16,0},{20,4},{24,8},{28,12},{1,17},{... | collective-permute-start | bytes 387080 | tf_op jit(solution)/shard_map/ppermute | solution.py:186
  43.7 33.0 %collective-permute-start.7 = (bf16[112,576]{0,1:T(8,128)(2,1)}, bf16[112,576]{0,1:T(8,128)(2,1)}, u32[]{:S(2)}, u32[]{:S(2)}) collective-permute-start(bf16[112,576]{0,1:T(8,128)(2,1)} %fusion.91), channel_id=1, source_target_pairs={{0,20},{4,16},{8,28},{12,24},{16,4},{20,0},{24,12},{28,8},{1,21},{... | collective-permute-start | bytes 387080 | tf_op jit(solution)/shard_map/ppermute | solution.py:186
  44.9 33.8 %collective-permute-start.8 = (bf16[112,576]{0,1:T(8,128)(2,1)}, bf16[112,576]{0,1:T(8,128)(2,1)}, u32[]{:S(2)}, u32[]{:S(2)}) collective-permute-start(bf16[112,576]{0,1:T(8,128)(2,1)} %fusion.91), channel_id=1, source_target_pairs={{0,24},{4,28},{8,16},{12,20},{16,8},{20,12},{24,0},{28,4},{1,25},{... | collective-permute-start | bytes 387080 | tf_op jit(solution)/shard_map/ppermute | solution.py:186
  46.4 34.6 %collective-permute-start.9 = (bf16[112,576]{0,1:T(8,128)(2,1)}, bf16[112,576]{0,1:T(8,128)(2,1)}, u32[]{:S(2)}, u32[]{:S(2)}) collective-permute-start(bf16[112,576]{0,1:T(8,128)(2,1)} %fusion.91), channel_id=1, source_target_pairs={{0,28},{4,24},{8,20},{12,16},{16,12},{20,8},{24,4},{28,0},{1,29},{... | collective-permute-start | bytes 387080 | tf_op jit(solution)/shard_map/ppermute | solution.py:186
  71.5 111.0 %collective-permute-start = (bf16[512,768]{1,0:T(8,128)(2,1)S(1)}, bf16[512,768]{1,0:T(8,128)(2,1)}, u32[]{:S(2)}, u32[]{:S(2)}) collective-permute-start(bf16[512,768]{1,0:T(8,128)(2,1)S(1)} %copy-done.8), channel_id=1, source_target_pairs={{0,1},{1,0},{2,3},{3,2},{4,5},{5,4},{6,7},{7,6},{8,9},{9,8},{10,11... | collective-permute-start | bytes 2359304 | tf_op jit(solution)/shard_map/ppermute | solution.py:186
  73.3 112.0 %collective-permute-start.1 = (bf16[512,768]{1,0:T(8,128)(2,1)S(1)}, bf16[512,768]{1,0:T(8,128)(2,1)S(1)}, u32[]{:S(2)}, u32[]{:S(2)}) collective-permute-start(bf16[512,768]{1,0:T(8,128)(2,1)S(1)} %copy-done.8), channel_id=1, source_target_pairs={{0,2},{1,3},{2,0},{3,1},{4,6},{5,7},{6,4},{7,5},{8,10},{9,11},{10,... | collective-permute-start | bytes 2359304 | tf_op jit(solution)/shard_map/ppermute | solution.py:186
  76.6 145.7 %collective-permute-start.35 = (bf16[512,768]{1,0:T(8,128)(2,1)}, bf16[512,768]{1,0:T(8,128)(2,1)}, u32[]{:S(2)}, u32[]{:S(2)}) collective-permute-start(bf16[512,768]{1,0:T(8,128)(2,1)} %param.19), channel_id=1, source_target_pairs={{0,1},{1,0},{2,3},{3,2},{4,5},{5,4},{6,7},{7,6},{8,9},{9,8},{10,11... | collective-permute-start | bytes 2359304 | tf_op jit(solution)/shard_map/ppermute | solution.py:186
  78.7 56.0 %collective-permute-start.23 = (bf16[96,768]{1,0:T(8,128)(2,1)S(1)}, bf16[96,768]{1,0:T(8,128)(2,1)}, u32[]{:S(2)}, u32[]{:S(2)}) collective-permute-start(bf16[96,768]{1,0:T(8,128)(2,1)S(1)} %copy-done.60), channel_id=1, source_target_pairs={{0,2},{1,3},{2,0},{3,1},{4,6},{5,7},{6,4},{7,5},{8,10},{9,11},{10,... | collective-permute-start | bytes 442376 | tf_op jit(solution)/shard_map/ppermute | solution.py:186
  154.7 102.6 %collective-permute-start.18 = (bf16[192,768]{1,0:T(8,128)(2,1)S(1)}, bf16[192,768]{1,0:T(8,128)(2,1)}, u32[]{:S(2)}, u32[]{:S(2)}) collective-permute-start(bf16[192,768]{1,0:T(8,128)(2,1)S(1)} %bitcast.312), channel_id=1, source_target_pairs={{0,1},{1,0},{2,3},{3,2},{4,5},{5,4},{6,7},{7,6},{8,9},{9,8},{10,11... | collective-permute-start | bytes 884744 | tf_op jit(solution)/shard_map/ppermute | solution.py:186
  181.7 37.5 %collective-permute-start.32 = (bf16[4,96,768]{2,1,0:T(8,128)(2,1)}, bf16[4,96,768]{2,1,0:T(8,128)(2,1)S(1)}, u32[]{:S(2)}, u32[]{:S(2)}) collective-permute-start(bf16[4,96,768]{2,1,0:T(8,128)(2,1)} %bitcast_dynamic-update-slice_fusion.9), channel_id=1, source_target_pairs={{0,4},{4,0},{8,12},{12,8},{16,20},{20,16},{24,28},{28,24},{1,5},{5... | collective-permute-start | bytes 1769480 | tf_op jit(solution)/shard_map/ppermute | solution.py:186
  182.4 34.6 %collective-permute-start.21 = (bf16[192,768]{1,0:T(8,128)(2,1)S(1)}, bf16[192,768]{1,0:T(8,128)(2,1)S(1)}, u32[]{:S(2)}, u32[]{:S(2)}) collective-permute-start(bf16[192,768]{1,0:T(8,128)(2,1)S(1)} %collective-permute-done.20), channel_id=1, source_target_pairs={{0,1},{1,0},{2,3},{3,2},{4,5},{5,4},{6,7},{7,6},{8,9},{9,8},{10,11... | collective-permute-start | bytes 884744 | tf_op jit(solution)/shard_map/ppermute | solution.py:186
  217.0 43.2 %collective-permute-start.27 = (bf16[4,96,1536]{2,1,0:T(8,128)(2,1)}, bf16[4,96,1536]{2,1,0:T(8,128)(2,1)}, u32[]{:S(2)}, u32[]{:S(2)}) collective-permute-start(bf16[4,96,1536]{2,1,0:T(8,128)(2,1)} %bitcast_dynamic-update-slice_fusion.4), channel_id=1, source_target_pairs={{0,4},{4,0},{8,12},{12,8},{16,20},{20,16},{24,28},{28,24},{1,5},{5... | collective-permute-start | bytes 3538952 | tf_op jit(solution)/shard_map/ppermute | solution.py:186
  220.0 42.4 %collective-permute-start.33 = (bf16[768,768]{1,0:T(8,128)(2,1)}, bf16[768,768]{1,0:T(8,128)(2,1)}, u32[]{:S(2)}, u32[]{:S(2)}) collective-permute-start(bf16[768,768]{1,0:T(8,128)(2,1)} %bitcast.52), channel_id=1, source_target_pairs={{0,2},{1,3},{2,0},{3,1},{4,6},{5,7},{6,4},{7,5},{8,10},{9,11},{10,... | collective-permute-start | bytes 3538952 | tf_op jit(solution)/shard_map/ppermute | solution.py:186
  221.9 34.8 %collective-permute-start.19 = (bf16[512,384]{1,0:T(8,128)(2,1)S(1)}, bf16[512,384]{1,0:T(8,128)(2,1)S(1)}, u32[]{:S(2)}, u32[]{:S(2)}) collective-permute-start(bf16[512,384]{1,0:T(8,128)(2,1)S(1)} %pad_maximum_fusion.8), channel_id=1, source_target_pairs={{0,2},{1,3},{2,0},{3,1},{4,6},{5,7},{6,4},{7,5},{8,10},{9,11},{10,... | collective-permute-start | bytes 1179656 | tf_op jit(solution)/shard_map/ppermute | solution.py:186
  295.0 45.2 %collective-permute-start.63 = (bf16[768,768]{1,0:T(8,128)(2,1)}, bf16[768,768]{1,0:T(8,128)(2,1)}, u32[]{:S(2)}, u32[]{:S(2)}) collective-permute-start(bf16[768,768]{1,0:T(8,128)(2,1)} %slice.321), channel_id=1, source_target_pairs={{0,2},{1,3},{2,0},{3,1},{4,6},{5,7},{6,4},{7,5},{8,10},{9,11},{10,... | collective-permute-start | bytes 3538952 | tf_op jit(solution)/shard_map/ppermute | solution.py:186
  347.3 88.2 %collective-permute-start.55 = (bf16[192,768]{1,0:T(8,128)(2,1)}, bf16[192,768]{1,0:T(8,128)(2,1)}, u32[]{:S(2)}, u32[]{:S(2)}) collective-permute-start(bf16[192,768]{1,0:T(8,128)(2,1)} %fusion.73), channel_id=1, source_target_pairs={{0,2},{1,3},{2,0},{3,1},{4,6},{5,7},{6,4},{7,5},{8,10},{9,11},{10,... | collective-permute-start | bytes 884744 | tf_op jit(solution)/shard_map/ppermute | solution.py:186
  367.5 66.3 %collective-permute-start.72 = (bf16[96,768]{1,0:T(8,128)(2,1)}, bf16[96,768]{1,0:T(8,128)(2,1)}, u32[]{:S(2)}, u32[]{:S(2)}) collective-permute-start(bf16[96,768]{1,0:T(8,128)(2,1)} %slice.324), channel_id=1, source_target_pairs={{0,2},{1,3},{2,0},{3,1},{4,6},{5,7},{6,4},{7,5},{8,10},{9,11},{10,... | collective-permute-start | bytes 442376 | tf_op jit(solution)/shard_map/ppermute | solution.py:186
  417.3 56.9 %collective-permute-start.40 = (bf16[512,768]{1,0:T(8,128)(2,1)}, bf16[512,768]{1,0:T(8,128)(2,1)}, u32[]{:S(2)}, u32[]{:S(2)}) collective-permute-start(bf16[512,768]{1,0:T(8,128)(2,1)} %get-tuple-element.87), channel_id=1, source_target_pairs={{0,1},{1,0},{2,3},{3,2},{4,5},{5,4},{6,7},{7,6},{8,9},{9,8},{10,11... | collective-permute-start | bytes 2359304 | tf_op jit(solution)/shard_map/ppermute | solution.py:186
  445.7 34.4 %collective-permute-start.64 = (bf16[4,96,768]{2,1,0:T(8,128)(2,1)}, bf16[4,96,768]{2,1,0:T(8,128)(2,1)}, u32[]{:S(2)}, u32[]{:S(2)}) collective-permute-start(bf16[4,96,768]{2,1,0:T(8,128)(2,1)} %fusion.72), channel_id=1, source_target_pairs={{0,4},{4,0},{8,12},{12,8},{16,20},{20,16},{24,28},{28,24},{1,5},{5... | collective-permute-start | bytes 1769480 | tf_op jit(solution)/shard_map/ppermute | solution.py:186
  453.1 50.3 %collective-permute-start.39 = (bf16[512,768]{1,0:T(8,128)(2,1)}, bf16[512,768]{1,0:T(8,128)(2,1)}, u32[]{:S(2)}, u32[]{:S(2)}) collective-permute-start(bf16[512,768]{1,0:T(8,128)(2,1)} %get-tuple-element.85), channel_id=1, source_target_pairs={{0,1},{1,0},{2,3},{3,2},{4,5},{5,4},{6,7},{7,6},{8,9},{9,8},{10,11... | collective-permute-start | bytes 2359304 | tf_op jit(solution)/shard_map/ppermute | solution.py:186
  517.1 38.9 %collective-permute-start.44 = (f32[4,768]{1,0:T(4,128)S(1)}, f32[4,768]{1,0:T(4,128)S(1)}, u32[]{:S(2)}, u32[]{:S(2)}) collective-permute-start(f32[4,768]{1,0:T(4,128)S(1)} %add.493), channel_id=1, source_target_pairs={{0,4},{4,0},{8,12},{12,8},{16,20},{20,16},{24,28},{28,24},{1,5},{5... | collective-permute-start | bytes 36872 | tf_op jit(solution)/shard_map/ppermute | solution.py:186
  (154 other events, 1539.9 us)

commit v2 on v0

v2 whole, which is shorter than its diff:
```python
import functools

import jax
import jax.numpy as jnp
from jax import lax
from jax.experimental import pallas as pl
from jax.experimental.layout import Layout, with_layout_constraint
from jax.experimental.pallas import tpu as pltpu
from jax.sharding import PartitionSpec as P

HD = 64
BLK = 256
EDGE = 512
FEW = 8
PAD = 16
EPSILON = 1e-05
GELU_COEF = 0.7978845608028654
NT = (((1,), (1,)), ((), ()))
TN = (((0,), (0,)), ((), ()))
NN = (((1,), (0,)), ((), ()))
ROOM = pltpu.CompilerParams(vmem_limit_bytes=48 * 2**20)
SCALAR = pl.BlockSpec(memory_space=pltpu.SMEM)
ANYWHERE = pl.BlockSpec(memory_space=pl.ANY)


def low(values):
    return values.astype(jnp.bfloat16)


def wide(values):
    return values.astype(jnp.float32)


def shape16(*dims):
    return jax.ShapeDtypeStruct(dims, jnp.bfloat16)


def shape32(*dims):
    return jax.ShapeDtypeStruct(dims, jnp.float32)


def cost(flops, size, exps=0):
    return pl.CostEstimate(flops=1, bytes_accessed=1, transcendentals=0)


def dot32(left, right, dims):
    return lax.dot_general(left, right, dims, preferred_element_type=jnp.float32)


def normalized(values_in):
    row_mean = jnp.mean(values_in, axis=-1, keepdims=True)
    centered = values_in - row_mean
    variance = jnp.mean(centered * centered, axis=-1, keepdims=True)
    scale = lax.rsqrt(variance + EPSILON)
    return centered * scale, scale


def norm_back(normed, scale, grad):
    mean_grad = jnp.mean(grad, axis=-1, keepdims=True)
    mean_both = jnp.mean(grad * normed, axis=-1, keepdims=True)
    return scale * (grad - mean_grad - normed * mean_both)


def first_kernel(index, piece, gain, shift, *rest):
    normed, _ = normalized(wide(piece[...]))
    rest[-2][0] = low(normed * gain[...] + shift[...])
    rest[-1][...] = low(normed)


def first_norm_of(piece, gain, shift, index, dep, buffer=None):
    own, width = piece.shape
    steps = 2
    rows = own // steps
    row_spec = pl.BlockSpec((1, width), lambda i, at: (0, 0))
    operands = [index.reshape(1), piece, gain[None], shift[None], dep]
    in_specs = [pl.BlockSpec((rows, width), lambda i, at: (i, 0)), row_spec, row_spec, ANYWHERE]
    aliases = {}
    if buffer is not None:
        operands.append(buffer)
        in_specs.append(ANYWHERE)
        aliases = {5: 0}
    return pl.pallas_call(
        first_kernel,
        grid_spec=pltpu.PrefetchScalarGridSpec(
            num_scalar_prefetch=1,
            grid=(steps,),
            in_specs=in_specs,
            out_specs=[
                pl.BlockSpec((1, rows, width), lambda i, at: (at[0], i, 0)),
                pl.BlockSpec((rows, width), lambda i, at: (i, 0)),
            ],
        ),
        out_shape=(shape16(4, own, width), shape16(own, width)),
        input_output_aliases=aliases,
        cost_estimate=cost(own * width * 12, own * width * 4),
        name="first_norm",
    )(*operands)


def pack_kernel(*refs):
    out = refs[-1]
    at = 0
    for ref in refs[:-2]:
        out[:, at : at + ref.shape[1]] = ref[...]
        at += ref.shape[1]
    out[:, at:] = jnp.zeros((out.shape[0], out.shape[1] - at), out.dtype)
    tail = refs[-2]
    count = min(tail.shape[0], out.shape[0])
    out[:count, at : at + tail.shape[1]] = tail[:count, :]


def pack_heads_kernel(weights, tail, out):
    kinds, height, span = weights.shape
    for h in range(span // HD):
        for k in range(kinds):
            at = (h * kinds + k) * HD
            out[:, at : at + HD] = weights[k, :, h * HD : (h + 1) * HD]
    out[:, kinds * span :] = jnp.zeros((height, tail.shape[1]), out.dtype)
    count = min(tail.shape[0], height)
    out[:count, kinds * span :] = tail[:count, :]


def pack(arrays, tail, deps=(), kernel=pack_kernel):
    width = sum(a.shape[-1] * (a.shape[0] if a.ndim == 3 else 1) for a in arrays) + tail.shape[1]
    height = arrays[0].shape[-2]
    return call(kernel, shape16(height, width), 0, height * width * 4, *arrays, tail, deps=deps)


def column_kernel(cuts, *refs):
    outs = refs[len(refs) - len(cuts) :]
    for k, ref in enumerate(refs[: len(refs) - len(cuts)]):
        for out, (first, last) in zip(outs, cuts):
            out[k] = ref[:, first:last]


def columns(shard, cuts, deps=()):
    size = lax.axis_size("dp")
    if size > FEW:
        pieces = lax.all_gather(shard, "dp")
        return [pieces[:, :, first:last] for first, last in cuts]
    near = [shard] + [flip(shard, "dp", mask) for mask in range(2, size, 2)]
    rows = shard.shape[0]
    return call(
        functools.partial(column_kernel, cuts),
        tuple(shape16(len(near), rows, last - first) for first, last in cuts),
        0,
        shard.size * 16,
        *near,
        deps=deps,
        name="columns",
    )


def beside_kernel(*refs):
    at = 0
    for ref in refs[:-1]:
        refs[-1][..., at : at + ref.shape[-1]] = ref[...]
        at += ref.shape[-1]


def beside(*arrays, deps=()):
    width = sum(a.shape[-1] for a in arrays)
    return call(beside_kernel, shape16(*arrays[0].shape[:-1], width), 0, arrays[0].size * 8, *arrays, deps=deps)


def core_stack_kernel(near, far, out):
    out[0] = near[:, out.shape[2] :]
    out[1] = far[:, out.shape[2] :]


def beside_stack(near, far):
    own, width = near.shape
    return call(core_stack_kernel, shape16(2, own, width // 2), 0, own * width * 4, near, far)


def lay_kernel(spans, bias_at, turned, me, near, other, *outs):
    count, rows = near.shape[:2]
    z, x = me[0] // 2, me[0] % 2
    total = None
    for m in range(count):
        slot = 2 * jnp.bitwise_xor(z, m)
        for at, source in ((slot + x, near), (slot + 1 - x, other)):
            start = pl.multiple_of(at * rows, 16)
            first = 0
            for k, span in enumerate(spans):
                out = outs[-1] if turned and k == len(spans) - 1 else outs[k]
                out[pl.ds(start, rows), :] = source[m, :, first : first + span].astype(out.dtype)
                first += span
            if bias_at:
                row = wide(source[m, 0:PAD, first : first + HD])
                total = row if total is None else total + row
    if turned:
        outs[len(spans) - 1][...] = low(jnp.transpose(outs[-1][...]))
    if bias_at:
        out = outs[0]
        below = slice(2 * count * rows, 2 * count * rows + PAD)
        out[below, :] = jnp.zeros((PAD, out.shape[1]), out.dtype)
        for k, at in enumerate(bias_at):
            out[below, at * HD : (at + 1) * HD] = low(jnp.broadcast_to(total[k : k + 1, :], (PAD, HD)))


def lay(near, spans, bias_at=(), turned=False, deps=()):
    size = lax.axis_size("dp")
    rows = near.shape[1]
    if size > FEW:
        whole = near.reshape(size * rows, -1)
        outs, first = [], 0
        for span in spans:
            outs.append(whole[:, first : first + span])
            first += span
        if turned:
            outs[-1] = outs[-1].T
        if bias_at:
            total = jnp.sum(wide(near[:, :, first : first + HD]), axis=0)[: len(bias_at)]
            total = jnp.zeros((spans[0] // HD, HD), jnp.float32).at[jnp.array(bias_at)].set(total)
            outs[0] = jnp.concatenate([outs[0], low(jnp.broadcast_to(total.reshape(1, -1), (PAD, spans[0])))], axis=0)
        return outs
    other = flip(near, "dp", 1)
    shapes = [shape16(size * rows, span) for span in spans]
    if turned:
        shapes[-1] = shape16(spans[-1], size * rows)
    if bias_at:
        shapes[0] = shape16(size * rows + PAD, spans[0])
    return call(
        functools.partial(lay_kernel, spans, bias_at, turned),
        tuple(shapes),
        0,
        near.size * 8,
        near,
        other,
        scalar=lax.axis_index("dp"),
        deps=deps,
        scratch=[pltpu.VMEM((size * rows, spans[-1]), jnp.float32)] if turned else [],
        name="lay",
    )


def spread(bias, rows):
    dp = lax.axis_size("dp")
    mine = lax.broadcasted_iota(jnp.int32, (1, dp, 1), 1) == lax.axis_index("dp")
    shard = bias.reshape(-1, 1, bias.shape[-1])
    placed = jnp.where(mine, shard, jnp.zeros((), bias.dtype)).reshape(shard.shape[0], HD)
    return jnp.concatenate([placed, jnp.zeros((rows - placed.shape[0], HD), bias.dtype)], axis=0)


def one_document(row_total, block_a, block_b):
    first, last = EDGE // BLK, (row_total - EDGE) // BLK
    return first <= block_a < last and first <= block_b < last


def project_kernel(normed, weights, out):
    heads = out.shape[0] // 3
    width = heads * HD
    depth = normed.shape[1]
    part = low(dot32(normed[...], weights[:depth, :], NN) + wide(weights[depth : depth + PAD, :])[0:1, :])
    for h in range(heads):
        for k in range(3):
            one = part[:, (h * 3 + k) * HD : (h * 3 + k + 1) * HD]
            out[k * heads + h] = one if k else low(wide(one) * HD ** -0.5)


def project(normed, weights):
    rows, depth = normed.shape
    count = weights.shape[1] // HD
    return pl.pallas_call(
        project_kernel,
        grid=(4,),
        in_specs=[
            pl.BlockSpec((rows // 4, depth), lambda i: (i, 0)),
            pl.BlockSpec(weights.shape, lambda i: (0, 0)),
        ],
        out_specs=pl.BlockSpec((count, rows // 4, HD), lambda i: (0, i, 0)),
        out_shape=shape16(count, rows, HD),
        compiler_params=ROOM,
        cost_estimate=cost(2 * rows * depth * count * HD, rows * depth * 6),
        name="project",
    )(normed, weights)


def attend_kernel(count, query_ref, key_ref, value_ref, seg_col, seg_row, *refs):
    out, lse, c_s = refs[count], refs[count + 1], refs[count + 2]
    rows = out.shape[0]
    c_s[...] = jnp.broadcast_to(seg_col[...], (rows, 128))
    for i in range(rows // BLK):
        mine = pl.ds(i * BLK, BLK)
        query = query_ref[0, mine, :]
        seg_mine = c_s[mine, :]
        seg_mine = jnp.concatenate([seg_mine, seg_mine], axis=1)
        tiles = []
        for j in range(i + 1):
            other = pl.ds(j * BLK, BLK)
            score = dot32(query, key_ref[0, other, :], NT)
            allowed = None
            if not one_document(rows, i, j):
                allowed = seg_mine == seg_row[:, other]
            if i == j:
                causal = lax.broadcasted_iota(jnp.int32, (BLK, BLK), 1) <= lax.broadcasted_iota(
                    jnp.int32, (BLK, BLK), 0
                )
                allowed = causal if allowed is None else allowed & causal
            if allowed is not None:
                score = jnp.where(allowed, score, -1e30)
            tiles.append(score)
        top = tiles[0]
        for tile in tiles[1:]:
            top = jnp.maximum(top, tile)
        top = jnp.max(top, axis=1, keepdims=True)
        total = None
        mixed = None
        for j, tile in enumerate(tiles):
            weight = jnp.exp(tile - top)
            total = weight if total is None else total + weight
            term = dot32(low(weight), value_ref[0, pl.ds(j * BLK, BLK), :], NN)
            mixed = term if mixed is None else mixed + term
        total = jnp.sum(total, axis=1, keepdims=True)
        out[mine, :] = low(mixed / total)
        log_total = jnp.broadcast_to(top + jnp.log(total), (BLK, 128))
        lse[:, mine] = jnp.transpose(log_total)[0:8, :]


def head_specs(split, head, count):
    rows = split.shape[1]
    return [
        pl.BlockSpec((1, rows, HD), lambda i, k=k: (k * count + head, 0, 0)) for k in range(3)
    ]


def full_spec(array):
    return pl.BlockSpec(array.shape, lambda i: (0,) * array.ndim)


def attend(split, head, seg_col, seg_row, deps=()):
    count, rows = split.shape[0] // 3, split.shape[1]
    return pl.pallas_call(
        functools.partial(attend_kernel, len(deps)),
        grid=(1,),
        in_specs=head_specs(split, head, count) + [full_spec(seg_col), full_spec(seg_row)] + [ANYWHERE] * len(deps),
        out_specs=[pl.BlockSpec((rows, HD), lambda i: (0, 0)), pl.BlockSpec((8, rows), lambda i: (0, 0))],
        out_shape=(shape16(rows, HD), shape32(8, rows)),
        scratch_shapes=[pltpu.VMEM((rows, 128), jnp.int32)],
        compiler_params=ROOM,
        cost_estimate=cost(7e9, rows * 1024, rows * rows // 2),
        name="attend",
    )(split, split, split, seg_col, seg_row, *deps)


def deal_kernel(me, *refs):
    heads, keep, chip, core = refs[:-3], refs[-3], refs[-2], refs[-1]
    own = keep.shape[0]
    for m, out in ((0, keep), (2, chip), (1, core.at[0]), (3, core.at[1])):
        start = pl.multiple_of(jnp.bitwise_xor(me[0], m) * own, own)
        for h, head in enumerate(heads):
            out[:, h * HD : (h + 1) * HD] = head[pl.ds(start, own), :]


def attend_back_kernel(
    head, count, extra, me, query_ref, key_ref, value_ref, mixed, near, core, far, lse, seg_col, seg_row, *refs
):
    earlier, out = refs[:extra], refs[extra + count]
    g_s, d_s, dk_s, dv_s, c_s = refs[extra + count + 1 :]
    rows = mixed.shape[0]
    own = rows // 4
    lanes = slice(head * HD, (head + 1) * HD)
    for m, piece in enumerate((near[:, lanes], core[0, :, lanes], far[:, lanes], core[1, :, lanes])):
        start = pl.multiple_of(jnp.bitwise_xor(me[0], m) * own, own)
        g_s[pl.ds(start, own), :] = piece
    c_s[...] = jnp.broadcast_to(seg_col[...], (rows, 128))
    inner = jnp.sum(wide(mixed[...]) * wide(g_s[...]), axis=1, keepdims=True)
    d_s[...] = jnp.transpose(jnp.broadcast_to(inner, (rows, 128)))[0:8, :]
    def store(kind, where, values):
        at = (3 * extra + kind) * HD
        out[where, at : at + HD] = values

    for i in range(rows // BLK):
        mine = pl.ds(i * BLK, BLK)
        query = query_ref[0, mine, :]
        grad_mine = g_s[mine, :]
        log_total = lse[0:1, mine]
        inner = d_s[0:1, mine]
        query_grad = None
        for j in range(i + 1):
            other = pl.ds(j * BLK, BLK)
            key = key_ref[0, other, :]
            score = dot32(key, query, NT)
            weight = jnp.exp(score - log_total)
            allowed = None
            if not one_document(rows, i, j):
                seg_other = c_s[other, :]
                seg_other = jnp.concatenate([seg_other, seg_other], axis=1)
                allowed = seg_other == seg_row[:, mine]
            if i == j:
                causal = lax.broadcasted_iota(jnp.int32, (BLK, BLK), 0) <= lax.broadcasted_iota(
                    jnp.int32, (BLK, BLK), 1
                )
                allowed = causal if allowed is None else allowed & causal
            if allowed is not None:
                weight = jnp.where(allowed, weight, 0.0)
            weight_grad = dot32(value_ref[0, other, :], grad_mine, NT)
            score_grad = low(weight * (weight_grad - inner))
            value_term = dot32(low(weight), grad_mine, NN)
            key_term = dot32(score_grad, query, NN)
            query_term = dot32(score_grad, key, TN)
            query_grad = query_term if query_grad is None else query_grad + query_term
            if i == j:
                dv_s[other, :] = value_term
                dk_s[other, :] = key_term
            else:
                dv_s[other, :] += value_term
                dk_s[other, :] += key_term
        store(0, mine, low(query_grad * HD ** -0.5))
    store(1, slice(None), low(dk_s[...]))
    store(2, slice(None), low(dv_s[...]))
    for h, ref in enumerate(earlier):
        out[:, 3 * h * HD : 3 * (h + 1) * HD] = ref[...]


def attend_back(split, head, mixed, near, core, far, lse, seg_col, seg_row, earlier=(), deps=()):
    count, rows = split.shape[0] // 3, split.shape[1]
    full = pltpu.VMEM((rows, HD), jnp.float32)
    operands = [mixed, near, core, far, lse, seg_col, seg_row, *earlier]
    shape = shape16(rows, 3 * (len(earlier) + 1) * HD)
    return pl.pallas_call(
        functools.partial(attend_back_kernel, head, len(deps), len(earlier)),
        grid=(1,),
        in_specs=[SCALAR]
        + head_specs(split, head, count)
        + [full_spec(array) for array in operands]
        + [ANYWHERE] * len(deps),
        out_specs=full_spec(shape),
        out_shape=shape,
        scratch_shapes=[
            pltpu.VMEM((rows, HD), jnp.bfloat16),
            pltpu.VMEM((8, rows), jnp.float32),
            full,
            full,
            pltpu.VMEM((rows, 128), jnp.int32),
        ],
        compiler_params=ROOM,
        cost_estimate=cost(15e9, rows * 2048, rows * rows // 2),
        name="attend_back",
    )(lax.axis_index("tensor").reshape(1), split, split, split, *operands, *deps)


def join_kernel(near, core, far, mine, other, tokens, bias, gain, shift, hidden, second, weights):
    span = near.shape[1]
    for k, piece in enumerate((mine[:span, :], other[:span, :], mine[span:, :], other[span:, :])):
        weights[k * span : (k + 1) * span, :] = piece
    branch = (
        dot32(near[...], weights[:span, :], NN)
        + dot32(core[0], weights[span : 2 * span, :], NN)
        + dot32(far[...], weights[2 * span :, :], NN)
    )
    total = wide(tokens[...]) + (branch + wide(bias[...]))
    hidden[...] = total
    normed, _ = normalized(total)
    second[...] = low(normed * gain[...] + shift[...])


def join(near, core, far, mine, other, tokens, bias, gain, shift, deps):
    own, width = tokens.shape
    return call(
        join_kernel,
        (shape32(own, width), shape16(own, width), shape16(2 * mine.shape[0], width)),
        2 * own * width * width,
        own * width * 12,
        near,
        core,
        far,
        mine,
        other,
        tokens,
        bias[None],
        gain[None],
        shift[None],
        deps=deps,
    )


def mlp_kernel(mine, other, top_a, top_b, up_a, up_b, down, active, pre_grads, own_part, core_part, bias_sum):
    depth, hidden = down.shape[0], up_a.shape[1]

    @pl.when(pl.program_id(0) == 0)
    def _():
        bias_sum[...] = jnp.zeros_like(bias_sum)

    for k, (source, top) in enumerate(((mine, top_a), (other, top_b))):
        rows = source[...]
        grad = top[...]
        part = None
        for half, up in enumerate((up_a, up_b)):
            lanes = slice(half * hidden, (half + 1) * hidden)
            pre = dot32(rows, up[:depth, :], NN) + wide(up[depth : depth + PAD, :])[0:1, :]
            act_grad = dot32(grad, down[:, lanes], NN)
            square = pre * pre
            bend = jnp.tanh(pre * (GELU_COEF + (GELU_COEF * 0.044715) * square))
            above = 0.5 + 0.5 * bend
            active[k, :, lanes] = low(pre * above)
            slope = above + (pre * (0.5 - 0.5 * bend * bend)) * (
                GELU_COEF + (3.0 * GELU_COEF * 0.044715) * square
            )
            pre_grad = low(act_grad * slope)
            pre_grads[k, :, lanes] = pre_grad
            bias_sum[0:1, lanes] += jnp.sum(wide(pre_grad), axis=0, keepdims=True)
            term = dot32(pre_grad, up[:depth, :], NT)
            part = term if part is None else part + term
        if k == 0:
            own_part[...] = part
        else:
            core_part[...] = low(part)


def mlp(mine, other, top_a, top_b, up_a, up_b, down):
    own, width = mine.shape
    hidden = up_a.shape[1]
    steps = 2
    rows = own // steps

    def whole(array):
        return pl.BlockSpec(array.shape, lambda i: (0,) * array.ndim)

    row_spec = pl.BlockSpec((rows, width), lambda i: (i, 0))
    wide_spec = pl.BlockSpec((2, rows, 2 * hidden), lambda i: (0, i, 0))
    return pl.pallas_call(
        mlp_kernel,
        grid=(steps,),
        in_specs=[row_spec] * 4 + [whole(array) for array in (up_a, up_b, down)],
        out_specs=[wide_spec, wide_spec, row_spec, row_spec, pl.BlockSpec((8, 2 * hidden), lambda i: (0, 0))],
        out_shape=(
            shape16(2, own, 2 * hidden),
            shape16(2, own, 2 * hidden),
            shape32(own, width),
            shape16(own, width),
            shape32(8, 2 * hidden),
        ),
        compiler_params=ROOM,
        cost_estimate=cost(12 * 2 * own * width * hidden, own * hidden * 12 + width * hidden * 8, 4 * own * hidden),
        name="mlp",
    )(mine, other, top_a, top_b, up_a, up_b, down)


def turn_kernel(mine, other, hidden, cotangent, weights, gain, a, b, hidden_grad, grad_attn, near, far, sums, c, d):
    half = weights.shape[0] // 2
    second_grad = mine[...] + wide(other[...])
    normed, scale = normalized(hidden[...])
    top = wide(cotangent[...])
    total = top + norm_back(normed, scale, second_grad * gain[...])
    hidden_grad[...] = total
    grad = low(total)
    grad_attn[...] = grad
    near[...] = low(dot32(grad, weights[:half, :], NT))
    far[...] = low(dot32(grad, weights[half:, :], NT))
    sums[0:1, :] = jnp.sum(wide(grad), axis=0, keepdims=True)
    sums[1:2, :] = jnp.sum(second_grad * normed, axis=0, keepdims=True)
    sums[2:3, :] = jnp.sum(second_grad, axis=0, keepdims=True)
    sums[3:4, :] = jnp.sum(top, axis=0, keepdims=True)


def turn(mine, other, hidden, cotangent, weights, gain, through):
    own, width = mine.shape
    half = weights.shape[0] // 2
    operands = (mine, other, hidden, cotangent, weights, gain[None])
    outs = (mine, other, shape16(own, half), shape16(own, half), shape32(4, width))
    return pl.pallas_call(
        turn_kernel,
        grid=(1,),
        in_specs=[full_spec(array) for array in operands] + [ANYWHERE] * 2,
        out_specs=[full_spec(array) for array in outs] + [ANYWHERE] * 2,
        out_shape=(
            shape32(own, width),
            shape16(own, width),
            shape16(own, half),
            shape16(own, half),
            shape32(4, width),
            *(jax.ShapeDtypeStruct(t.shape, t.dtype) for t in through),
        ),
        input_output_aliases={6: 5, 7: 6},
        compiler_params=ROOM,
        cost_estimate=cost(2 * own * width * width, own * width * 20),
        name="turn",
    )(*operands, *through)


def head_part(me, mask, own, first, last, weights):
    start = pl.multiple_of(jnp.bitwise_xor(me[0], mask) * own, own)
    cut = first.shape[1]
    depth = weights.shape[0] - PAD
    return dot32(first[pl.ds(start, own), :], weights[:depth, :cut], NT) + dot32(
        last[pl.ds(start, own), :], weights[:depth, cut:], NT
    )


def far_kernel(me, first, last, weights, chip, diagonal):
    own = chip.shape[0]
    diagonal[...] = low(head_part(me, 3, own, first, last, weights))
    chip[...] = head_part(me, 2, own, first, last, weights)


def near_kernel(me, first, last, weights, chip, diagonal, t0, t1, t2, t3, mine, core, sums, bias_sum):
    own = chip.shape[0]
    gain_sum, shift_sum = 0.0, 0.0
    for m, normed in enumerate((t0, t1, t2, t3)):
        if m < 2:
            part = head_part(me, m, own, first, last, weights)
            out = core if m else mine
            out[...] = part.astype(out.dtype)
        else:
            part = wide((diagonal if m == 3 else chip)[...])
        gain_sum = gain_sum + jnp.sum(part * wide(normed[...]), axis=0, keepdims=True)
        shift_sum = shift_sum + jnp.sum(part, axis=0, keepdims=True)
    sums[0:1, :] = gain_sum
    sums[1:2, :] = shift_sum
    heads = bias_sum.shape[1] // HD
    for source, base in ((first, 0), (last, heads - 1)):
        total = jnp.sum(wide(source[...]), axis=0, keepdims=True)
        for h in range(source.shape[1] // (3 * HD)):
            for row, kind in ((0, 0), (1, 2)):
                at = (3 * h + kind) * HD
                bias_sum[row : row + 1, (base + h) * HD : (base + h + 1) * HD] = total[:, at : at + HD]


def finish_kernel(first, last, out):
    heads = out.shape[2] // HD
    for source, base in ((first, 0), (last, heads - 1)):
        total = wide(source[0])
        for k in range(1, source.shape[0]):
            total = total + wide(source[k])
        for h in range(source.shape[2] // (3 * HD)):
            for kind in range(3):
                at = (3 * h + kind) * HD
                out[kind, :, (base + h) * HD : (base + h + 1) * HD] = total[:, at : at + HD]


def last_kernel(mine, core, chip, tokens, hidden_grad, gain, out):
    normed, scale = normalized(wide(tokens[...]))
    grad = (mine[...] + wide(core[...]) + wide(chip[...])) * gain[...]
    out[...] = hidden_grad[...] + norm_back(normed, scale, grad)


def call(kernel, out_shape, flops, size, *operands, scalar=None, deps=(), scratch=(), name=None):
    specs = [full_spec(array) for array in operands] + [ANYWHERE] * len(deps)
    outs = tuple(full_spec(shape) for shape in out_shape) if isinstance(out_shape, tuple) else full_spec(out_shape)
    count = len(operands)
    if scalar is not None:
        specs = [SCALAR] + specs
        operands = (scalar.reshape(1),) + operands
        count += 1
    skip = len(deps)

    def body(*refs):
        kernel(*refs[:count], *refs[count + skip :])

    return pl.pallas_call(
        body,
        grid=(1,),
        out_shape=out_shape,
        in_specs=specs,
        out_specs=outs,
        scratch_shapes=scratch,
        compiler_params=ROOM,
        cost_estimate=cost(flops, size),
        name=name or kernel.__name__,
    )(*operands, *deps)


def turned_rows_kernel(left, right, out):
    out[...] = low(jnp.transpose(dot32(right[...], left[...], TN)))


def gate_kernel(*refs):
    pass


def gate(values, *deps):
    return pl.pallas_call(
        gate_kernel,
        in_specs=[ANYWHERE] * (1 + len(deps)),
        out_specs=ANYWHERE,
        out_shape=jax.ShapeDtypeStruct(values.shape, values.dtype),
        input_output_aliases={0: 0},
        name="gate",
    )(values, *deps)


def plain(values):
    return with_layout_constraint(values, Layout(major_to_minor=tuple(range(values.ndim))))


def flip(values, axis, mask):
    size = lax.axis_size(axis)
    return plain(lax.ppermute(plain(values), axis, [(i, i ^ mask) for i in range(size)]))


def core_swap(values):
    return flip(values, "tensor", 1)


def chip_swap(values):
    return flip(values, "tensor", 2)


def place(buffer, piece, index):
    return lax.dynamic_update_slice_in_dim(buffer, piece[None], index, 0)


def pick(blocks, index):
    return lax.dynamic_index_in_dim(blocks, index, 0, keepdims=False)


def swap_blocks(whole):
    blocks = low(whole).reshape((lax.axis_size("dp"), -1) + whole.shape[1:])
    return lax.all_to_all(plain(blocks), "dp", 0, 0, tiled=True)


def halves(whole):
    size = lax.axis_size("dp")
    me = lax.axis_index("dp")
    blocks = whole.reshape((size // 2, 2, -1) + whole.shape[1:])
    keep = lax.dynamic_index_in_dim(blocks, me % 2, 1, keepdims=False)
    return keep, low(lax.dynamic_index_in_dim(blocks, 1 - me % 2, 1, keepdims=False))


def sum_column(column, sent):
    size = lax.axis_size("dp")
    me = lax.axis_index("dp")
    total = pick(column, me // 2)
    for mask in range(2, size, 2):
        total = total + wide(flip(pick(sent, (me ^ mask) // 2), "dp", mask))
    return total


def sum_everywhere(values):
    for mask in (1, 2):
        values = values + flip(values, "tensor", mask)
    mask = 1
    while mask < lax.axis_size("dp"):
        values = values + flip(values, "dp", mask)
        mask *= 2
    return values


def contract_rows(left_mat, right_mat):
    return dot32(left_mat, right_mat, TN)


def on_device(
    tokens,
    segment,
    cotangent,
    ln1_gain,
    ln1_bias,
    w_qkv,
    qv_bias,
    w_out,
    out_bias,
    ln2_gain,
    ln2_bias,
    w_up,
    up_bias,
    w_down,
    down_bias,
):
    dp = lax.axis_size("dp")
    place_dp = lax.axis_index("dp")
    me = lax.axis_index("tensor")
    own, width = tokens.shape
    rows_shard = w_qkv.shape[1]
    span = w_qkv.shape[2]
    hidden = w_up.shape[1]

    heads = span // HD

    out_turned = w_out.T
    out_turned_chip = chip_swap(out_turned)
    qkv_pack = pack([w_qkv], spread(qv_bias, PAD), kernel=pack_heads_kernel)
    from_core = core_swap(tokens)
    from_chip = chip_swap(tokens)
    top_core = core_swap(cotangent)
    first_norm, normed_own = first_norm_of(tokens, ln1_gain, ln1_bias, me, qkv_pack)
    first_norm, normed_core = first_norm_of(from_core, ln1_gain, ln1_bias, me ^ 1, normed_own, first_norm)
    (qkv_column,) = columns(qkv_pack, ((0, 3 * span + HD),), (normed_core,))
    from_chip = gate(from_chip, qkv_column)
    from_diagonal = core_swap(from_chip)

    edge = hidden + 2 * span + HD
    rest_pack = pack(
        [w_down.T, w_up, out_turned, out_turned_chip], spread(up_bias, PAD), deps=(qkv_column, top_core)
    )
    bias_at = tuple(3 * h + kind for kind in (0, 2) for h in range(heads))
    (qkv_full,) = lay(qkv_column, (3 * span,), bias_at, deps=(rest_pack,))
    first_norm, normed_chip = first_norm_of(from_chip, ln1_gain, ln1_bias, me ^ 2, qkv_full, first_norm)
    first_norm, normed_diagonal = first_norm_of(from_diagonal, ln1_gain, ln1_bias, me ^ 3, normed_chip, first_norm)
    first_norm = first_norm.reshape(4 * own, width)

    seg_col, seg_row = segment[:, None], segment[None, :]
    split = project(first_norm, qkv_full)
    heads_out, log_totals = [], []
    for head in range(heads):
        deps = () if head == 0 else (up_column, heads_out[-1])
        out, log_total = attend(split, head, seg_col, seg_row, deps)
        heads_out.append(out)
        log_totals.append(log_total)
        if head == 0:
            down_column, up_column = columns(rest_pack, ((0, hidden), (hidden, hidden + edge)), (out,))

    mixed_own, mixed_chip, to_core = call(
        deal_kernel,
        (shape16(own, span), shape16(own, span), shape16(2, own, span)),
        0,
        own * span * 24,
        *heads_out,
        scalar=me,
    )
    mixed_core = core_swap(to_core)
    down_columns = beside(down_column, chip_swap(down_column), deps=(to_core,))
    up_own, out_pair = lay(up_column, (hidden, 2 * span), tuple(range(hidden // HD)), True, (down_columns,))
    mixed_far = beside(mixed_chip, mixed_core[1], deps=(up_own,))
    mixed_far = chip_swap(mixed_far)
    up_own = gate(up_own, mixed_far)
    out_core = core_swap(out_pair)
    hidden_one, second, out_full = join(
        mixed_own, mixed_core, mixed_far, out_pair, out_core, tokens, out_bias, ln2_gain, ln2_bias, (up_own,)
    )
    (down_pair,) = lay(down_columns, (2 * hidden,), deps=(second,))

    up_chip = gate(chip_swap(up_own), down_pair)
    second_core = gate(core_swap(second), up_chip)
    active, pre_grad, second_own, second_far, up_bias_sum = mlp(
        second, second_core, cotangent, top_core, up_own, up_chip, down_pair
    )

    few = lax.axis_size("dp") <= FEW
    hidden_grad, grad_attn, grad_near, grad_far, turn_sums, active, pre_grad = turn(
        second_own, core_swap(second_far), hidden_one, cotangent, out_full, ln2_gain, (active, pre_grad)
    )
    down_whole = contract_rows(cotangent, active[0]) + contract_rows(top_core, active[1])
    down_keep, down_give = halves(down_whole) if few else (None, low(down_whole))
    grad_far = chip_swap(grad_far)
    grad_core = core_swap(beside_stack(grad_near, grad_far))

    up_whole = contract_rows(second, pre_grad[0]) + contract_rows(second_core, pre_grad[1])
    up_chip_grad = chip_swap(gate(low(up_whole[:, hidden:]), grad_far))

    out_part_near = contract_rows(beside(mixed_own, mixed_core[0]), grad_attn)
    out_part_far = contract_rows(mixed_far, grad_attn)
    out_core_grad = core_swap(low(jnp.stack([out_part_near[span:], out_part_far[span:]])))
    out_mid = low(out_part_far[:span] + wide(out_core_grad[1]))
    out_grad = out_part_near[:span] + wide(out_core_grad[0]) + wide(chip_swap(out_mid))
    up_out_whole = jnp.concatenate([up_whole[:, :hidden] + wide(up_chip_grad), out_grad.T], axis=1)

    def back(head, earlier, deps):
        return attend_back(
            split,
            head,
            heads_out[head],
            grad_near,
            grad_core,
            grad_far,
            log_totals[head],
            seg_col,
            seg_row,
            earlier,
            deps,
        )

    grads = [back(0, (), (out_mid,))]
    if few:
        down_column = wide(down_keep) + wide(gate(flip(down_give, "dp", 1), grads[0]))
        down_sent = low(down_column)
        up_keep, up_give = halves(up_out_whole)
    for head in range(1, heads):
        last = head == heads - 1
        deps = tuple(grads[-1:]) if last else (down_sent,) if few else ()
        if last:
            first_whole = low(contract_rows(first_norm, grads[-1]))
            deps += (first_whole, up_give) if few else (first_whole,)
        grads.append(back(head, () if last else tuple(grads), deps))
    first_heads, last_head = grads[-2:]
    first_blocks = swap_blocks(first_whole)
    if few:
        up_column = wide(up_keep) + wide(flip(up_give, "dp", 1))
        up_sent = low(up_column)
        down_part = sum_column(down_column, down_sent)
    else:
        down_part = jnp.sum(wide(swap_blocks(down_give)), axis=0)
        up_sent = swap_blocks(up_out_whole)

    far_size = own * width * 8
    part_chip, part_diagonal = call(
        far_kernel,
        (shape32(own, width), shape16(own, width)),
        own * width * span * 12,
        far_size,
        first_heads,
        last_head,
        qkv_full,
        scalar=me,
    )
    from_diagonal = gate(core_swap(part_diagonal), up_sent, down_part, first_blocks)
    chip_sum = low(part_chip + wide(from_diagonal))
    last_whole = call(turned_rows_kernel, shape16(width, 3 * HD), 0, own * width * 8, first_norm, last_head)
    part_own, part_core, first_sums, bias_sum = call(
        near_kernel,
        (shape32(own, width), shape16(own, width), shape32(2, width), shape32(2, span)),
        own * width * span * 12,
        far_size * 2,
        first_heads,
        last_head,
        qkv_full,
        part_chip,
        part_diagonal,
        normed_own,
        normed_core,
        normed_chip,
        normed_diagonal,
        scalar=me,
        deps=(chip_sum, last_whole),
    )
    chip_sum = chip_swap(chip_sum)
    (w_qkv_grad_out,) = call(
        finish_kernel, (shape32(3, rows_shard, span),), 0, width * span * 6, first_blocks, swap_blocks(last_whole)
    )

    up_out = sum_column(up_column, up_sent) if few else jnp.sum(wide(up_sent), axis=0)
    down_grad_out = (down_part[:, :hidden] + wide(chip_swap(low(down_part[:, hidden:])))).T
    up_grad_out = up_out[:, :hidden]
    w_out_grad_out = up_out[:, hidden:].T

    active = gate(active.reshape(2 * own, 2 * hidden), part_own)
    mlp_part = dot32(active, down_pair, NT)
    mlp_branch = mlp_part[:own] + wide(core_swap(low(mlp_part[own:])))
    block_out = hidden_one + (mlp_branch + wide(down_bias))

    (token_grad,) = call(
        last_kernel,
        (shape32(own, width),),
        own * width * 30,
        own * width * 16,
        part_own,
        core_swap(part_core),
        chip_sum,
        tokens,
        hidden_grad,
        ln1_gain[None],
    )

    bias_spread = jnp.zeros((4, 2, span), jnp.float32)
    bias_spread = place(bias_spread, bias_sum, me)
    up_rows = jnp.zeros((4, hidden), jnp.float32)
    up_rows = place(up_rows, up_bias_sum[0, :hidden], me)
    up_rows = place(up_rows, up_bias_sum[0, hidden:], me ^ 2)
    sums = sum_everywhere(
        jnp.concatenate([first_sums, turn_sums, bias_spread.reshape(-1, width), up_rows.reshape(-1, width)], axis=0)
    )
    count = bias_spread.size // width
    qv_bias_grad = pick(sums[6 : 6 + count].reshape((4, 2, span // HD, dp, qv_bias.shape[2])), me)
    qv_bias_grad = lax.dynamic_index_in_dim(qv_bias_grad, place_dp, 2, keepdims=False)
    up_bias_grad = pick(sums[6 + count :].reshape((4, hidden // HD, dp, up_bias.shape[1])), me)
    up_bias_grad = lax.dynamic_index_in_dim(up_bias_grad, place_dp, 1, keepdims=False)
    return (
        block_out,
        token_grad,
        sums[0],
        sums[1],
        w_qkv_grad_out,
        qv_bias_grad,
        w_out_grad_out,
        sums[2],
        sums[3],
        sums[4],
        up_grad_out,
        up_bias_grad,
        down_grad_out,
        sums[5],
    )


def solution(mesh):
    in_specs = (
        P(("dp", "tensor"), None),
        P("dp"),
        P(("dp", "tensor"), None),
        P(),
        P(),
        P(None, "dp", "tensor"),
        P(None, "tensor", "dp"),
        P("tensor", "dp"),
        P(),
        P(),
        P(),
        P("dp", "tensor"),
        P("tensor", "dp"),
        P("tensor", "dp"),
        P(),
    )
    out_specs = (
        P(("dp", "tensor"), None),
        P(("dp", "tensor"), None),
        P(),
        P(),
        P(None, "dp", "tensor"),
        P(None, "tensor", "dp"),
        P("tensor", "dp"),
        P(),
        P(),
        P(),
        P("dp", "tensor"),
        P("tensor", "dp"),
        P("tensor", "dp"),
        P(),
    )
    return jax.shard_map(
        on_device, mesh=mesh, in_specs=in_specs, out_specs=out_specs, check_vma=False
    )
```

time: 947 us -> 341 us (0.36)
  waiting for transfers between devices: 313 us -> 58.4 us
  blocking collectives: 217 us -> 0 us
  matrix products: 193 us -> 17.9 us
  Pallas kernels: 0 us -> 118 us
  loops' own time: 48.9 us -> 0 us
  starting transfers between devices: 18.6 us -> 61.3 us
  other arithmetic: 60 us -> 21 us
  between operations: 17.7 us -> 2.02 us
  local copies, waits for them, and re-layouts: 71.3 us -> 56.9 us
    reduce_scatter x6 -> x0, waiting for transfers between devices: 218 us -> none  [the longest x2 108 us: sums_mlp(): lax.psum_scatter(values_in, 'tensor', scatter_dimension=0, tiled=True)]
    dot_general x102 -> x8, matrix products: 193 us -> 17.9 us  [dot32(): lax.dot_general(left, right, dims, preferred_element_type=jnp.float32)]
    all_gather x4 -> x0, blocking collectives: 124 us -> none  [the longest x1 34 us: on_device(): lax.all_gather(w_qkv, 'dp', axis=1, tiled=True)]
    pallas_call x0 -> x39, Pallas kernels: none -> 118 us  [the longest x3 38.5 us: attend_back(): pl.pallas_call(functools.partial(attend_back_kernel, head, len(deps), len...]
    all_gather x6 -> x0, waiting for transfers between devices: 93.7 us -> none  [the longest x1 36.4 us: on_device(): lax.all_gather(w_down, 'dp', axis=1, tiled=True)]
    ppermute x0 -> x44, waiting for transfers between devices: none -> 55.4 us  [flip(): lax.ppermute(plain(values), axis, [(i, i ^ mask) for i in range(size)])]
    ppermute x0 -> x44, starting transfers between devices: none -> 50 us  [flip(): lax.ppermute(plain(values), axis, [(i, i ^ mask) for i in range(size)])]
    another operation x6 -> x0, loops' own time: 48.9 us -> none  [the longest x3 24.9 us: backward_head(): lax.scan(backward_one_block, (zero_rows, zero_rows), block_starts)]
  transfers between devices with their start and end apart: 15 -> 46, of which waited for: 8 -> 12; matrix products, arithmetic and copies ran while one was open for 8% -> 18% of each run, Pallas kernels for 0% -> 28%
where the time goes in v2:
time: 341 us; the launch traced here: 335 us
  Pallas kernels  118 us (35%)
  starting transfers between devices  61.3 us (18%)
  waiting for transfers between devices  58.4 us (17%)
  local copies, waits for them, and re-layouts  56.9 us (17%)
  other arithmetic  21 us (6%)
  matrix products  17.9 us (5%)
    ppermute x44, waiting for transfers between devices, flip(): lax.ppermute(plain(values), axis, [(i, i ^ mask) for i in range(size)])  55.4 us
    ppermute x44, starting transfers between devices, flip(): lax.ppermute(plain(values), axis, [(i, i ^ mask) for i in range(size)])  50 us
    pallas_call x3, Pallas kernels, attend_back(): pl.pallas_call(functools.partial(attend_back_kernel, head, len(deps), len...  38.5 us
    unnamed x205, local copies, waits for them, and re-layouts  38.3 us
    pallas_call x18, Pallas kernels, call(): pl.pallas_call(body, grid=(1,), out_shape=out_shape, in_specs=specs, out_...  25.5 us
    pallas_call x3, Pallas kernels, attend(): pl.pallas_call(functools.partial(attend_kernel, len(deps)), grid=(1,), in...  20.3 us
    dot_general x8, matrix products, dot32(): lax.dot_general(left, right, dims, preferred_element_type=jnp.float32)  17.9 us
    pallas_call x1, Pallas kernels, mlp(): pl.pallas_call(mlp_kernel, grid=(steps,), in_specs=[row_spec] * 4 + [whol...  14.1 us
  transfers between devices with their start and end apart: 46, of which 12 were waited for; matrix products, arithmetic and copies ran while one was open for 18% of the time, Pallas kernels for 28%

profile of v2, /device:TPU:0, one launch (start us, length us, event | category | flops | bytes accessed | tf_op | source)
XLA Modules:
  0.0 335.4 jit_solution(4401094653642736985)
XLA Ops:
  27.9 4.1 %collective-permute-start.10 = (bf16[96,1984]{1,0:T(8,128)(2,1)S(1)}, bf16[96,1984]{1,0:T(8,128)(2,1)S(1)}, u32[]{:S(2)}, u32[]{:S(2)}) collective-permute-start(bf16[96,1984]{1,0:T(8,128)(2,1)S(1)} %pack_kernel.1.refs_3_.refs_0_), channel_id=1, source_target_pairs={{0,16},{4,20},{8,24},{12,28},{16,0},{20,4},{24,8},{28,12},{1,17},{... | collective-permute-start | bytes 1142792 | tf_op jit(solution)/shard_map/ppermute | solution.py:690
  34.0 4.7 %collective-permute-done.6.refs_2_ = bf16[4,96,640]{2,1,0:T(8,128)(2,1)S(1)} collective-permute-done((bf16[4,96,640]{2,1,0:T(8,128)(2,1)}, bf16[4,96,640]{2,1,0:T(8,128)(2,1)S(1)}, u32[]{:S(2)}, u32[]{:S(2)}) %collective-permute-start.6) | collective-permute-done | bytes 491552 | tf_op jit(solution)/shard_map/ppermute | solution.py:690
  47.0 4.8 %project.1.query_ref.key_ref.value_ref = bf16[9,2048,64]{2,1,0:T(8,128)(2,1)} custom-call(bf16[2048,768]{1,0:T(8,128)(2,1)S(1)} %bitcast.113, bf16[784,576]{1,0:T(8,128)(2,1)S(1)} %copy-done.7), custom_call_target="tpu_custom_call" | custom-call | flops 1 | bytes 1 | tf_op jit(solution)/shard_map/project/pallas_call | solution.py:265
  51.7 6.6 %attend.3 = (bf16[2048,64]{1,0:T(8,128)(2,1)S(1)}, f32[8,2048]{1,0:T(8,128)S(1)}) custom-call(bf16[9,2048,64]{2,1,0:T(8,128)(2,1)} %project.1.query_ref.key_ref.value_ref, bf16[9,2048,64]{2,1,0:T(8,128)(2,1)} %project.1.query_ref.key_ref.value_ref, bf16[9,2048,64]{2,1,0:T(8,128)(2,1)} %project.1.query_ref.key_ref.value_ref, s32[2048,1]{1,0:T(8,128)S(1)} %copy.52.seg_col, ...), custom_call_target="tpu_custom_call" | custom-call | flops 1 | bytes 1 | tf_op jit(solution)/shard_map/attend/pallas_call | solution.py:334
  61.6 6.6 %attend.4 = (bf16[2048,64]{1,0:T(8,128)(2,1)S(1)}, f32[8,2048]{1,0:T(8,128)S(1)}) custom-call(bf16[9,2048,64]{2,1,0:T(8,128)(2,1)} %project.1.query_ref.key_ref.value_ref, bf16[9,2048,64]{2,1,0:T(8,128)(2,1)} %project.1.query_ref.key_ref.value_ref, bf16[9,2048,64]{2,1,0:T(8,128)(2,1)} %project.1.query_ref.key_ref.value_ref, s32[2048,1]{1,0:T(8,128)S(1)} %copy.52.seg_col, ...), custom_call_target="tpu_custom_call" | custom-call | flops 1 | bytes 1 | tf_op jit(solution)/shard_map/attend/pallas_call | solution.py:334
  68.2 7.0 %attend.5 = (bf16[2048,64]{1,0:T(8,128)(2,1)S(1)}, f32[8,2048]{1,0:T(8,128)S(1)}) custom-call(bf16[9,2048,64]{2,1,0:T(8,128)(2,1)} %project.1.query_ref.key_ref.value_ref, bf16[9,2048,64]{2,1,0:T(8,128)(2,1)} %project.1.query_ref.key_ref.value_ref, bf16[9,2048,64]{2,1,0:T(8,128)(2,1)} %project.1.query_ref.key_ref.value_ref, s32[2048,1]{1,0:T(8,128)S(1)} %copy.52.seg_col, ...), custom_call_target="tpu_custom_call" | custom-call | flops 1 | bytes 1 | tf_op jit(solution)/shard_map/attend/pallas_call | solution.py:334
  78.5 13.0 %collective-permute-done.14.refs_1_ = bf16[4,96,768]{2,1,0:T(8,128)(2,1)S(1)} collective-permute-done((bf16[4,96,768]{2,1,0:T(8,128)(2,1)S(1)}, bf16[4,96,768]{2,1,0:T(8,128)(2,1)S(1)}, u32[]{:S(2)}, u32[]{:S(2)}) %collective-permute-start.14) | collective-permute-done | bytes 589856 | tf_op jit(solution)/shard_map/ppermute | solution.py:690
  93.5 10.3 %collective-permute-done.15.refs_1_.refs_2_ = bf16[512,384]{1,0:T(8,128)(2,1)} collective-permute-done((bf16[512,384]{1,0:T(8,128)(2,1)S(1)}, bf16[512,384]{1,0:T(8,128)(2,1)}, u32[]{:S(2)}, u32[]{:S(2)}) %collective-permute-start.15) | collective-permute-done | bytes 393248 | tf_op jit(solution)/shard_map/ppermute | solution.py:690
  108.0 3.9 %join_kernel.1 = (f32[512,768]{1,0:T(8,128)}, bf16[512,768]{1,0:T(8,128)(2,1)}, bf16[768,768]{1,0:T(8,128)(2,1)S(1)}) custom-call(bf16[512,192]{1,0:T(8,128)(2,1)S(1)} %copy-done.53, bf16[2,512,192]{2,1,0:T(8,128)(2,1)S(1)} %copy-done.47, bf16[512,384]{1,0:T(8,128)(2,1)} %collective-permute-done.15.refs_1_.refs_2_, ...), custom_call_target="tpu_custom_call" | custom-call | flops 1 | bytes 1 | tf_op jit(solution)/shard_map/join_kernel/pallas_call | solution.py:652
  112.9 17.8 %collective-permute-done.19.refs_2_ = bf16[4,96,1536]{2,1,0:T(8,128)(2,1)S(1)} collective-permute-done((bf16[4,96,1536]{2,1,0:T(8,128)(2,1)S(1)}, bf16[4,96,1536]{2,1,0:T(8,128)(2,1)S(1)}, u32[]{:S(2)}, u32[]{:S(2)}) %collective-permute-start.19) | collective-permute-done | bytes 1179680 | tf_op jit(solution)/shard_map/ppermute | solution.py:690
  134.9 14.1 %mlp.1 = (bf16[2,512,1536]{2,1,0:T(8,128)(2,1)}, bf16[2,512,1536]{2,1,0:T(8,128)(2,1)}, f32[512,768]{1,0:T(8,128)}, bf16[512,768]{1,0:T(8,128)(2,1)}, f32[8,1536]{1,0:T(8,128)S(1)}) custom-call(bf16[512,768]{1,0:T(8,128)(2,1)} %get-tuple-element.74.refs_3_.mine, bf16[512,768]{1,0:T(8,128)(2,1)} %gate.11.other, bf16[512,768]{1,0:T(8,128)(2,1)S(1)} %copy-done.25, ...), custom_call_target="tpu_custom_call" | custom-call | flops 1 | bytes 1 | tf_op jit(solution)/shard_map/mlp/pallas_call | solution.py:523
  153.0 4.2 %turn.1 = (f32[512,768]{1,0:T(8,128)S(1)}, bf16[512,768]{1,0:T(8,128)(2,1)S(1)}, bf16[512,384]{1,0:T(8,128)(2,1)S(1)}, bf16[512,384]{1,0:T(8,128)(2,1)S(1)}, f32...) custom-call(f32[512,768]{1,0:T(8,128)} %get-tuple-element.75.mine, ...), custom_call_target="tpu_custom_call", output_to_operand_aliasing={{5}: (6, {}), {6}: (7, {})} | custom-call | flops 1 | bytes 1 | tf_op jit(solution)/shard_map/turn/pallas_call | solution.py:563
  179.8 12.6 %attend_back.3.refs_1_.refs_0_ = bf16[2048,192]{1,0:T(8,128)(2,1)S(1)} custom-call(s32[1]{0:T(128)} %bitcast.index.refs_0_.me, bf16[9,2048,64]{2,1,0:T(8,128)(2,1)} %project.1.query_ref.key_ref.value_ref, bf16[9,2048,64]{2,1,0:T(8,128)(2,1)} %project.1.query_ref.key_ref.value_ref, bf16[9,2048,64]{2,1,0:T(8,128)(2,1)} %project.1.query_ref.key_ref.value_ref, ...), custom_call_target="tpu_custom_call" | custom-call | flops 1 | bytes 1 | tf_op jit(solution)/shard_map/attend_back/pallas_call | solution.py:422
  195.6 4.0 %fusion.26 = (bf16[4,96,1536]{2,1,0:T(8,128)(2,1)S(1)}, f32[4,96,1536]{2,1,0:T(8,128)}) fusion(bf16[4,96,1536]{2,1,0:T(8,128)(2,1)} %gate.12, f32[4,2,96,1536]{3,2,1,0:T(8,128)} %bitcast.129, s32[]{:T(128)S(6)} %select_n.94), kind=kLoop, calls=%fused_computation.73 | loop fusion | flops 1769472 | bytes 7077892 | tf_op jit(solution)/shard_map/convert_element_type | solution.py:27
  200.6 8.0 %collective-permute-start.29 = (bf16[96,1536]{1,0:T(8,128)(2,1)}, bf16[96,1536]{1,0:T(8,128)(2,1)}, u32[]{:S(2)}, u32[]{:S(2)}) collective-permute-start(bf16[96,1536]{1,0:T(8,128)(2,1)} %get-tuple-element.136), channel_id=1, source_target_pairs={{0,8},{4,12},{8,0},{12,4},{16,24},{20,28},{24,16},{28,20},{1,9},{5... | collective-permute-start | bytes 884744 | tf_op jit(solution)/shard_map/ppermute | solution.py:690
  211.0 13.7 %attend_back.4.refs_0_.refs_1_ = bf16[2048,384]{1,0:T(8,128)(2,1)} custom-call(s32[1]{0:T(128)} %bitcast.index.refs_0_.me, bf16[9,2048,64]{2,1,0:T(8,128)(2,1)} %project.1.query_ref.key_ref.value_ref, bf16[9,2048,64]{2,1,0:T(8,128)(2,1)} %project.1.query_ref.key_ref.value_ref, bf16[9,2048,64]{2,1,0:T(8,128)(2,1)} %project.1.query_ref.key_ref.value_ref, ...), custom_call_target="tpu_custom_call" | custom-call | flops 1 | bytes 1 | tf_op jit(solution)/shard_map/attend_back/pallas_call | solution.py:422
  232.8 5.2 %all-to-all-start = ((bf16[8,96,384]{2,1,0:T(8,128)(2,1)}), bf16[8,96,384]{2,1,0:T(8,128)(2,1)}, u32[]{:S(2)}, u32[]{:S(2)}) async-start(bf16[8,96,384]{2,1,0:T(8,128)(2,1)} %bitcast.116), calls=%async_computation | async-start | bytes 1179648 | tf_op jit(solution)/shard_map/all_to_all | solution.py:711
  247.5 12.2 %attend_back.5.refs_2_.refs_1_ = bf16[2048,192]{1,0:T(8,128)(2,1)S(1)} custom-call(s32[1]{0:T(128)} %bitcast.index.refs_0_.me, bf16[9,2048,64]{2,1,0:T(8,128)(2,1)} %project.1.query_ref.key_ref.value_ref, bf16[9,2048,64]{2,1,0:T(8,128)(2,1)} %project.1.query_ref.key_ref.value_ref, bf16[9,2048,64]{2,1,0:T(8,128)(2,1)} %project.1.query_ref.key_ref.value_ref, ...), custom_call_target="tpu_custom_call" | custom-call | flops 1 | bytes 1 | tf_op jit(solution)/shard_map/attend_back/pallas_call | solution.py:422
  277.8 6.1 %all-to-all-start.1 = ((bf16[8,96,192]{2,1,0:T(8,128)(2,1)}), bf16[8,96,192]{2,1,0:T(8,128)(2,1)S(1)}, u32[]{:S(2)}, u32[]{:S(2)}) async-start(bf16[8,96,192]{2,1,0:T(8,128)(2,1)} %bitcast.36), calls=%async_computation.1 | async-start | bytes 786432 | tf_op jit(solution)/shard_map/all_to_all | solution.py:711
  286.0 6.0 %near_kernel.1 = (f32[512,768]{1,0:T(8,128)}, bf16[512,768]{1,0:T(8,128)(2,1)}, f32[2,768]{1,0:T(2,128)S(1)}, f32[2,192]{1,0:T(2,128)S(1)}) custom-call(s32[1]{0:T(128)} %bitcast.index.refs_0_.me, bf16[2048,384]{1,0:T(8,128)(2,1)} %attend_back.4.refs_0_.refs_1_, bf16[2048,192]{1,0:T(8,128)(2,1)} %copy-done.13, bf16[784,576]{1,0:T(8,128)(2,1)} %copy-done.6, ...), custom_call_target="tpu_custom_call" | custom-call | flops 1 | bytes 1 | tf_op jit(solution)/shard_map/near_kernel/pallas_call | solution.py:652
  307.4 4.5 %fusion.30 = f32[1024,768]{1,0:T(8,128)S(1)} fusion(bf16[1024,1536]{1,0:T(8,128)(2,1)} %gate.15, bf16[768,1536]{1,0:T(8,128)(2,1)S(1)} %copy-done.10), kind=kOutput, calls=%fused_computation.77 | convolution fusion | flops 2415919104 | bytes 8650752 | tf_op jit(solution)/shard_map/dot_general | solution.py:47
  313.9 4.6 %collective-permute-start.38 = (f32[12,768]{1,0:T(8,128)S(1)}, f32[12,768]{1,0:T(8,128)S(1)}, u32[]{:S(2)}, u32[]{:S(2)}) collective-permute-start(f32[12,768]{1,0:T(8,128)S(1)} %add.180), channel_id=1, source_target_pairs={{0,8},{4,12},{8,0},{12,4},{16,24},{20,28},{24,16},{28,20},{1,9},{5... | collective-permute-start | bytes 110600 | tf_op jit(solution)/shard_map/ppermute | solution.py:690
  328.6 3.1 fusion.1
  331.8 3.4 %last_kernel.1 = f32[512,768]{1,0:T(8,128)} custom-call(f32[512,768]{1,0:T(8,128)S(1)} %copy-done.31, bf16[512,768]{1,0:T(8,128)(2,1)S(1)} %collective-permute-done.33.refs_1_, bf16[512,768]{1,0:T(8,128)(2,1)} %collective-permute-done.34.refs_2_, bf16[512,768]{1,0:T(8,128)(2,1)S(1)} %copy-done.24, f32[512,768]{1,0:T(8,128)S(1)} %copy-done.49, ...), custom_call_target="tpu_custom_call" | custom-call | flops 1 | bytes 1 | tf_op jit(solution)/shard_map/last_kernel/pallas_call | solution.py:652
  (385 shorter events, 152.7 us)
Async XLA Ops:
  1.2 21.4 %collective-permute-start = (bf16[512,768]{1,0:T(8,128)(2,1)}, bf16[512,768]{1,0:T(8,128)(2,1)S(1)}, u32[]{:S(2)}, u32[]{:S(2)}) collective-permute-start(bf16[512,768]{1,0:T(8,128)(2,1)} %refs_3_.1), channel_id=1, source_target_pairs={{0,2},{1,3},{2,0},{3,1},{4,6},{5,7},{6,4},{7,5},{8,10},{9,11},{10,... | collective-permute-start | bytes 2359304 | tf_op jit(solution)/shard_map/ppermute | solution.py:690
  3.8 24.0 %collective-permute-start.8 = (bf16[512,768]{1,0:T(8,128)(2,1)}, bf16[512,768]{1,0:T(8,128)(2,1)S(1)}, u32[]{:S(2)}, u32[]{:S(2)}) collective-permute-start(bf16[512,768]{1,0:T(8,128)(2,1)} %cotangent.1), channel_id=1, source_target_pairs={{0,1},{1,0},{2,3},{3,2},{4,5},{5,4},{6,7},{7,6},{8,9},{9,8},{10,11... | collective-permute-start | bytes 2359304 | tf_op jit(solution)/shard_map/ppermute | solution.py:690
  23.4 18.9 %collective-permute-start.5 = (bf16[512,768]{1,0:T(8,128)(2,1)}, bf16[512,768]{1,0:T(8,128)(2,1)}, u32[]{:S(2)}, u32[]{:S(2)}) collective-permute-start(bf16[512,768]{1,0:T(8,128)(2,1)} %gate.8.piece), channel_id=1, source_target_pairs={{0,1},{1,0},{2,3},{3,2},{4,5},{5,4},{6,7},{7,6},{8,9},{9,8},{10,11... | collective-permute-start | bytes 2359304 | tf_op jit(solution)/shard_map/ppermute | solution.py:690
  27.9 30.5 %collective-permute-start.10 = (bf16[96,1984]{1,0:T(8,128)(2,1)S(1)}, bf16[96,1984]{1,0:T(8,128)(2,1)S(1)}, u32[]{:S(2)}, u32[]{:S(2)}) collective-permute-start(bf16[96,1984]{1,0:T(8,128)(2,1)S(1)} %pack_kernel.1.refs_3_.refs_0_), channel_id=1, source_target_pairs={{0,16},{4,20},{8,24},{12,28},{16,0},{20,4},{24,8},{28,12},{1,17},{... | collective-permute-start | bytes 1142792 | tf_op jit(solution)/shard_map/ppermute | solution.py:690
  32.0 26.9 %collective-permute-start.9 = (bf16[96,1984]{1,0:T(8,128)(2,1)S(1)}, bf16[96,1984]{1,0:T(8,128)(2,1)S(1)}, u32[]{:S(2)}, u32[]{:S(2)}) collective-permute-start(bf16[96,1984]{1,0:T(8,128)(2,1)S(1)} %pack_kernel.1.refs_3_.refs_0_), channel_id=1, source_target_pairs={{0,8},{4,12},{8,0},{12,4},{16,24},{20,28},{24,16},{28,20},{1,9},{5... | collective-permute-start | bytes 1142792 | tf_op jit(solution)/shard_map/ppermute | solution.py:690
  32.0 26.9 %collective-permute-start.11 = (bf16[96,1984]{1,0:T(8,128)(2,1)S(1)}, bf16[96,1984]{1,0:T(8,128)(2,1)}, u32[]{:S(2)}, u32[]{:S(2)}) collective-permute-start(bf16[96,1984]{1,0:T(8,128)(2,1)S(1)} %pack_kernel.1.refs_3_.refs_0_), channel_id=1, source_target_pairs={{0,24},{4,28},{8,16},{12,20},{16,8},{20,12},{24,0},{28,4},{1,25},{... | collective-permute-start | bytes 1142792 | tf_op jit(solution)/shard_map/ppermute | solution.py:690
  60.0 31.6 %collective-permute-start.13 = (bf16[4,96,1216]{2,1,0:T(8,128)(2,1)S(1)}, bf16[4,96,1216]{2,1,0:T(8,128)(2,1)S(1)}, u32[]{:S(2)}, u32[]{:S(2)}) collective-permute-start(bf16[4,96,1216]{2,1,0:T(8,128)(2,1)S(1)} %get-tuple-element.64.refs_0_.refs_1_), channel_id=1, source_target_pairs={{0,4},{4,0},{8,12},{12,8},{16,20},{20,16},{24,28},{28,24},{1,5},{5... | collective-permute-start | bytes 2801672 | tf_op jit(solution)/shard_map/ppermute | solution.py:690
  75.7 15.7 %collective-permute-start.14 = (bf16[4,96,768]{2,1,0:T(8,128)(2,1)S(1)}, bf16[4,96,768]{2,1,0:T(8,128)(2,1)S(1)}, u32[]{:S(2)}, u32[]{:S(2)}) collective-permute-start(bf16[4,96,768]{2,1,0:T(8,128)(2,1)S(1)} %get-tuple-element.70.refs_0_), channel_id=1, source_target_pairs={{0,2},{1,3},{2,0},{3,1},{4,6},{5,7},{6,4},{7,5},{8,10},{9,11},{10,... | collective-permute-start | bytes 1769480 | tf_op jit(solution)/shard_map/ppermute | solution.py:690
  103.9 28.4 %collective-permute-start.18 = (bf16[784,768]{1,0:T(8,128)(2,1)}, bf16[784,768]{1,0:T(8,128)(2,1)}, u32[]{:S(2)}, u32[]{:S(2)}) collective-permute-start(bf16[784,768]{1,0:T(8,128)(2,1)} %gate.9.refs_9_.up_a), channel_id=1, source_target_pairs={{0,2},{1,3},{2,0},{3,1},{4,6},{5,7},{6,4},{7,5},{8,10},{9,11},{10,... | collective-permute-start | bytes 3612680 | tf_op jit(solution)/shard_map/ppermute | solution.py:690
  104.3 26.4 %collective-permute-start.19 = (bf16[4,96,1536]{2,1,0:T(8,128)(2,1)S(1)}, bf16[4,96,1536]{2,1,0:T(8,128)(2,1)S(1)}, u32[]{:S(2)}, u32[]{:S(2)}) collective-permute-start(bf16[4,96,1536]{2,1,0:T(8,128)(2,1)S(1)} %beside_kernel.3.refs_3_.refs_1_), channel_id=1, source_target_pairs={{0,4},{4,0},{8,12},{12,8},{16,20},{20,16},{24,28},{28,24},{1,5},{5... | collective-permute-start | bytes 3538952 | tf_op jit(solution)/shard_map/ppermute | solution.py:690
  112.9 19.4 %collective-permute-start.17 = (bf16[512,768]{1,0:T(8,128)(2,1)}, bf16[512,768]{1,0:T(8,128)(2,1)}, u32[]{:S(2)}, u32[]{:S(2)}) collective-permute-start(bf16[512,768]{1,0:T(8,128)(2,1)} %get-tuple-element.74.refs_3_.mine), channel_id=1, source_target_pairs={{0,1},{1,0},{2,3},{3,2},{4,5},{5,4},{6,7},{7,6},{8,9},{9,8},{10,11... | collective-permute-start | bytes 2359304 | tf_op jit(solution)/shard_map/ppermute | solution.py:690
  166.9 28.7 %collective-permute-start.24 = (bf16[4,96,1536]{2,1,0:T(8,128)(2,1)}, bf16[4,96,1536]{2,1,0:T(8,128)(2,1)}, u32[]{:S(2)}, u32[]{:S(2)}) collective-permute-start(bf16[4,96,1536]{2,1,0:T(8,128)(2,1)} %fusion.12), channel_id=1, source_target_pairs={{0,4},{4,0},{8,12},{12,8},{16,20},{20,16},{24,28},{28,24},{1,5},{5... | collective-permute-start | bytes 3538952 | tf_op jit(solution)/shard_map/ppermute | solution.py:690
  171.7 21.7 %collective-permute-start.26 = (bf16[192,768]{1,0:T(8,128)(2,1)S(1)}, bf16[192,768]{1,0:T(8,128)(2,1)}, u32[]{:S(2)}, u32[]{:S(2)}) collective-permute-start(bf16[192,768]{1,0:T(8,128)(2,1)S(1)} %fusion.16.refs_0_), channel_id=1, source_target_pairs={{0,2},{1,3},{2,0},{3,1},{4,6},{5,7},{6,4},{7,5},{8,10},{9,11},{10,... | collective-permute-start | bytes 884744 | tf_op jit(solution)/shard_map/ppermute | solution.py:690
  178.2 46.5 %collective-permute-start.25 = (bf16[768,768]{1,0:T(8,128)(2,1)}, bf16[768,768]{1,0:T(8,128)(2,1)}, u32[]{:S(2)}, u32[]{:S(2)}) collective-permute-start(bf16[768,768]{1,0:T(8,128)(2,1)} %gate.13), channel_id=1, source_target_pairs={{0,2},{1,3},{2,0},{3,1},{4,6},{5,7},{6,4},{7,5},{8,10},{9,11},{10,... | collective-permute-start | bytes 3538952 | tf_op jit(solution)/shard_map/ppermute | solution.py:690
  200.6 68.7 %collective-permute-start.29 = (bf16[96,1536]{1,0:T(8,128)(2,1)}, bf16[96,1536]{1,0:T(8,128)(2,1)}, u32[]{:S(2)}, u32[]{:S(2)}) collective-permute-start(bf16[96,1536]{1,0:T(8,128)(2,1)} %get-tuple-element.136), channel_id=1, source_target_pairs={{0,8},{4,12},{8,0},{12,4},{16,24},{20,28},{24,16},{28,20},{1,9},{5... | collective-permute-start | bytes 884744 | tf_op jit(solution)/shard_map/ppermute | solution.py:690
  208.6 60.7 %collective-permute-start.31 = (bf16[96,1536]{1,0:T(8,128)(2,1)}, bf16[96,1536]{1,0:T(8,128)(2,1)}, u32[]{:S(2)}, u32[]{:S(2)}) collective-permute-start(bf16[96,1536]{1,0:T(8,128)(2,1)} %get-tuple-element.137), channel_id=1, source_target_pairs={{0,24},{4,28},{8,16},{12,20},{16,8},{20,12},{24,0},{28,4},{1,25},{... | collective-permute-start | bytes 884744 | tf_op jit(solution)/shard_map/ppermute | solution.py:690
  210.9 58.4 %collective-permute-start.30 = (bf16[96,1536]{1,0:T(8,128)(2,1)}, bf16[96,1536]{1,0:T(8,128)(2,1)}, u32[]{:S(2)}, u32[]{:S(2)}) collective-permute-start(bf16[96,1536]{1,0:T(8,128)(2,1)} %get-tuple-element.138), channel_id=1, source_target_pairs={{0,16},{4,20},{8,24},{12,28},{16,0},{20,4},{24,8},{28,12},{1,17},{... | collective-permute-start | bytes 884744 | tf_op jit(solution)/shard_map/ppermute | solution.py:690
  227.9 47.0 %collective-permute-start.28 = (bf16[4,96,960]{2,1,0:T(8,128)(2,1)}, bf16[4,96,960]{2,1,0:T(8,128)(2,1)}, u32[]{:S(2)}, u32[]{:S(2)}) collective-permute-start(bf16[4,96,960]{2,1,0:T(8,128)(2,1)} %fusion.13.refs_2_), channel_id=1, source_target_pairs={{0,4},{4,0},{8,12},{12,8},{16,20},{20,16},{24,28},{28,24},{1,5},{5... | collective-permute-start | bytes 2211848 | tf_op jit(solution)/shard_map/ppermute | solution.py:690
  232.8 45.0 %all-to-all-start = ((bf16[8,96,384]{2,1,0:T(8,128)(2,1)}), bf16[8,96,384]{2,1,0:T(8,128)(2,1)}, u32[]{:S(2)}, u32[]{:S(2)}) async-start(bf16[8,96,384]{2,1,0:T(8,128)(2,1)} %bitcast.116), calls=%async_computation | async-start | bytes 1179648 | tf_op jit(solution)/shard_map/all_to_all | solution.py:711
  271.7 20.6 %collective-permute-start.43 = (bf16[96,768]{1,0:T(8,128)(2,1)S(1)}, bf16[96,768]{1,0:T(8,128)(2,1)S(1)}, u32[]{:S(2)}, u32[]{:S(2)}) collective-permute-start(bf16[96,768]{1,0:T(8,128)(2,1)S(1)} %slice.208), channel_id=1, source_target_pairs={{0,2},{1,3},{2,0},{3,1},{4,6},{5,7},{6,4},{7,5},{8,10},{9,11},{10,... | collective-permute-start | bytes 442376 | tf_op jit(solution)/shard_map/ppermute | solution.py:690
  277.8 18.2 %all-to-all-start.1 = ((bf16[8,96,192]{2,1,0:T(8,128)(2,1)}), bf16[8,96,192]{2,1,0:T(8,128)(2,1)S(1)}, u32[]{:S(2)}, u32[]{:S(2)}) async-start(bf16[8,96,192]{2,1,0:T(8,128)(2,1)} %bitcast.36), calls=%async_computation.1 | async-start | bytes 786432 | tf_op jit(solution)/shard_map/all_to_all | solution.py:711
  302.2 17.8 %collective-permute-start.41 = (bf16[96,960]{1,0:T(8,128)(2,1)S(1)}, bf16[96,960]{1,0:T(8,128)(2,1)}, u32[]{:S(2)}, u32[]{:S(2)}) collective-permute-start(bf16[96,960]{1,0:T(8,128)(2,1)S(1)} %get-tuple-element.141), channel_id=1, source_target_pairs={{0,16},{4,20},{8,24},{12,28},{16,0},{20,4},{24,8},{28,12},{1,17},{... | collective-permute-start | bytes 552968 | tf_op jit(solution)/shard_map/ppermute | solution.py:690
  303.7 28.0 %collective-permute-start.34 = (bf16[512,768]{1,0:T(8,128)(2,1)S(1)}, bf16[512,768]{1,0:T(8,128)(2,1)}, u32[]{:S(2)}, u32[]{:S(2)}) collective-permute-start(bf16[512,768]{1,0:T(8,128)(2,1)S(1)} %add_convert_fusion.refs_10_), channel_id=1, source_target_pairs={{0,2},{1,3},{2,0},{3,1},{4,6},{5,7},{6,4},{7,5},{8,10},{9,11},{10,... | collective-permute-start | bytes 2359304 | tf_op jit(solution)/shard_map/ppermute | solution.py:690
  313.9 17.9 %collective-permute-start.33 = (bf16[512,768]{1,0:T(8,128)(2,1)}, bf16[512,768]{1,0:T(8,128)(2,1)S(1)}, u32[]{:S(2)}, u32[]{:S(2)}) collective-permute-start(bf16[512,768]{1,0:T(8,128)(2,1)} %get-tuple-element.92), channel_id=1, source_target_pairs={{0,1},{1,0},{2,3},{3,2},{4,5},{5,4},{6,7},{7,6},{8,9},{9,8},{10,11... | collective-permute-start | bytes 2359304 | tf_op jit(solution)/shard_map/ppermute | solution.py:690
  (122 other events, 968.6 us)

commit v3 on v2

--- a/solution.py
+++ b/solution.py
@@ -277,10 +277,10 @@
     )(normed, weights)
 
 
-def attend_kernel(count, query_ref, key_ref, value_ref, seg_col, seg_row, *refs):
+def attend_kernel(count, query_ref, key_ref, value_ref, seg_row, *refs):
     out, lse, c_s = refs[count], refs[count + 1], refs[count + 2]
     rows = out.shape[0]
-    c_s[...] = jnp.broadcast_to(seg_col[...], (rows, 128))
+    c_s[...] = jnp.transpose(jnp.broadcast_to(seg_row[...], (128, rows)))
     for i in range(rows // BLK):
         mine = pl.ds(i * BLK, BLK)
         query = query_ref[0, mine, :]
@@ -329,19 +329,19 @@
     return pl.BlockSpec(array.shape, lambda i: (0,) * array.ndim)
 
 
-def attend(split, head, seg_col, seg_row, deps=()):
+def attend(split, head, seg_row, deps=()):
     count, rows = split.shape[0] // 3, split.shape[1]
     return pl.pallas_call(
         functools.partial(attend_kernel, len(deps)),
         grid=(1,),
-        in_specs=head_specs(split, head, count) + [full_spec(seg_col), full_spec(seg_row)] + [ANYWHERE] * len(deps),
+        in_specs=head_specs(split, head, count) + [full_spec(seg_row)] + [ANYWHERE] * len(deps),
         out_specs=[pl.BlockSpec((rows, HD), lambda i: (0, 0)), pl.BlockSpec((8, rows), lambda i: (0, 0))],
         out_shape=(shape16(rows, HD), shape32(8, rows)),
         scratch_shapes=[pltpu.VMEM((rows, 128), jnp.int32)],
         compiler_params=ROOM,
         cost_estimate=cost(7e9, rows * 1024, rows * rows // 2),
         name="attend",
-    )(split, split, split, seg_col, seg_row, *deps)
+    )(split, split, split, seg_row, *deps)
 
 
 def deal_kernel(me, *refs):
@@ -354,7 +354,7 @@
 
 
 def attend_back_kernel(
-    head, count, extra, me, query_ref, key_ref, value_ref, mixed, near, core, far, lse, seg_col, seg_row, *refs
+    head, count, extra, me, query_ref, key_ref, value_ref, mixed, near, core, far, lse, seg_row, *refs
 ):
     earlier, out = refs[:extra], refs[extra + count]
     g_s, d_s, dk_s, dv_s, c_s = refs[extra + count + 1 :]
@@ -364,7 +364,7 @@
     for m, piece in enumerate((near[:, lanes], core[0, :, lanes], far[:, lanes], core[1, :, lanes])):
         start = pl.multiple_of(jnp.bitwise_xor(me[0], m) * own, own)
         g_s[pl.ds(start, own), :] = piece
-    c_s[...] = jnp.broadcast_to(seg_col[...], (rows, 128))
+    c_s[...] = jnp.transpose(jnp.broadcast_to(seg_row[...], (128, rows)))
     inner = jnp.sum(wide(mixed[...]) * wide(g_s[...]), axis=1, keepdims=True)
     d_s[...] = jnp.transpose(jnp.broadcast_to(inner, (rows, 128)))[0:8, :]
     def store(kind, where, values):
@@ -414,10 +414,10 @@
         out[:, 3 * h * HD : 3 * (h + 1) * HD] = ref[...]
 
 
-def attend_back(split, head, mixed, near, core, far, lse, seg_col, seg_row, earlier=(), deps=()):
+def attend_back(split, head, mixed, near, core, far, lse, seg_row, earlier=(), deps=()):
     count, rows = split.shape[0] // 3, split.shape[1]
     full = pltpu.VMEM((rows, HD), jnp.float32)
-    operands = [mixed, near, core, far, lse, seg_col, seg_row, *earlier]
+    operands = [mixed, near, core, far, lse, seg_row, *earlier]
     shape = shape16(rows, 3 * (len(earlier) + 1) * HD)
     return pl.pallas_call(
         functools.partial(attend_back_kernel, head, len(deps), len(earlier)),
@@ -595,17 +595,23 @@
     chip[...] = head_part(me, 2, own, first, last, weights)
 
 
-def near_kernel(me, first, last, weights, chip, diagonal, t0, t1, t2, t3, mine, core, sums, bias_sum):
+def near_kernel(
+    me, first, last, weights, chip, diagonal, t0, t1, t2, t3, mine, core, sums, bias_sum, normed_s, arrived
+):
     own = chip.shape[0]
+    copies = [pltpu.make_async_copy(t, normed_s.at[k], arrived.at[k]) for k, t in enumerate((t0, t1, t2, t3))]
+    for copy in copies:
+        copy.start()
     gain_sum, shift_sum = 0.0, 0.0
-    for m, normed in enumerate((t0, t1, t2, t3)):
+    for m, copy in enumerate(copies):
         if m < 2:
             part = head_part(me, m, own, first, last, weights)
             out = core if m else mine
             out[...] = part.astype(out.dtype)
         else:
             part = wide((diagonal if m == 3 else chip)[...])
-        gain_sum = gain_sum + jnp.sum(part * wide(normed[...]), axis=0, keepdims=True)
+        copy.wait()
+        gain_sum = gain_sum + jnp.sum(part * wide(normed_s[m]), axis=0, keepdims=True)
         shift_sum = shift_sum + jnp.sum(part, axis=0, keepdims=True)
     sums[0:1, :] = gain_sum
     sums[1:2, :] = shift_sum
@@ -618,16 +624,19 @@
                 bias_sum[row : row + 1, (base + h) * HD : (base + h + 1) * HD] = total[:, at : at + HD]
 
 
-def finish_kernel(first, last, out):
+def finish_kernel(first, last, out, vectors):
+    rows = out.shape[1]
     heads = out.shape[2] // HD
     for source, base in ((first, 0), (last, heads - 1)):
         total = wide(source[0])
         for k in range(1, source.shape[0]):
             total = total + wide(source[k])
+        if base:
+            vectors[...] = total[rows:, :]
         for h in range(source.shape[2] // (3 * HD)):
             for kind in range(3):
                 at = (3 * h + kind) * HD
-                out[kind, :, (base + h) * HD : (base + h + 1) * HD] = total[:, at : at + HD]
+                out[kind, :, (base + h) * HD : (base + h + 1) * HD] = total[:rows, at : at + HD]
 
 
 def last_kernel(mine, core, chip, tokens, hidden_grad, gain, out):
@@ -636,8 +645,9 @@
     out[...] = hidden_grad[...] + norm_back(normed, scale, grad)
 
 
-def call(kernel, out_shape, flops, size, *operands, scalar=None, deps=(), scratch=(), name=None):
-    specs = [full_spec(array) for array in operands] + [ANYWHERE] * len(deps)
+def call(kernel, out_shape, flops, size, *operands, scalar=None, direct=(), deps=(), scratch=(), name=None):
+    specs = [full_spec(array) for array in operands] + [ANYWHERE] * (len(direct) + len(deps))
+    operands = operands + tuple(direct)
     outs = tuple(full_spec(shape) for shape in out_shape) if isinstance(out_shape, tuple) else full_spec(out_shape)
     count = len(operands)
     if scalar is not None:
@@ -726,16 +736,6 @@
     for mask in range(2, size, 2):
         total = total + wide(flip(pick(sent, (me ^ mask) // 2), "dp", mask))
     return total
-
-
-def sum_everywhere(values):
-    for mask in (1, 2):
-        values = values + flip(values, "tensor", mask)
-    mask = 1
-    while mask < lax.axis_size("dp"):
-        values = values + flip(values, "dp", mask)
-        mask *= 2
-    return values
 
 
 def contract_rows(left_mat, right_mat):
@@ -781,9 +781,10 @@
     from_chip = gate(from_chip, qkv_column)
     from_diagonal = core_swap(from_chip)
 
-    edge = hidden + 2 * span + HD
+    edges = (0, hidden, hidden + 2 * span, 2 * hidden + 2 * span + HD)
+    cuts = tuple(zip(edges, edges[1:]))
     rest_pack = pack(
-        [w_down.T, w_up, out_turned, out_turned_chip], spread(up_bias, PAD), deps=(qkv_column, top_core)
+        [w_down.T, out_turned, out_turned_chip, w_up], spread(up_bias, PAD), deps=(qkv_column, top_core)
     )
     bias_at = tuple(3 * h + kind for kind in (0, 2) for h in range(heads))
     (qkv_full,) = lay(qkv_column, (3 * span,), bias_at, deps=(rest_pack,))
@@ -791,17 +792,19 @@
     first_norm, normed_diagonal = first_norm_of(from_diagonal, ln1_gain, ln1_bias, me ^ 3, normed_chip, first_norm)
     first_norm = first_norm.reshape(4 * own, width)
 
-    seg_col, seg_row = segment[:, None], segment[None, :]
+    seg_row = segment[None, :]
     split = project(first_norm, qkv_full)
     heads_out, log_totals = [], []
     for head in range(heads):
         deps = () if head == 0 else (up_column, heads_out[-1])
-        out, log_total = attend(split, head, seg_col, seg_row, deps)
+        out, log_total = attend(split, head, seg_row, deps)
         heads_out.append(out)
         log_totals.append(log_total)
         if head == 0:
-            down_column, up_column = columns(rest_pack, ((0, hidden), (hidden, hidden + edge)), (out,))
-
+            down_column, out_column, up_column = columns(rest_pack, cuts, (out,))
+
+    (up_own,) = lay(up_column, (hidden,), tuple(range(hidden // HD)), deps=(heads_out[-1],))
+    down_columns = beside(down_column, chip_swap(down_column), deps=(up_own,))
     mixed_own, mixed_chip, to_core = call(
         deal_kernel,
         (shape16(own, span), shape16(own, span), shape16(2, own, span)),
@@ -809,13 +812,12 @@
         own * span * 24,
         *heads_out,
         scalar=me,
+        deps=(down_columns,),
     )
     mixed_core = core_swap(to_core)
-    down_columns = beside(down_column, chip_swap(down_column), deps=(to_core,))
-    up_own, out_pair = lay(up_column, (hidden, 2 * span), tuple(range(hidden // HD)), True, (down_columns,))
-    mixed_far = beside(mixed_chip, mixed_core[1], deps=(up_own,))
+    mixed_far = beside(mixed_chip, mixed_core[1])
+    (out_pair,) = lay(out_column, (2 * span,), turned=True, deps=(mixed_far,))
     mixed_far = chip_swap(mixed_far)
-    up_own = gate(up_own, mixed_far)
     out_core = core_swap(out_pair)
     hidden_one, second, out_full = join(
         mixed_own, mixed_core, mixed_far, out_pair, out_core, tokens, out_bias, ln2_gain, ln2_bias, (up_own,)
@@ -856,7 +858,6 @@
             grad_core,
             grad_far,
             log_totals[head],
-            seg_col,
             seg_row,
             earlier,
             deps,
@@ -908,24 +909,37 @@
         qkv_full,
         part_chip,
         part_diagonal,
-        normed_own,
-        normed_core,
-        normed_chip,
-        normed_diagonal,
         scalar=me,
+        direct=(normed_own, normed_core, normed_chip, normed_diagonal),
+        scratch=[pltpu.VMEM((4, own, width), jnp.bfloat16), pltpu.SemaphoreType.DMA((4,))],
         deps=(chip_sum, last_whole),
     )
     chip_sum = chip_swap(chip_sum)
-    (w_qkv_grad_out,) = call(
-        finish_kernel, (shape32(3, rows_shard, span),), 0, width * span * 6, first_blocks, swap_blocks(last_whole)
-    )
-
+
+    bias_spread = place(jnp.zeros((4, 2, span), jnp.float32), bias_sum, me)
+    up_rows = place(jnp.zeros((4, hidden), jnp.float32), up_bias_sum[0, :hidden], me)
+    up_rows = place(up_rows, up_bias_sum[0, hidden:], me ^ 2)
+    sums = jnp.concatenate(
+        [first_sums, turn_sums, bias_spread.reshape(-1, width), up_rows.reshape(-1, width)], axis=0
+    )
     up_out = sum_column(up_column, up_sent) if few else jnp.sum(wide(up_sent), axis=0)
+    packed = gate(low(sums).reshape(-1, 3 * HD), up_out, chip_sum)
+    last_blocks = lax.all_to_all(
+        plain(
+            jnp.concatenate(
+                [last_whole.reshape(dp, rows_shard, 3 * HD), jnp.broadcast_to(packed, (dp,) + packed.shape)], axis=1
+            )
+        ),
+        "dp",
+        0,
+        0,
+        tiled=True,
+    )
     down_grad_out = (down_part[:, :hidden] + wide(chip_swap(low(down_part[:, hidden:])))).T
     up_grad_out = up_out[:, :hidden]
     w_out_grad_out = up_out[:, hidden:].T
 
-    active = gate(active.reshape(2 * own, 2 * hidden), part_own)
+    active = gate(active.reshape(2 * own, 2 * hidden), packed)
     mlp_part = dot32(active, down_pair, NT)
     mlp_branch = mlp_part[:own] + wide(core_swap(low(mlp_part[own:])))
     block_out = hidden_one + (mlp_branch + wide(down_bias))
@@ -943,14 +957,18 @@
         ln1_gain[None],
     )
 
-    bias_spread = jnp.zeros((4, 2, span), jnp.float32)
-    bias_spread = place(bias_spread, bias_sum, me)
-    up_rows = jnp.zeros((4, hidden), jnp.float32)
-    up_rows = place(up_rows, up_bias_sum[0, :hidden], me)
-    up_rows = place(up_rows, up_bias_sum[0, hidden:], me ^ 2)
-    sums = sum_everywhere(
-        jnp.concatenate([first_sums, turn_sums, bias_spread.reshape(-1, width), up_rows.reshape(-1, width)], axis=0)
-    )
+    w_qkv_grad_out, packed = call(
+        finish_kernel,
+        (shape32(3, rows_shard, span), shape32(*packed.shape)),
+        0,
+        width * span * 6,
+        first_blocks,
+        last_blocks,
+        deps=(token_grad,),
+    )
+    sums = packed.reshape(sums.shape)
+    sums = sums + core_swap(sums) + chip_swap(sums) + flip(sums, "tensor", 3)
+
     count = bias_spread.size // width
     qv_bias_grad = pick(sums[6 : 6 + count].reshape((4, 2, span // HD, dp, qv_bias.shape[2])), me)
     qv_bias_grad = lax.dynamic_index_in_dim(qv_bias_grad, place_dp, 2, keepdims=False)

time: 341 us -> 345 us (1.012)
  Pallas kernels: 118 us -> 107 us
  other arithmetic: 21 us -> 30.8 us
  local copies, waits for them, and re-layouts: 56.9 us -> 65.9 us
  starting transfers between devices: 61.3 us -> 57.3 us
    pallas_call x18, Pallas kernels: 25.5 us -> 16.9 us  [call(): pl.pallas_call(body, grid=(1,), out_shape=out_shape, in_specs=specs, out_...]
    unnamed x205 -> x193, local copies, waits for them, and re-layouts: 38.3 us -> 46.6 us
    pallas_call x0 -> x1, other arithmetic: none -> 7.36 us  [call(): pl.pallas_call(body, grid=(1,), out_shape=out_shape, in_specs=specs, out_...]
    all_to_all x2 -> x1, starting transfers between devices: 11.3 us -> 5.09 us  [swap_blocks(): return lax.all_to_all(plain(blocks), 'dp', 0, 0, tiled=True)]
    all_to_all x0 -> x1, starting transfers between devices: none -> 4.94 us  [on_device(): lax.all_to_all(plain(jnp.concatenate([last_whole.reshape(dp, rows_shard,...]
    ppermute x44 -> x43, waiting for transfers between devices: 55.4 us -> 59.5 us  [flip(): lax.ppermute(plain(values), axis, [(i, i ^ mask) for i in range(size)])]
    ppermute x44 -> x43, starting transfers between devices: 50 us -> 47.3 us  [flip(): lax.ppermute(plain(values), axis, [(i, i ^ mask) for i in range(size)])]
  transfers between devices with their start and end apart: 46 -> 45, of which waited for: 12 -> 10; matrix products, arithmetic and copies ran while one was open for 18% -> 19% of each run, Pallas kernels for 28% -> 26%
where the time goes in v3:
time: 345 us; the launch traced here: 339 us
  Pallas kernels  107 us (31%)
  local copies, waits for them, and re-layouts  65.9 us (19%)
  waiting for transfers between devices  59.5 us (17%)
  starting transfers between devices  57.3 us (17%)
  other arithmetic  30.8 us (9%)
  matrix products  16.6 us (5%)
    ppermute x43, waiting for transfers between devices, flip(): lax.ppermute(plain(values), axis, [(i, i ^ mask) for i in range(size)])  59.5 us
    ppermute x43, starting transfers between devices, flip(): lax.ppermute(plain(values), axis, [(i, i ^ mask) for i in range(size)])  47.3 us
    unnamed x193, local copies, waits for them, and re-layouts  46.6 us
    pallas_call x3, Pallas kernels, attend_back(): pl.pallas_call(functools.partial(attend_back_kernel, head, len(deps), len...  37.7 us
    pallas_call x3, Pallas kernels, attend(): pl.pallas_call(functools.partial(attend_kernel, len(deps)), grid=(1,), in...  19.3 us
    pallas_call x18, Pallas kernels, call(): pl.pallas_call(body, grid=(1,), out_shape=out_shape, in_specs=specs, out_...  16.9 us
    dot_general x8, matrix products, dot32(): lax.dot_general(left, right, dims, preferred_element_type=jnp.float32)  16.6 us
    pallas_call x1, Pallas kernels, mlp(): pl.pallas_call(mlp_kernel, grid=(steps,), in_specs=[row_spec] * 4 + [whol...  13.8 us
  transfers between devices with their start and end apart: 45, of which 10 were waited for; matrix products, arithmetic and copies ran while one was open for 19% of the time, Pallas kernels for 26%

profile of v3, /device:TPU:0, one launch (start us, length us, event | category | flops | bytes accessed | tf_op | source)
XLA Modules:
  0.0 339.5 jit_solution(11867055187405929540)
XLA Ops:
  27.9 4.1 %collective-permute-start.10 = (bf16[96,1984]{1,0:T(8,128)(2,1)S(1)}, bf16[96,1984]{1,0:T(8,128)(2,1)S(1)}, u32[]{:S(2)}, u32[]{:S(2)}) collective-permute-start(bf16[96,1984]{1,0:T(8,128)(2,1)S(1)} %pack_kernel.1.refs_3_.refs_0_), channel_id=1, source_target_pairs={{0,16},{4,20},{8,24},{12,28},{16,0},{20,4},{24,8},{28,12},{1,17},{... | collective-permute-start | bytes 1142792 | tf_op jit(solution)/shard_map/ppermute | solution.py:700
  33.6 4.9 %collective-permute-done.6.refs_2_ = bf16[4,96,640]{2,1,0:T(8,128)(2,1)S(1)} collective-permute-done((bf16[4,96,640]{2,1,0:T(8,128)(2,1)S(1)}, bf16[4,96,640]{2,1,0:T(8,128)(2,1)S(1)}, u32[]{:S(2)}, u32[]{:S(2)}) %collective-permute-start.6) | collective-permute-done | bytes 491552 | tf_op jit(solution)/shard_map/ppermute | solution.py:700
  46.8 4.9 %project.1.query_ref.key_ref.value_ref = bf16[9,2048,64]{2,1,0:T(8,128)(2,1)} custom-call(bf16[2048,768]{1,0:T(8,128)(2,1)S(1)} %bitcast.112, bf16[784,576]{1,0:T(8,128)(2,1)S(1)} %copy-done.8), custom_call_target="tpu_custom_call" | custom-call | flops 1 | bytes 1 | tf_op jit(solution)/shard_map/project/pallas_call | solution.py:265
  54.1 5.3 %attend.3 = (bf16[2048,64]{1,0:T(8,128)(2,1)S(1)}, f32[8,2048]{1,0:T(8,128)S(1)}) custom-call(bf16[9,2048,64]{2,1,0:T(8,128)(2,1)S(1)} %copy-done, bf16[9,2048,64]{2,1,0:T(8,128)(2,1)S(1)} %copy-done, bf16[9,2048,64]{2,1,0:T(8,128)(2,1)S(1)} %copy-done, s32[1,2048]{1,0:T(1,128)S(1)} %bitcast.117), custom_call_target="tpu_custom_call" | custom-call | flops 1 | bytes 1 | tf_op jit(solution)/shard_map/attend/pallas_call | solution.py:334
  63.0 6.6 %attend.4 = (bf16[2048,64]{1,0:T(8,128)(2,1)S(1)}, f32[8,2048]{1,0:T(8,128)S(1)}) custom-call(bf16[9,2048,64]{2,1,0:T(8,128)(2,1)} %project.1.query_ref.key_ref.value_ref, bf16[9,2048,64]{2,1,0:T(8,128)(2,1)} %project.1.query_ref.key_ref.value_ref, bf16[9,2048,64]{2,1,0:T(8,128)(2,1)} %project.1.query_ref.key_ref.value_ref, s32[1,2048]{1,0:T(1,128)S(1)} %bitcast.118, ...), custom_call_target="tpu_custom_call" | custom-call | flops 1 | bytes 1 | tf_op jit(solution)/shard_map/attend/pallas_call | solution.py:334
  70.3 7.4 %attend.5 = (bf16[2048,64]{1,0:T(8,128)(2,1)S(1)}, f32[8,2048]{1,0:T(8,128)S(1)}) custom-call(bf16[9,2048,64]{2,1,0:T(8,128)(2,1)} %project.1.query_ref.key_ref.value_ref, bf16[9,2048,64]{2,1,0:T(8,128)(2,1)} %project.1.query_ref.key_ref.value_ref, bf16[9,2048,64]{2,1,0:T(8,128)(2,1)} %project.1.query_ref.key_ref.value_ref, s32[1,2048]{1,0:T(1,128)S(1)} %bitcast.119, ...), custom_call_target="tpu_custom_call" | custom-call | flops 1 | bytes 1 | tf_op jit(solution)/shard_map/attend/pallas_call | solution.py:334
  81.8 6.7 %collective-permute-done.16.refs_2_ = bf16[4,96,384]{2,1,0:T(8,128)(2,1)S(1)} collective-permute-done((bf16[4,96,384]{2,1,0:T(8,128)(2,1)S(1)}, bf16[4,96,384]{2,1,0:T(8,128)(2,1)S(1)}, u32[]{:S(2)}, u32[]{:S(2)}) %collective-permute-start.16) | collective-permute-done | bytes 294944 | tf_op jit(solution)/shard_map/ppermute | solution.py:700
  91.9 34.3 %collective-permute-done.15.refs_2_ = bf16[512,384]{1,0:T(8,128)(2,1)S(1)} collective-permute-done((bf16[512,384]{1,0:T(8,128)(2,1)S(1)}, bf16[512,384]{1,0:T(8,128)(2,1)S(1)}, u32[]{:S(2)}, u32[]{:S(2)}) %collective-permute-start.15) | collective-permute-done | bytes 393248 | tf_op jit(solution)/shard_map/ppermute | solution.py:700
  133.8 13.8 %mlp.1 = (bf16[2,512,1536]{2,1,0:T(8,128)(2,1)}, bf16[2,512,1536]{2,1,0:T(8,128)(2,1)}, f32[512,768]{1,0:T(8,128)}, bf16[512,768]{1,0:T(8,128)(2,1)}, f32[8,1536]{1,0:T(8,128)S(1)}) custom-call(bf16[512,768]{1,0:T(8,128)(2,1)S(1)} %get-tuple-element.74.refs_3_.mine, bf16[512,768]{1,0:T(8,128)(2,1)} %gate.10.other, bf16[512,768]{1,0:T(8,128)(2,1)S(1)} %copy-done.26, ...), custom_call_target="tpu_custom_call" | custom-call | flops 1 | bytes 1 | tf_op jit(solution)/shard_map/mlp/pallas_call | solution.py:523
  151.7 4.2 %turn.1 = (f32[512,768]{1,0:T(8,128)S(1)}, bf16[512,768]{1,0:T(8,128)(2,1)S(1)}, bf16[512,384]{1,0:T(8,128)(2,1)S(1)}, bf16[512,384]{1,0:T(8,128)(2,1)S(1)}, f32...) custom-call(f32[512,768]{1,0:T(8,128)} %get-tuple-element.75.mine, ...), custom_call_target="tpu_custom_call", output_to_operand_aliasing={{5}: (6, {}), {6}: (7, {})} | custom-call | flops 1 | bytes 1 | tf_op jit(solution)/shard_map/turn/pallas_call | solution.py:563
  178.7 12.7 %attend_back.3.refs_1_.refs_0_ = bf16[2048,192]{1,0:T(8,128)(2,1)S(1)} custom-call(s32[1]{0:T(128)} %bitcast.index.refs_0_.me, bf16[9,2048,64]{2,1,0:T(8,128)(2,1)} %project.1.query_ref.key_ref.value_ref, bf16[9,2048,64]{2,1,0:T(8,128)(2,1)} %project.1.query_ref.key_ref.value_ref, bf16[9,2048,64]{2,1,0:T(8,128)(2,1)} %project.1.query_ref.key_ref.value_ref, ...), custom_call_target="tpu_custom_call" | custom-call | flops 1 | bytes 1 | tf_op jit(solution)/shard_map/attend_back/pallas_call | solution.py:422
  194.6 3.9 %fusion.30 = (bf16[4,96,1536]{2,1,0:T(8,128)(2,1)S(1)}, f32[4,96,1536]{2,1,0:T(8,128)}) fusion(bf16[4,96,1536]{2,1,0:T(8,128)(2,1)} %gate.11, f32[4,2,96,1536]{3,2,1,0:T(8,128)} %bitcast.128, s32[]{:T(128)S(6)} %select_n.94), kind=kLoop, calls=%fused_computation.79 | loop fusion | flops 1769472 | bytes 7077892 | tf_op jit(solution)/shard_map/convert_element_type | solution.py:27
  199.5 7.8 %collective-permute-start.30 = (bf16[96,1536]{1,0:T(8,128)(2,1)}, bf16[96,1536]{1,0:T(8,128)(2,1)}, u32[]{:S(2)}, u32[]{:S(2)}) collective-permute-start(bf16[96,1536]{1,0:T(8,128)(2,1)} %get-tuple-element.146), channel_id=1, source_target_pairs={{0,8},{4,12},{8,0},{12,4},{16,24},{20,28},{24,16},{28,20},{1,9},{5... | collective-permute-start | bytes 884744 | tf_op jit(solution)/shard_map/ppermute | solution.py:700
  209.5 12.8 %attend_back.4.refs_0_.refs_1_ = bf16[2048,384]{1,0:T(8,128)(2,1)S(1)} custom-call(s32[1]{0:T(128)} %bitcast.index.refs_0_.me, bf16[9,2048,64]{2,1,0:T(8,128)(2,1)} %project.1.query_ref.key_ref.value_ref, bf16[9,2048,64]{2,1,0:T(8,128)(2,1)} %project.1.query_ref.key_ref.value_ref, bf16[9,2048,64]{2,1,0:T(8,128)(2,1)} %project.1.query_ref.key_ref.value_ref, ...), custom_call_target="tpu_custom_call" | custom-call | flops 1 | bytes 1 | tf_op jit(solution)/shard_map/attend_back/pallas_call | solution.py:422
  230.4 5.1 %all-to-all-start = ((bf16[8,96,384]{2,1,0:T(8,128)(2,1)}), bf16[8,96,384]{2,1,0:T(8,128)(2,1)}, u32[]{:S(2)}, u32[]{:S(2)}) async-start(bf16[8,96,384]{2,1,0:T(8,128)(2,1)} %bitcast.115), calls=%async_computation | async-start | bytes 1179648 | tf_op jit(solution)/shard_map/all_to_all | solution.py:721
  241.9 12.3 %attend_back.5.refs_2_.refs_1_ = bf16[2048,192]{1,0:T(8,128)(2,1)S(1)} custom-call(s32[1]{0:T(128)} %bitcast.index.refs_0_.me, bf16[9,2048,64]{2,1,0:T(8,128)(2,1)} %project.1.query_ref.key_ref.value_ref, bf16[9,2048,64]{2,1,0:T(8,128)(2,1)} %project.1.query_ref.key_ref.value_ref, bf16[9,2048,64]{2,1,0:T(8,128)(2,1)} %project.1.query_ref.key_ref.value_ref, ...), custom_call_target="tpu_custom_call" | custom-call | flops 1 | bytes 1 | tf_op jit(solution)/shard_map/attend_back/pallas_call | solution.py:422
  264.7 2.9 fusion.29
  282.3 7.4 %near_kernel.1 = (f32[4,2,192]{2,1,0:T(2,128)S(1)}, f32[2,768]{1,0:T(2,128)S(1)}, f32[512,768]{1,0:T(8,128)}, bf16[512,768]{1,0:T(8,128)(2,1)}) fusion(f32[4,2,192]{2,1,0:T(2,128)S(1)} %broadcast_in_dim.108, s32[]{:T(128)S(6)} %select_n.104, s32[1]{0:T(128)} %bitcast.index.refs_0_.me, bf16[2048,384]{1,0:T(8,128)(2,1)S(1)} %copy-done.6, ...), kind=kCustom, calls=%fused_computation.63 | custom fusion | flops 1 | bytes 12677128 | tf_op jit(solution)/shard_map/near_kernel/pallas_call | solution.py:662
  290.5 5.2 %collective-permute-done.34 = bf16[96,960]{1,0:T(8,128)(2,1)} collective-permute-done((bf16[96,960]{1,0:T(8,128)(2,1)}, bf16[96,960]{1,0:T(8,128)(2,1)}, u32[]{:S(2)}, u32[]{:S(2)}) %collective-permute-start.34) | collective-permute-done | bytes 184352 | tf_op jit(solution)/shard_map/ppermute | solution.py:700
  299.5 4.5 %fusion.34 = f32[1024,768]{1,0:T(8,128)S(1)} fusion(bf16[1024,1536]{1,0:T(8,128)(2,1)} %gate.15, bf16[768,1536]{1,0:T(8,128)(2,1)S(1)} %copy-done.12), kind=kOutput, calls=%fused_computation.83 | convolution fusion | flops 2415919104 | bytes 8650752 | tf_op jit(solution)/shard_map/dot_general | solution.py:47
  306.9 4.9 %all-to-all-start.1 = ((bf16[8,144,192]{2,1,0:T(8,128)(2,1)}), bf16[8,144,192]{2,1,0:T(8,128)(2,1)S(1)}, u32[]{:S(2)}, u32[]{:S(2)}) async-start(bf16[8,144,192]{2,1,0:T(8,128)(2,1)} %pad_maximum_fusion.2), calls=%async_computation.1 | async-start | bytes 1179648 | tf_op jit(solution)/shard_map/all_to_all | solution.py:927
  313.8 4.3 %collective-permute-done.42 = bf16[96,768]{1,0:T(8,128)(2,1)S(1)} collective-permute-done((bf16[96,768]{1,0:T(8,128)(2,1)S(1)}, bf16[96,768]{1,0:T(8,128)(2,1)S(1)}, u32[]{:S(2)}, u32[]{:S(2)}) %collective-permute-start.42) | collective-permute-done | bytes 147488 | tf_op jit(solution)/shard_map/ppermute | solution.py:700
  324.5 3.7 %last_kernel.1.refs_2_ = f32[512,768]{1,0:T(8,128)} custom-call(f32[512,768]{1,0:T(8,128)S(1)} %copy-done.34, bf16[512,768]{1,0:T(8,128)(2,1)} %collective-permute-done.38.refs_1_, bf16[512,768]{1,0:T(8,128)(2,1)} %collective-permute-done.36.refs_2_, bf16[512,768]{1,0:T(8,128)(2,1)S(1)} %copy-done.25, f32[512,768]{1,0:T(8,128)S(1)} %copy-done.48, ...), custom_call_target="tpu_custom_call" | custom-call | flops 1 | bytes 1 | tf_op jit(solution)/shard_map/last_kernel/pallas_call | solution.py:662
  334.0 3.0 fusion.1
  (373 shorter events, 154.7 us)
Async XLA Ops:
  1.2 21.5 %collective-permute-start = (bf16[512,768]{1,0:T(8,128)(2,1)}, bf16[512,768]{1,0:T(8,128)(2,1)S(1)}, u32[]{:S(2)}, u32[]{:S(2)}) collective-permute-start(bf16[512,768]{1,0:T(8,128)(2,1)} %refs_3_.3), channel_id=1, source_target_pairs={{0,2},{1,3},{2,0},{3,1},{4,6},{5,7},{6,4},{7,5},{8,10},{9,11},{10,... | collective-permute-start | bytes 2359304 | tf_op jit(solution)/shard_map/ppermute | solution.py:700
  3.8 24.1 %collective-permute-start.8 = (bf16[512,768]{1,0:T(8,128)(2,1)}, bf16[512,768]{1,0:T(8,128)(2,1)S(1)}, u32[]{:S(2)}, u32[]{:S(2)}) collective-permute-start(bf16[512,768]{1,0:T(8,128)(2,1)} %cotangent.1), channel_id=1, source_target_pairs={{0,1},{1,0},{2,3},{3,2},{4,5},{5,4},{6,7},{7,6},{8,9},{9,8},{10,11... | collective-permute-start | bytes 2359304 | tf_op jit(solution)/shard_map/ppermute | solution.py:700
  23.5 18.7 %collective-permute-start.5 = (bf16[512,768]{1,0:T(8,128)(2,1)}, bf16[512,768]{1,0:T(8,128)(2,1)}, u32[]{:S(2)}, u32[]{:S(2)}) collective-permute-start(bf16[512,768]{1,0:T(8,128)(2,1)} %gate.8.piece), channel_id=1, source_target_pairs={{0,1},{1,0},{2,3},{3,2},{4,5},{5,4},{6,7},{7,6},{8,9},{9,8},{10,11... | collective-permute-start | bytes 2359304 | tf_op jit(solution)/shard_map/ppermute | solution.py:700
  27.9 31.4 %collective-permute-start.10 = (bf16[96,1984]{1,0:T(8,128)(2,1)S(1)}, bf16[96,1984]{1,0:T(8,128)(2,1)S(1)}, u32[]{:S(2)}, u32[]{:S(2)}) collective-permute-start(bf16[96,1984]{1,0:T(8,128)(2,1)S(1)} %pack_kernel.1.refs_3_.refs_0_), channel_id=1, source_target_pairs={{0,16},{4,20},{8,24},{12,28},{16,0},{20,4},{24,8},{28,12},{1,17},{... | collective-permute-start | bytes 1142792 | tf_op jit(solution)/shard_map/ppermute | solution.py:700
  32.1 27.3 %collective-permute-start.9 = (bf16[96,1984]{1,0:T(8,128)(2,1)S(1)}, bf16[96,1984]{1,0:T(8,128)(2,1)}, u32[]{:S(2)}, u32[]{:S(2)}) collective-permute-start(bf16[96,1984]{1,0:T(8,128)(2,1)S(1)} %pack_kernel.1.refs_3_.refs_0_), channel_id=1, source_target_pairs={{0,8},{4,12},{8,0},{12,4},{16,24},{20,28},{24,16},{28,20},{1,9},{5... | collective-permute-start | bytes 1142792 | tf_op jit(solution)/shard_map/ppermute | solution.py:700
  32.1 27.3 %collective-permute-start.11 = (bf16[96,1984]{1,0:T(8,128)(2,1)S(1)}, bf16[96,1984]{1,0:T(8,128)(2,1)}, u32[]{:S(2)}, u32[]{:S(2)}) collective-permute-start(bf16[96,1984]{1,0:T(8,128)(2,1)S(1)} %pack_kernel.1.refs_3_.refs_0_), channel_id=1, source_target_pairs={{0,24},{4,28},{8,16},{12,20},{16,8},{20,12},{24,0},{28,4},{1,25},{... | collective-permute-start | bytes 1142792 | tf_op jit(solution)/shard_map/ppermute | solution.py:700
  88.8 37.4 %collective-permute-start.17 = (bf16[384,768]{1,0:T(8,128)(2,1)S(1)}, bf16[384,768]{1,0:T(8,128)(2,1)S(1)}, u32[]{:S(2)}, u32[]{:S(2)}) collective-permute-start(bf16[384,768]{1,0:T(8,128)(2,1)S(1)} %lay.6.refs_3_), channel_id=1, source_target_pairs={{0,1},{1,0},{2,3},{3,2},{4,5},{5,4},{6,7},{7,6},{8,9},{9,8},{10,11... | collective-permute-start | bytes 1769480 | tf_op jit(solution)/shard_map/ppermute | solution.py:700
  88.9 42.2 %collective-permute-start.19 = (bf16[784,768]{1,0:T(8,128)(2,1)S(1)}, bf16[784,768]{1,0:T(8,128)(2,1)}, u32[]{:S(2)}, u32[]{:S(2)}) collective-permute-start(bf16[784,768]{1,0:T(8,128)(2,1)S(1)} %lay.5.refs_2_.refs_9_.up_a), channel_id=1, source_target_pairs={{0,2},{1,3},{2,0},{3,1},{4,6},{5,7},{6,4},{7,5},{8,10},{9,11},{10,... | collective-permute-start | bytes 3612680 | tf_op jit(solution)/shard_map/ppermute | solution.py:700
  90.2 36.0 %collective-permute-start.15 = (bf16[512,384]{1,0:T(8,128)(2,1)S(1)}, bf16[512,384]{1,0:T(8,128)(2,1)S(1)}, u32[]{:S(2)}, u32[]{:S(2)}) collective-permute-start(bf16[512,384]{1,0:T(8,128)(2,1)S(1)} %beside_kernel.4.refs_3_), channel_id=1, source_target_pairs={{0,2},{1,3},{2,0},{3,1},{4,6},{5,7},{6,4},{7,5},{8,10},{9,11},{10,... | collective-permute-start | bytes 1179656 | tf_op jit(solution)/shard_map/ppermute | solution.py:700
  91.0 38.6 %collective-permute-start.20 = (bf16[4,96,1536]{2,1,0:T(8,128)(2,1)S(1)}, bf16[4,96,1536]{2,1,0:T(8,128)(2,1)S(1)}, u32[]{:S(2)}, u32[]{:S(2)}) collective-permute-start(bf16[4,96,1536]{2,1,0:T(8,128)(2,1)S(1)} %beside_kernel.3.refs_4_.refs_1_), channel_id=1, source_target_pairs={{0,4},{4,0},{8,12},{12,8},{16,20},{20,16},{24,28},{28,24},{1,5},{5... | collective-permute-start | bytes 3538952 | tf_op jit(solution)/shard_map/ppermute | solution.py:700
  165.6 29.0 %collective-permute-start.25 = (bf16[4,96,1536]{2,1,0:T(8,128)(2,1)}, bf16[4,96,1536]{2,1,0:T(8,128)(2,1)}, u32[]{:S(2)}, u32[]{:S(2)}) collective-permute-start(bf16[4,96,1536]{2,1,0:T(8,128)(2,1)} %fusion.12), channel_id=1, source_target_pairs={{0,4},{4,0},{8,12},{12,8},{16,20},{20,16},{24,28},{28,24},{1,5},{5... | collective-permute-start | bytes 3538952 | tf_op jit(solution)/shard_map/ppermute | solution.py:700
  170.4 21.9 %collective-permute-start.27 = (bf16[192,768]{1,0:T(8,128)(2,1)S(1)}, bf16[192,768]{1,0:T(8,128)(2,1)}, u32[]{:S(2)}, u32[]{:S(2)}) collective-permute-start(bf16[192,768]{1,0:T(8,128)(2,1)S(1)} %fusion.16.refs_0_), channel_id=1, source_target_pairs={{0,2},{1,3},{2,0},{3,1},{4,6},{5,7},{6,4},{7,5},{8,10},{9,11},{10,... | collective-permute-start | bytes 884744 | tf_op jit(solution)/shard_map/ppermute | solution.py:700
  177.7 44.6 %collective-permute-start.26 = (bf16[768,768]{1,0:T(8,128)(2,1)}, bf16[768,768]{1,0:T(8,128)(2,1)}, u32[]{:S(2)}, u32[]{:S(2)}) collective-permute-start(bf16[768,768]{1,0:T(8,128)(2,1)} %gate.12), channel_id=1, source_target_pairs={{0,2},{1,3},{2,0},{3,1},{4,6},{5,7},{6,4},{7,5},{8,10},{9,11},{10,... | collective-permute-start | bytes 3538952 | tf_op jit(solution)/shard_map/ppermute | solution.py:700
  199.5 62.9 %collective-permute-start.30 = (bf16[96,1536]{1,0:T(8,128)(2,1)}, bf16[96,1536]{1,0:T(8,128)(2,1)}, u32[]{:S(2)}, u32[]{:S(2)}) collective-permute-start(bf16[96,1536]{1,0:T(8,128)(2,1)} %get-tuple-element.146), channel_id=1, source_target_pairs={{0,8},{4,12},{8,0},{12,4},{16,24},{20,28},{24,16},{28,20},{1,9},{5... | collective-permute-start | bytes 884744 | tf_op jit(solution)/shard_map/ppermute | solution.py:700
  207.2 55.1 %collective-permute-start.32 = (bf16[96,1536]{1,0:T(8,128)(2,1)}, bf16[96,1536]{1,0:T(8,128)(2,1)}, u32[]{:S(2)}, u32[]{:S(2)}) collective-permute-start(bf16[96,1536]{1,0:T(8,128)(2,1)} %get-tuple-element.147), channel_id=1, source_target_pairs={{0,24},{4,28},{8,16},{12,20},{16,8},{20,12},{24,0},{28,4},{1,25},{... | collective-permute-start | bytes 884744 | tf_op jit(solution)/shard_map/ppermute | solution.py:700
  209.4 52.9 %collective-permute-start.31 = (bf16[96,1536]{1,0:T(8,128)(2,1)}, bf16[96,1536]{1,0:T(8,128)(2,1)}, u32[]{:S(2)}, u32[]{:S(2)}) collective-permute-start(bf16[96,1536]{1,0:T(8,128)(2,1)} %get-tuple-element.148), channel_id=1, source_target_pairs={{0,16},{4,20},{8,24},{12,28},{16,0},{20,4},{24,8},{28,12},{1,17},{... | collective-permute-start | bytes 884744 | tf_op jit(solution)/shard_map/ppermute | solution.py:700
  226.0 38.7 %collective-permute-start.29 = (bf16[4,96,960]{2,1,0:T(8,128)(2,1)}, bf16[4,96,960]{2,1,0:T(8,128)(2,1)}, u32[]{:S(2)}, u32[]{:S(2)}) collective-permute-start(bf16[4,96,960]{2,1,0:T(8,128)(2,1)} %fusion.13.refs_2_), channel_id=1, source_target_pairs={{0,4},{4,0},{8,12},{12,8},{16,20},{20,16},{24,28},{28,24},{1,5},{5... | collective-permute-start | bytes 2211848 | tf_op jit(solution)/shard_map/ppermute | solution.py:700
  230.4 37.2 %all-to-all-start = ((bf16[8,96,384]{2,1,0:T(8,128)(2,1)}), bf16[8,96,384]{2,1,0:T(8,128)(2,1)}, u32[]{:S(2)}, u32[]{:S(2)}) async-start(bf16[8,96,384]{2,1,0:T(8,128)(2,1)} %bitcast.115), calls=%async_computation | async-start | bytes 1179648 | tf_op jit(solution)/shard_map/all_to_all | solution.py:721
  270.2 27.6 %collective-permute-start.36 = (bf16[512,768]{1,0:T(8,128)(2,1)}, bf16[512,768]{1,0:T(8,128)(2,1)}, u32[]{:S(2)}, u32[]{:S(2)}) collective-permute-start(bf16[512,768]{1,0:T(8,128)(2,1)} %add_convert_fusion), channel_id=1, source_target_pairs={{0,2},{1,3},{2,0},{3,1},{4,6},{5,7},{6,4},{7,5},{8,10},{9,11},{10,... | collective-permute-start | bytes 2359304 | tf_op jit(solution)/shard_map/ppermute | solution.py:700
  273.3 17.2 %collective-permute-start.33 = (bf16[96,960]{1,0:T(8,128)(2,1)}, bf16[96,960]{1,0:T(8,128)(2,1)}, u32[]{:S(2)}, u32[]{:S(2)}) collective-permute-start(bf16[96,960]{1,0:T(8,128)(2,1)} %get-tuple-element.149), channel_id=1, source_target_pairs={{0,8},{4,12},{8,0},{12,4},{16,24},{20,28},{24,16},{28,20},{1,9},{5... | collective-permute-start | bytes 552968 | tf_op jit(solution)/shard_map/ppermute | solution.py:700
  277.9 17.8 %collective-permute-start.34 = (bf16[96,960]{1,0:T(8,128)(2,1)}, bf16[96,960]{1,0:T(8,128)(2,1)}, u32[]{:S(2)}, u32[]{:S(2)}) collective-permute-start(bf16[96,960]{1,0:T(8,128)(2,1)} %get-tuple-element.151), channel_id=1, source_target_pairs={{0,16},{4,20},{8,24},{12,28},{16,0},{20,4},{24,8},{28,12},{1,17},{... | collective-permute-start | bytes 552968 | tf_op jit(solution)/shard_map/ppermute | solution.py:700
  290.5 32.6 %collective-permute-start.38 = (bf16[512,768]{1,0:T(8,128)(2,1)}, bf16[512,768]{1,0:T(8,128)(2,1)}, u32[]{:S(2)}, u32[]{:S(2)}) collective-permute-start(bf16[512,768]{1,0:T(8,128)(2,1)} %get-tuple-element.135), channel_id=1, source_target_pairs={{0,1},{1,0},{2,3},{3,2},{4,5},{5,4},{6,7},{7,6},{8,9},{9,8},{10,11... | collective-permute-start | bytes 2359304 | tf_op jit(solution)/shard_map/ppermute | solution.py:700
  305.1 29.0 %collective-permute-start.37 = (bf16[512,768]{1,0:T(8,128)(2,1)}, bf16[512,768]{1,0:T(8,128)(2,1)}, u32[]{:S(2)}, u32[]{:S(2)}) collective-permute-start(bf16[512,768]{1,0:T(8,128)(2,1)} %slice.207), channel_id=1, source_target_pairs={{0,1},{1,0},{2,3},{3,2},{4,5},{5,4},{6,7},{7,6},{8,9},{9,8},{10,11... | collective-permute-start | bytes 2359304 | tf_op jit(solution)/shard_map/ppermute | solution.py:700
  306.9 21.3 %all-to-all-start.1 = ((bf16[8,144,192]{2,1,0:T(8,128)(2,1)}), bf16[8,144,192]{2,1,0:T(8,128)(2,1)S(1)}, u32[]{:S(2)}, u32[]{:S(2)}) async-start(bf16[8,144,192]{2,1,0:T(8,128)(2,1)} %pad_maximum_fusion.2), calls=%async_computation.1 | async-start | bytes 1179648 | tf_op jit(solution)/shard_map/all_to_all | solution.py:927
  (115 other events, 751.8 us)

commit v4 on v3

--- a/solution.py
+++ b/solution.py
@@ -924,22 +924,17 @@
     )
     up_out = sum_column(up_column, up_sent) if few else jnp.sum(wide(up_sent), axis=0)
     packed = gate(low(sums).reshape(-1, 3 * HD), up_out, chip_sum)
-    last_blocks = lax.all_to_all(
-        plain(
-            jnp.concatenate(
-                [last_whole.reshape(dp, rows_shard, 3 * HD), jnp.broadcast_to(packed, (dp,) + packed.shape)], axis=1
-            )
-        ),
-        "dp",
-        0,
-        0,
-        tiled=True,
-    )
+    last_blocks = plain(
+        jnp.concatenate(
+            [last_whole.reshape(dp, rows_shard, 3 * HD), jnp.broadcast_to(packed, (dp,) + packed.shape)], axis=1
+        )
+    )
+    active = gate(active.reshape(2 * own, 2 * hidden), last_blocks)
+    last_blocks = lax.all_to_all(last_blocks, "dp", 0, 0, tiled=True)
     down_grad_out = (down_part[:, :hidden] + wide(chip_swap(low(down_part[:, hidden:])))).T
     up_grad_out = up_out[:, :hidden]
     w_out_grad_out = up_out[:, hidden:].T
 
-    active = gate(active.reshape(2 * own, 2 * hidden), packed)
     mlp_part = dot32(active, down_pair, NT)
     mlp_branch = mlp_part[:own] + wide(core_swap(low(mlp_part[own:])))
     block_out = hidden_one + (mlp_branch + wide(down_bias))

time: 345 us -> 347 us (level)
  no operation moved by 1% of the time
where the time goes in v4:
time: 347 us; the launch traced here: 342 us
  Pallas kernels  107 us (31%)
  local copies, waits for them, and re-layouts  67.1 us (19%)
  waiting for transfers between devices  60.5 us (17%)
  starting transfers between devices  57.3 us (17%)
  other arithmetic  30.7 us (9%)
  matrix products  16.6 us (5%)
    ppermute x43, waiting for transfers between devices, flip(): lax.ppermute(plain(values), axis, [(i, i ^ mask) for i in range(size)])  60.5 us
    unnamed x193, local copies, waits for them, and re-layouts  47.4 us
    ppermute x43, starting transfers between devices, flip(): lax.ppermute(plain(values), axis, [(i, i ^ mask) for i in range(size)])  47.2 us
    pallas_call x3, Pallas kernels, attend_back(): pl.pallas_call(functools.partial(attend_back_kernel, head, len(deps), len...  37.7 us
    pallas_call x3, Pallas kernels, attend(): pl.pallas_call(functools.partial(attend_kernel, len(deps)), grid=(1,), in...  19.3 us
    pallas_call x18, Pallas kernels, call(): pl.pallas_call(body, grid=(1,), out_shape=out_shape, in_specs=specs, out_...  16.9 us
    dot_general x8, matrix products, dot32(): lax.dot_general(left, right, dims, preferred_element_type=jnp.float32)  16.6 us
    pallas_call x1, Pallas kernels, mlp(): pl.pallas_call(mlp_kernel, grid=(steps,), in_specs=[row_spec] * 4 + [whol...  13.8 us
  transfers between devices with their start and end apart: 45, of which 10 were waited for; matrix products, arithmetic and copies ran while one was open for 19% of the time, Pallas kernels for 26%

profile of v4, /device:TPU:0, one launch (start us, length us, event | category | flops | bytes accessed | tf_op | source)
XLA Modules:
  0.0 341.6 jit_solution(1150240323302156873)
XLA Ops:
  27.9 4.1 %collective-permute-start.10 = (bf16[96,1984]{1,0:T(8,128)(2,1)S(1)}, bf16[96,1984]{1,0:T(8,128)(2,1)S(1)}, u32[]{:S(2)}, u32[]{:S(2)}) collective-permute-start(bf16[96,1984]{1,0:T(8,128)(2,1)S(1)} %pack_kernel.1.refs_3_.refs_0_), channel_id=1, source_target_pairs={{0,16},{4,20},{8,24},{12,28},{16,0},{20,4},{24,8},{28,12},{1,17},{... | collective-permute-start | bytes 1142792 | tf_op jit(solution)/shard_map/ppermute | solution.py:700
  33.6 4.9 %collective-permute-done.6.refs_2_ = bf16[4,96,640]{2,1,0:T(8,128)(2,1)S(1)} collective-permute-done((bf16[4,96,640]{2,1,0:T(8,128)(2,1)S(1)}, bf16[4,96,640]{2,1,0:T(8,128)(2,1)S(1)}, u32[]{:S(2)}, u32[]{:S(2)}) %collective-permute-start.6) | collective-permute-done | bytes 491552 | tf_op jit(solution)/shard_map/ppermute | solution.py:700
  46.8 4.9 %project.1.query_ref.key_ref.value_ref = bf16[9,2048,64]{2,1,0:T(8,128)(2,1)} custom-call(bf16[2048,768]{1,0:T(8,128)(2,1)S(1)} %bitcast.112, bf16[784,576]{1,0:T(8,128)(2,1)S(1)} %copy-done.8), custom_call_target="tpu_custom_call" | custom-call | flops 1 | bytes 1 | tf_op jit(solution)/shard_map/project/pallas_call | solution.py:265
  54.1 5.3 %attend.3 = (bf16[2048,64]{1,0:T(8,128)(2,1)S(1)}, f32[8,2048]{1,0:T(8,128)S(1)}) custom-call(bf16[9,2048,64]{2,1,0:T(8,128)(2,1)S(1)} %copy-done, bf16[9,2048,64]{2,1,0:T(8,128)(2,1)S(1)} %copy-done, bf16[9,2048,64]{2,1,0:T(8,128)(2,1)S(1)} %copy-done, s32[1,2048]{1,0:T(1,128)S(1)} %bitcast.117), custom_call_target="tpu_custom_call" | custom-call | flops 1 | bytes 1 | tf_op jit(solution)/shard_map/attend/pallas_call | solution.py:334
  63.0 6.6 %attend.4 = (bf16[2048,64]{1,0:T(8,128)(2,1)S(1)}, f32[8,2048]{1,0:T(8,128)S(1)}) custom-call(bf16[9,2048,64]{2,1,0:T(8,128)(2,1)} %project.1.query_ref.key_ref.value_ref, bf16[9,2048,64]{2,1,0:T(8,128)(2,1)} %project.1.query_ref.key_ref.value_ref, bf16[9,2048,64]{2,1,0:T(8,128)(2,1)} %project.1.query_ref.key_ref.value_ref, s32[1,2048]{1,0:T(1,128)S(1)} %bitcast.118, ...), custom_call_target="tpu_custom_call" | custom-call | flops 1 | bytes 1 | tf_op jit(solution)/shard_map/attend/pallas_call | solution.py:334
  70.3 7.4 %attend.5 = (bf16[2048,64]{1,0:T(8,128)(2,1)S(1)}, f32[8,2048]{1,0:T(8,128)S(1)}) custom-call(bf16[9,2048,64]{2,1,0:T(8,128)(2,1)} %project.1.query_ref.key_ref.value_ref, bf16[9,2048,64]{2,1,0:T(8,128)(2,1)} %project.1.query_ref.key_ref.value_ref, bf16[9,2048,64]{2,1,0:T(8,128)(2,1)} %project.1.query_ref.key_ref.value_ref, s32[1,2048]{1,0:T(1,128)S(1)} %bitcast.119, ...), custom_call_target="tpu_custom_call" | custom-call | flops 1 | bytes 1 | tf_op jit(solution)/shard_map/attend/pallas_call | solution.py:334
  81.8 6.7 %collective-permute-done.16.refs_2_ = bf16[4,96,384]{2,1,0:T(8,128)(2,1)S(1)} collective-permute-done((bf16[4,96,384]{2,1,0:T(8,128)(2,1)S(1)}, bf16[4,96,384]{2,1,0:T(8,128)(2,1)S(1)}, u32[]{:S(2)}, u32[]{:S(2)}) %collective-permute-start.16) | collective-permute-done | bytes 294944 | tf_op jit(solution)/shard_map/ppermute | solution.py:700
  91.9 34.3 %collective-permute-done.15.refs_2_ = bf16[512,384]{1,0:T(8,128)(2,1)S(1)} collective-permute-done((bf16[512,384]{1,0:T(8,128)(2,1)S(1)}, bf16[512,384]{1,0:T(8,128)(2,1)S(1)}, u32[]{:S(2)}, u32[]{:S(2)}) %collective-permute-start.15) | collective-permute-done | bytes 393248 | tf_op jit(solution)/shard_map/ppermute | solution.py:700
  133.8 13.8 %mlp.1 = (bf16[2,512,1536]{2,1,0:T(8,128)(2,1)}, bf16[2,512,1536]{2,1,0:T(8,128)(2,1)}, f32[512,768]{1,0:T(8,128)}, bf16[512,768]{1,0:T(8,128)(2,1)}, f32[8,1536]{1,0:T(8,128)S(1)}) custom-call(bf16[512,768]{1,0:T(8,128)(2,1)S(1)} %get-tuple-element.74.refs_3_.mine, bf16[512,768]{1,0:T(8,128)(2,1)} %gate.10.other, bf16[512,768]{1,0:T(8,128)(2,1)S(1)} %copy-done.26, ...), custom_call_target="tpu_custom_call" | custom-call | flops 1 | bytes 1 | tf_op jit(solution)/shard_map/mlp/pallas_call | solution.py:523
  151.7 4.2 %turn.1 = (f32[512,768]{1,0:T(8,128)S(1)}, bf16[512,768]{1,0:T(8,128)(2,1)S(1)}, bf16[512,384]{1,0:T(8,128)(2,1)S(1)}, bf16[512,384]{1,0:T(8,128)(2,1)S(1)}, f32...) custom-call(f32[512,768]{1,0:T(8,128)} %get-tuple-element.75.mine, ...), custom_call_target="tpu_custom_call", output_to_operand_aliasing={{5}: (6, {}), {6}: (7, {})} | custom-call | flops 1 | bytes 1 | tf_op jit(solution)/shard_map/turn/pallas_call | solution.py:563
  178.7 12.7 %attend_back.3.refs_1_.refs_0_ = bf16[2048,192]{1,0:T(8,128)(2,1)S(1)} custom-call(s32[1]{0:T(128)} %bitcast.index.refs_0_.me, bf16[9,2048,64]{2,1,0:T(8,128)(2,1)} %project.1.query_ref.key_ref.value_ref, bf16[9,2048,64]{2,1,0:T(8,128)(2,1)} %project.1.query_ref.key_ref.value_ref, bf16[9,2048,64]{2,1,0:T(8,128)(2,1)} %project.1.query_ref.key_ref.value_ref, ...), custom_call_target="tpu_custom_call" | custom-call | flops 1 | bytes 1 | tf_op jit(solution)/shard_map/attend_back/pallas_call | solution.py:422
  194.6 3.9 %fusion.30 = (bf16[4,96,1536]{2,1,0:T(8,128)(2,1)S(1)}, f32[4,96,1536]{2,1,0:T(8,128)}) fusion(bf16[4,96,1536]{2,1,0:T(8,128)(2,1)} %gate.11, f32[4,2,96,1536]{3,2,1,0:T(8,128)} %bitcast.128, s32[]{:T(128)S(6)} %select_n.94), kind=kLoop, calls=%fused_computation.79 | loop fusion | flops 1769472 | bytes 7077892 | tf_op jit(solution)/shard_map/convert_element_type | solution.py:27
  199.5 7.8 %collective-permute-start.30 = (bf16[96,1536]{1,0:T(8,128)(2,1)}, bf16[96,1536]{1,0:T(8,128)(2,1)}, u32[]{:S(2)}, u32[]{:S(2)}) collective-permute-start(bf16[96,1536]{1,0:T(8,128)(2,1)} %get-tuple-element.146), channel_id=1, source_target_pairs={{0,8},{4,12},{8,0},{12,4},{16,24},{20,28},{24,16},{28,20},{1,9},{5... | collective-permute-start | bytes 884744 | tf_op jit(solution)/shard_map/ppermute | solution.py:700
  209.5 12.8 %attend_back.4.refs_0_.refs_1_ = bf16[2048,384]{1,0:T(8,128)(2,1)S(1)} custom-call(s32[1]{0:T(128)} %bitcast.index.refs_0_.me, bf16[9,2048,64]{2,1,0:T(8,128)(2,1)} %project.1.query_ref.key_ref.value_ref, bf16[9,2048,64]{2,1,0:T(8,128)(2,1)} %project.1.query_ref.key_ref.value_ref, bf16[9,2048,64]{2,1,0:T(8,128)(2,1)} %project.1.query_ref.key_ref.value_ref, ...), custom_call_target="tpu_custom_call" | custom-call | flops 1 | bytes 1 | tf_op jit(solution)/shard_map/attend_back/pallas_call | solution.py:422
  230.4 5.1 %all-to-all-start = ((bf16[8,96,384]{2,1,0:T(8,128)(2,1)}), bf16[8,96,384]{2,1,0:T(8,128)(2,1)}, u32[]{:S(2)}, u32[]{:S(2)}) async-start(bf16[8,96,384]{2,1,0:T(8,128)(2,1)} %bitcast.115), calls=%async_computation | async-start | bytes 1179648 | tf_op jit(solution)/shard_map/all_to_all | solution.py:721
  241.9 12.3 %attend_back.5.refs_1_.refs_2_ = bf16[2048,192]{1,0:T(8,128)(2,1)S(1)} custom-call(s32[1]{0:T(128)} %bitcast.index.refs_0_.me, bf16[9,2048,64]{2,1,0:T(8,128)(2,1)} %project.1.query_ref.key_ref.value_ref, bf16[9,2048,64]{2,1,0:T(8,128)(2,1)} %project.1.query_ref.key_ref.value_ref, bf16[9,2048,64]{2,1,0:T(8,128)(2,1)} %project.1.query_ref.key_ref.value_ref, ...), custom_call_target="tpu_custom_call" | custom-call | flops 1 | bytes 1 | tf_op jit(solution)/shard_map/attend_back/pallas_call | solution.py:422
  264.7 2.9 fusion.29
  282.3 7.4 %near_kernel.1 = (f32[4,2,192]{2,1,0:T(2,128)S(1)}, f32[2,768]{1,0:T(2,128)S(1)}, f32[512,768]{1,0:T(8,128)}, bf16[512,768]{1,0:T(8,128)(2,1)}) fusion(f32[4,2,192]{2,1,0:T(2,128)S(1)} %broadcast_in_dim.108, s32[]{:T(128)S(6)} %select_n.104, s32[1]{0:T(128)} %bitcast.index.refs_0_.me, bf16[2048,384]{1,0:T(8,128)(2,1)S(1)} %copy-done.6, ...), kind=kCustom, calls=%fused_computation.63 | custom fusion | flops 1 | bytes 12677128 | tf_op jit(solution)/shard_map/near_kernel/pallas_call | solution.py:662
  290.5 5.2 %collective-permute-done.34 = bf16[96,960]{1,0:T(8,128)(2,1)} collective-permute-done((bf16[96,960]{1,0:T(8,128)(2,1)}, bf16[96,960]{1,0:T(8,128)(2,1)}, u32[]{:S(2)}, u32[]{:S(2)}) %collective-permute-start.34) | collective-permute-done | bytes 184352 | tf_op jit(solution)/shard_map/ppermute | solution.py:700
  301.1 4.5 %fusion.34 = f32[1024,768]{1,0:T(8,128)S(1)} fusion(bf16[1024,1536]{1,0:T(8,128)(2,1)} %gate.15, bf16[768,1536]{1,0:T(8,128)(2,1)S(1)} %copy-done.12), kind=kOutput, calls=%fused_computation.83 | convolution fusion | flops 2415919104 | bytes 8650752 | tf_op jit(solution)/shard_map/dot_general | solution.py:47
  308.4 5.0 %all-to-all-start.1 = ((bf16[8,144,192]{2,1,0:T(8,128)(2,1)}), bf16[8,144,192]{2,1,0:T(8,128)(2,1)S(1)}, u32[]{:S(2)}, u32[]{:S(2)}) async-start(bf16[8,144,192]{2,1,0:T(8,128)(2,1)} %pad_maximum_fusion.2.refs_1_), calls=%async_computation.1 | async-start | bytes 1179648 | tf_op jit(solution)/shard_map/all_to_all | solution.py:933
  314.9 5.3 %collective-permute-done.42 = bf16[96,768]{1,0:T(8,128)(2,1)} collective-permute-done((bf16[96,768]{1,0:T(8,128)(2,1)}, bf16[96,768]{1,0:T(8,128)(2,1)}, u32[]{:S(2)}, u32[]{:S(2)}) %collective-permute-start.42) | collective-permute-done | bytes 147488 | tf_op jit(solution)/shard_map/ppermute | solution.py:700
  326.6 3.7 %last_kernel.1.refs_2_ = f32[512,768]{1,0:T(8,128)} custom-call(f32[512,768]{1,0:T(8,128)S(1)} %copy-done.34, bf16[512,768]{1,0:T(8,128)(2,1)} %collective-permute-done.38.refs_1_, bf16[512,768]{1,0:T(8,128)(2,1)} %collective-permute-done.36.refs_2_, bf16[512,768]{1,0:T(8,128)(2,1)S(1)} %copy-done.25, f32[512,768]{1,0:T(8,128)S(1)} %copy-done.48, ...), custom_call_target="tpu_custom_call" | custom-call | flops 1 | bytes 1 | tf_op jit(solution)/shard_map/last_kernel/pallas_call | solution.py:662
  336.1 3.0 fusion.1
  (373 shorter events, 155.8 us)
Async XLA Ops:
  1.2 21.5 %collective-permute-start = (bf16[512,768]{1,0:T(8,128)(2,1)}, bf16[512,768]{1,0:T(8,128)(2,1)S(1)}, u32[]{:S(2)}, u32[]{:S(2)}) collective-permute-start(bf16[512,768]{1,0:T(8,128)(2,1)} %refs_3_.3), channel_id=1, source_target_pairs={{0,2},{1,3},{2,0},{3,1},{4,6},{5,7},{6,4},{7,5},{8,10},{9,11},{10,... | collective-permute-start | bytes 2359304 | tf_op jit(solution)/shard_map/ppermute | solution.py:700
  3.8 24.1 %collective-permute-start.8 = (bf16[512,768]{1,0:T(8,128)(2,1)}, bf16[512,768]{1,0:T(8,128)(2,1)S(1)}, u32[]{:S(2)}, u32[]{:S(2)}) collective-permute-start(bf16[512,768]{1,0:T(8,128)(2,1)} %cotangent.1), channel_id=1, source_target_pairs={{0,1},{1,0},{2,3},{3,2},{4,5},{5,4},{6,7},{7,6},{8,9},{9,8},{10,11... | collective-permute-start | bytes 2359304 | tf_op jit(solution)/shard_map/ppermute | solution.py:700
  23.5 18.7 %collective-permute-start.5 = (bf16[512,768]{1,0:T(8,128)(2,1)}, bf16[512,768]{1,0:T(8,128)(2,1)}, u32[]{:S(2)}, u32[]{:S(2)}) collective-permute-start(bf16[512,768]{1,0:T(8,128)(2,1)} %gate.8.piece), channel_id=1, source_target_pairs={{0,1},{1,0},{2,3},{3,2},{4,5},{5,4},{6,7},{7,6},{8,9},{9,8},{10,11... | collective-permute-start | bytes 2359304 | tf_op jit(solution)/shard_map/ppermute | solution.py:700
  27.9 31.4 %collective-permute-start.10 = (bf16[96,1984]{1,0:T(8,128)(2,1)S(1)}, bf16[96,1984]{1,0:T(8,128)(2,1)S(1)}, u32[]{:S(2)}, u32[]{:S(2)}) collective-permute-start(bf16[96,1984]{1,0:T(8,128)(2,1)S(1)} %pack_kernel.1.refs_3_.refs_0_), channel_id=1, source_target_pairs={{0,16},{4,20},{8,24},{12,28},{16,0},{20,4},{24,8},{28,12},{1,17},{... | collective-permute-start | bytes 1142792 | tf_op jit(solution)/shard_map/ppermute | solution.py:700
  32.1 27.3 %collective-permute-start.9 = (bf16[96,1984]{1,0:T(8,128)(2,1)S(1)}, bf16[96,1984]{1,0:T(8,128)(2,1)}, u32[]{:S(2)}, u32[]{:S(2)}) collective-permute-start(bf16[96,1984]{1,0:T(8,128)(2,1)S(1)} %pack_kernel.1.refs_3_.refs_0_), channel_id=1, source_target_pairs={{0,8},{4,12},{8,0},{12,4},{16,24},{20,28},{24,16},{28,20},{1,9},{5... | collective-permute-start | bytes 1142792 | tf_op jit(solution)/shard_map/ppermute | solution.py:700
  32.1 27.3 %collective-permute-start.11 = (bf16[96,1984]{1,0:T(8,128)(2,1)S(1)}, bf16[96,1984]{1,0:T(8,128)(2,1)}, u32[]{:S(2)}, u32[]{:S(2)}) collective-permute-start(bf16[96,1984]{1,0:T(8,128)(2,1)S(1)} %pack_kernel.1.refs_3_.refs_0_), channel_id=1, source_target_pairs={{0,24},{4,28},{8,16},{12,20},{16,8},{20,12},{24,0},{28,4},{1,25},{... | collective-permute-start | bytes 1142792 | tf_op jit(solution)/shard_map/ppermute | solution.py:700
  88.8 37.4 %collective-permute-start.17 = (bf16[384,768]{1,0:T(8,128)(2,1)S(1)}, bf16[384,768]{1,0:T(8,128)(2,1)S(1)}, u32[]{:S(2)}, u32[]{:S(2)}) collective-permute-start(bf16[384,768]{1,0:T(8,128)(2,1)S(1)} %lay.6.refs_3_), channel_id=1, source_target_pairs={{0,1},{1,0},{2,3},{3,2},{4,5},{5,4},{6,7},{7,6},{8,9},{9,8},{10,11... | collective-permute-start | bytes 1769480 | tf_op jit(solution)/shard_map/ppermute | solution.py:700
  88.9 42.2 %collective-permute-start.19 = (bf16[784,768]{1,0:T(8,128)(2,1)S(1)}, bf16[784,768]{1,0:T(8,128)(2,1)}, u32[]{:S(2)}, u32[]{:S(2)}) collective-permute-start(bf16[784,768]{1,0:T(8,128)(2,1)S(1)} %lay.5.refs_2_.refs_9_.up_a), channel_id=1, source_target_pairs={{0,2},{1,3},{2,0},{3,1},{4,6},{5,7},{6,4},{7,5},{8,10},{9,11},{10,... | collective-permute-start | bytes 3612680 | tf_op jit(solution)/shard_map/ppermute | solution.py:700
  90.2 36.0 %collective-permute-start.15 = (bf16[512,384]{1,0:T(8,128)(2,1)S(1)}, bf16[512,384]{1,0:T(8,128)(2,1)S(1)}, u32[]{:S(2)}, u32[]{:S(2)}) collective-permute-start(bf16[512,384]{1,0:T(8,128)(2,1)S(1)} %beside_kernel.4.refs_3_), channel_id=1, source_target_pairs={{0,2},{1,3},{2,0},{3,1},{4,6},{5,7},{6,4},{7,5},{8,10},{9,11},{10,... | collective-permute-start | bytes 1179656 | tf_op jit(solution)/shard_map/ppermute | solution.py:700
  91.0 38.6 %collective-permute-start.20 = (bf16[4,96,1536]{2,1,0:T(8,128)(2,1)S(1)}, bf16[4,96,1536]{2,1,0:T(8,128)(2,1)S(1)}, u32[]{:S(2)}, u32[]{:S(2)}) collective-permute-start(bf16[4,96,1536]{2,1,0:T(8,128)(2,1)S(1)} %beside_kernel.3.refs_4_.refs_1_), channel_id=1, source_target_pairs={{0,4},{4,0},{8,12},{12,8},{16,20},{20,16},{24,28},{28,24},{1,5},{5... | collective-permute-start | bytes 3538952 | tf_op jit(solution)/shard_map/ppermute | solution.py:700
  165.6 29.0 %collective-permute-start.25 = (bf16[4,96,1536]{2,1,0:T(8,128)(2,1)}, bf16[4,96,1536]{2,1,0:T(8,128)(2,1)}, u32[]{:S(2)}, u32[]{:S(2)}) collective-permute-start(bf16[4,96,1536]{2,1,0:T(8,128)(2,1)} %fusion.12), channel_id=1, source_target_pairs={{0,4},{4,0},{8,12},{12,8},{16,20},{20,16},{24,28},{28,24},{1,5},{5... | collective-permute-start | bytes 3538952 | tf_op jit(solution)/shard_map/ppermute | solution.py:700
  170.4 21.9 %collective-permute-start.27 = (bf16[192,768]{1,0:T(8,128)(2,1)S(1)}, bf16[192,768]{1,0:T(8,128)(2,1)}, u32[]{:S(2)}, u32[]{:S(2)}) collective-permute-start(bf16[192,768]{1,0:T(8,128)(2,1)S(1)} %fusion.16.refs_0_), channel_id=1, source_target_pairs={{0,2},{1,3},{2,0},{3,1},{4,6},{5,7},{6,4},{7,5},{8,10},{9,11},{10,... | collective-permute-start | bytes 884744 | tf_op jit(solution)/shard_map/ppermute | solution.py:700
  177.7 44.6 %collective-permute-start.26 = (bf16[768,768]{1,0:T(8,128)(2,1)}, bf16[768,768]{1,0:T(8,128)(2,1)}, u32[]{:S(2)}, u32[]{:S(2)}) collective-permute-start(bf16[768,768]{1,0:T(8,128)(2,1)} %gate.12), channel_id=1, source_target_pairs={{0,2},{1,3},{2,0},{3,1},{4,6},{5,7},{6,4},{7,5},{8,10},{9,11},{10,... | collective-permute-start | bytes 3538952 | tf_op jit(solution)/shard_map/ppermute | solution.py:700
  199.5 62.9 %collective-permute-start.30 = (bf16[96,1536]{1,0:T(8,128)(2,1)}, bf16[96,1536]{1,0:T(8,128)(2,1)}, u32[]{:S(2)}, u32[]{:S(2)}) collective-permute-start(bf16[96,1536]{1,0:T(8,128)(2,1)} %get-tuple-element.146), channel_id=1, source_target_pairs={{0,8},{4,12},{8,0},{12,4},{16,24},{20,28},{24,16},{28,20},{1,9},{5... | collective-permute-start | bytes 884744 | tf_op jit(solution)/shard_map/ppermute | solution.py:700
  207.2 55.1 %collective-permute-start.32 = (bf16[96,1536]{1,0:T(8,128)(2,1)}, bf16[96,1536]{1,0:T(8,128)(2,1)}, u32[]{:S(2)}, u32[]{:S(2)}) collective-permute-start(bf16[96,1536]{1,0:T(8,128)(2,1)} %get-tuple-element.147), channel_id=1, source_target_pairs={{0,24},{4,28},{8,16},{12,20},{16,8},{20,12},{24,0},{28,4},{1,25},{... | collective-permute-start | bytes 884744 | tf_op jit(solution)/shard_map/ppermute | solution.py:700
  209.4 52.9 %collective-permute-start.31 = (bf16[96,1536]{1,0:T(8,128)(2,1)}, bf16[96,1536]{1,0:T(8,128)(2,1)}, u32[]{:S(2)}, u32[]{:S(2)}) collective-permute-start(bf16[96,1536]{1,0:T(8,128)(2,1)} %get-tuple-element.148), channel_id=1, source_target_pairs={{0,16},{4,20},{8,24},{12,28},{16,0},{20,4},{24,8},{28,12},{1,17},{... | collective-permute-start | bytes 884744 | tf_op jit(solution)/shard_map/ppermute | solution.py:700
  226.0 38.7 %collective-permute-start.29 = (bf16[4,96,960]{2,1,0:T(8,128)(2,1)}, bf16[4,96,960]{2,1,0:T(8,128)(2,1)}, u32[]{:S(2)}, u32[]{:S(2)}) collective-permute-start(bf16[4,96,960]{2,1,0:T(8,128)(2,1)} %fusion.13.refs_2_), channel_id=1, source_target_pairs={{0,4},{4,0},{8,12},{12,8},{16,20},{20,16},{24,28},{28,24},{1,5},{5... | collective-permute-start | bytes 2211848 | tf_op jit(solution)/shard_map/ppermute | solution.py:700
  230.4 37.2 %all-to-all-start = ((bf16[8,96,384]{2,1,0:T(8,128)(2,1)}), bf16[8,96,384]{2,1,0:T(8,128)(2,1)}, u32[]{:S(2)}, u32[]{:S(2)}) async-start(bf16[8,96,384]{2,1,0:T(8,128)(2,1)} %bitcast.115), calls=%async_computation | async-start | bytes 1179648 | tf_op jit(solution)/shard_map/all_to_all | solution.py:721
  270.2 27.6 %collective-permute-start.36 = (bf16[512,768]{1,0:T(8,128)(2,1)}, bf16[512,768]{1,0:T(8,128)(2,1)}, u32[]{:S(2)}, u32[]{:S(2)}) collective-permute-start(bf16[512,768]{1,0:T(8,128)(2,1)} %add_convert_fusion), channel_id=1, source_target_pairs={{0,2},{1,3},{2,0},{3,1},{4,6},{5,7},{6,4},{7,5},{8,10},{9,11},{10,... | collective-permute-start | bytes 2359304 | tf_op jit(solution)/shard_map/ppermute | solution.py:700
  273.3 17.2 %collective-permute-start.33 = (bf16[96,960]{1,0:T(8,128)(2,1)}, bf16[96,960]{1,0:T(8,128)(2,1)}, u32[]{:S(2)}, u32[]{:S(2)}) collective-permute-start(bf16[96,960]{1,0:T(8,128)(2,1)} %get-tuple-element.149), channel_id=1, source_target_pairs={{0,8},{4,12},{8,0},{12,4},{16,24},{20,28},{24,16},{28,20},{1,9},{5... | collective-permute-start | bytes 552968 | tf_op jit(solution)/shard_map/ppermute | solution.py:700
  277.9 17.8 %collective-permute-start.34 = (bf16[96,960]{1,0:T(8,128)(2,1)}, bf16[96,960]{1,0:T(8,128)(2,1)}, u32[]{:S(2)}, u32[]{:S(2)}) collective-permute-start(bf16[96,960]{1,0:T(8,128)(2,1)} %get-tuple-element.151), channel_id=1, source_target_pairs={{0,16},{4,20},{8,24},{12,28},{16,0},{20,4},{24,8},{28,12},{1,17},{... | collective-permute-start | bytes 552968 | tf_op jit(solution)/shard_map/ppermute | solution.py:700
  290.5 34.7 %collective-permute-start.38 = (bf16[512,768]{1,0:T(8,128)(2,1)}, bf16[512,768]{1,0:T(8,128)(2,1)}, u32[]{:S(2)}, u32[]{:S(2)}) collective-permute-start(bf16[512,768]{1,0:T(8,128)(2,1)} %get-tuple-element.135), channel_id=1, source_target_pairs={{0,1},{1,0},{2,3},{3,2},{4,5},{5,4},{6,7},{7,6},{8,9},{9,8},{10,11... | collective-permute-start | bytes 2359304 | tf_op jit(solution)/shard_map/ppermute | solution.py:700
  308.4 27.7 %collective-permute-start.37 = (bf16[512,768]{1,0:T(8,128)(2,1)}, bf16[512,768]{1,0:T(8,128)(2,1)}, u32[]{:S(2)}, u32[]{:S(2)}) collective-permute-start(bf16[512,768]{1,0:T(8,128)(2,1)} %slice.207), channel_id=1, source_target_pairs={{0,1},{1,0},{2,3},{3,2},{4,5},{5,4},{6,7},{7,6},{8,9},{9,8},{10,11... | collective-permute-start | bytes 2359304 | tf_op jit(solution)/shard_map/ppermute | solution.py:700
  308.4 22.0 %all-to-all-start.1 = ((bf16[8,144,192]{2,1,0:T(8,128)(2,1)}), bf16[8,144,192]{2,1,0:T(8,128)(2,1)S(1)}, u32[]{:S(2)}, u32[]{:S(2)}) async-start(bf16[8,144,192]{2,1,0:T(8,128)(2,1)} %pad_maximum_fusion.2.refs_1_), calls=%async_computation.1 | async-start | bytes 1179648 | tf_op jit(solution)/shard_map/all_to_all | solution.py:933
  (115 other events, 758.1 us)
